TPU v7x, 128 devices: a whole 4x4x4 slice. The times are simulated.
128 devices in a mesh: dp: 16 (over x, y), tensor: 8 (over z, core).
Axes of the slice: x: 4, y: 4, z: 4, core: 2. Of those that a mesh axis runs over, the one named last changes fastest.
Arguments:
- out_grad: bfloat16 [16384, 5120], P(('dp', 'tensor')), may hold values from -0.796875 to 0.796875
- normed: bfloat16 [16384, 5120], P(('dp', 'tensor')), may hold values from -24 to 24
- router: bfloat16 [5120, 128], replicated, may hold values from -1 to 1
- expert_ids: int32 [16384, 6], P(('dp', 'tensor')), may hold values from 0 to 127, all different within a row; in each aligned block of 128 rows (0 to 127, 128 to 255, ...) at most 8 rows name the same one
- hidden_act: bfloat16 [128, 1024, 768], P(('dp', 'tensor')), may hold values from -6 to 6
- down_weight: bfloat16 [128, 768, 5120], P(('dp', 'tensor')), may hold values from -0.21875 to 0.21875
Outputs:
- d_down: bfloat16 [128, 768, 5120], P(('dp', 'tensor'))
- d_hidden: bfloat16 [128, 1024, 768], P(('dp', 'tensor'))
- d_router: float32 [5120, 128], P(('dp', 'tensor'))
- d_normed: bfloat16 [16384, 5120], P(('dp', 'tensor'))
Inputs may be any that keep to these rules, and one draw needn't show every extreme that they name: `expert_ids`: each row names 6 different experts; within the 128 rows of one device no expert is named more than 8 times, and in every draw some expert is named exactly 8 times by the rows of some device.
All inputs are finite; a program needn't handle non-finite values.
Results may differ from a plain program's by a relative error of at most 0.034.
Values may be sent and summed in bfloat16 or wider, within the bound.
No kernel may reach another device: no remote copies, remote signals or barrier semaphores. Data moves between devices by JAX's collectives and lax.ppermute only.
A program may use at most 128 MiB of HBM per device.

v0:
```python
import jax
import jax.numpy as jnp
from jax import lax
from jax.sharding import PartitionSpec as P

route_scale = 16.0


def body(out_grad, normed, router, expert_ids, hidden_act, down_weight):
    groups = lax.axis_size(("dp", "tensor"))
    tok_rows = out_grad.shape[0]
    model_width = out_grad.shape[1]
    top_count = expert_ids.shape[1]
    experts = router.shape[1]
    capacity = hidden_act.shape[1] // groups
    hidden_rows = hidden_act[0]
    weight = down_weight[0]
    logits = jnp.dot(normed, router, preferred_element_type=jnp.float32)
    router_prob = jax.nn.softmax(logits, axis=-1)
    chosen = jnp.take_along_axis(router_prob, expert_ids, axis=1)
    gate_vals = (route_scale * chosen).astype(jnp.bfloat16)
    flat_ids = expert_ids.reshape(-1)
    expert_range = jnp.arange(experts, dtype=jnp.int32)
    onehot = (flat_ids[:, None] == expert_range[None, :]).astype(jnp.int32)
    slot_rank = jnp.sum((jnp.cumsum(onehot, axis=0) - onehot) * onehot, axis=1)
    slot_rows = flat_ids * capacity + slot_rank
    token_ids = jnp.arange(tok_rows * top_count, dtype=jnp.int32) // top_count
    token_of_row = jnp.full((groups * capacity,), tok_rows, jnp.int32).at[slot_rows].set(token_ids)
    gate_of_row = (
        jnp.zeros((groups * capacity,), jnp.bfloat16).at[slot_rows].set(gate_vals.reshape(-1))
    )
    padded = jnp.concatenate([out_grad, jnp.zeros((1, model_width), out_grad.dtype)], axis=0)
    send_rows = padded[token_of_row].reshape(groups, capacity, model_width)
    send_gates = gate_of_row.reshape(groups, capacity)
    expert_out = jnp.dot(hidden_rows, weight, preferred_element_type=jnp.float32)
    got_rows, got_gates = (
        lax.all_to_all(send_rows, ("dp", "tensor"), split_axis=0, concat_axis=0, tiled=True),
        lax.all_to_all(send_gates, ("dp", "tensor"), split_axis=0, concat_axis=0, tiled=True),
    )
    got_rows = got_rows.reshape(groups * capacity, model_width)
    got_gates = got_gates.reshape(groups * capacity)
    local_grad = (got_gates.astype(jnp.float32)[:, None] * got_rows.astype(jnp.float32)).astype(
        jnp.bfloat16
    )
    slot_score = jnp.sum(got_rows.astype(jnp.float32) * expert_out, axis=1)
    returned = lax.all_to_all(
        slot_score.reshape(groups, capacity),
        ("dp", "tensor"),
        split_axis=0,
        concat_axis=0,
        tiled=True,
    )
    grad_hidden = lax.dot_general(
        local_grad, weight, (((1,), (1,)), ((), ())), preferred_element_type=jnp.float32
    ).astype(jnp.bfloat16)
    grad_weight = lax.dot_general(
        hidden_rows, local_grad, (((0,), (0,)), ((), ())), preferred_element_type=jnp.float32
    ).astype(jnp.bfloat16)
    gate_grad = returned.reshape(-1)[slot_rows].reshape(tok_rows, top_count)
    prob_grad = route_scale * jnp.sum(
        jnp.where(
            expert_ids[:, :, None] == expert_range[None, None, :],
            gate_grad[:, :, None],
            jnp.float32(0.0),
        ),
        axis=1,
    )
    logit_grad = (
        router_prob * (prob_grad - jnp.sum(router_prob * prob_grad, axis=1, keepdims=True))
    ).astype(jnp.bfloat16)
    d_router = lax.psum_scatter(
        lax.dot_general(
            normed, logit_grad, (((0,), (0,)), ((), ())), preferred_element_type=jnp.float32
        ),
        ("dp", "tensor"),
        scatter_dimension=0,
        tiled=True,
    )
    d_normed = lax.dot_general(
        logit_grad, router, (((1,), (1,)), ((), ())), preferred_element_type=jnp.float32
    ).astype(jnp.bfloat16)
    return (grad_weight[None], grad_hidden[None], d_router, d_normed)


def solution(mesh):
    in_specs = (
        P(("dp", "tensor"), None),
        P(("dp", "tensor"), None),
        P(),
        P(("dp", "tensor"), None),
        P(("dp", "tensor"), None, None),
        P(("dp", "tensor"), None, None),
    )
    out_specs = (
        P(("dp", "tensor"), None, None),
        P(("dp", "tensor"), None, None),
        P(("dp", "tensor"), None),
        P(("dp", "tensor"), None),
    )
    return jax.shard_map(body, mesh=mesh, in_specs=in_specs, out_specs=out_specs, check_vma=False)
```

profile of v0, /device:TPU:1, one launch (start us, length us, event | category | flops | bytes accessed | tf_op | source)
XLA Modules:
  0.0 394.9 jit_solution(9201976997688181923)
XLA Ops:
  7.2 0.8 broadcast_multiply_fusion
  8.0 0.8 copy.58
  8.8 0.1 eq.42
  8.9 0.1 eq.38
  9.1 0.1 copy.57
  9.2 0.1 mul.54
  9.3 0.1 copy.60
  9.4 0.2 fusion.28
  9.7 0.1 copy.61
  9.8 0.3 fusion.31
  10.1 3.4 scatter_custom_fusion.1
  13.5 1.4 concatenate.3
  15.0 8.7 %gather_fusion = bf16[1024,5120]{1,0:T(8,128)(2,1)} fusion(bf16[129,5120]{1,0:T(8,128)(2,1)S(1)} %concatenate.3, s32[1024]{0:T(1024)S(1)} %fusion.37), kind=kCustom, calls=%fused_computation | custom fusion | bytes 20975616 | tf_op jit(solution)/shard_map/gather | solution.py:33
  23.7 11.9 %all-to-all-start.1 = ((bf16[128,8,5120]{2,1,0:T(8,128)(2,1)}), bf16[128,8,5120]{2,1,0:T(8,128)(2,1)}, u32[]{:S(2)}, u32[]{:S(2)}) async-start(bf16[128,8,5120]{2,1,0:T(8,128)(2,1)} %bitcast.68), calls=%async_computation.1 | async-start | bytes 20971520 | tf_op jit(solution)/shard_map/all_to_all | solution.py:37
  35.6 2.0 fusion.45
  37.6 126.9 %all-to-all-done.1 = bf16[128,8,5120]{2,1,0:T(8,128)(2,1)} async-done(((bf16[128,8,5120]{2,1,0:T(8,128)(2,1)}), bf16[128,8,5120]{2,1,0:T(8,128)(2,1)}, u32[]{:S(2)}, u32[]{:S(2)}) %all-to-all-start.1) | async-done | bytes 10485792 | tf_op jit(solution)/shard_map/all_to_all | solution.py:37
  164.5 13.5 %fusion.2 = f32[1024]{0:T(1024)S(1)} fusion(bf16[128,8,5120]{2,1,0:T(8,128)(2,1)} %all-to-all-done.1, bf16[1,768,5120]{2,1,0:T(8,128)(2,1)} %param.11, bf16[1,1024,768]{2,1,0:T(8,128)(2,1)S(1)} %copy-done), kind=kOutput, calls=%fused_computation.9 | convolution fusion | flops 8068791296 | bytes 19927040 | tf_op jit(solution)/shard_map/dot_general | solution.py:35
  177.9 0.7 all_to_all.18
  178.7 14.3 %all-to-all-start.2 = ((f32[128,1,8]{2,1,0:T(1,128)}), f32[128,1,8]{2,1,0:T(1,128)S(1)}, u32[]{:S(2)}, u32[]{:S(2)}) async-start(f32[128,1,8]{2,1,0:T(1,128)} %bitcast.13), calls=%async_computation.2 | async-start | bytes 131072 | tf_op jit(solution)/shard_map/all_to_all | solution.py:46
  192.9 0.1 copy.62
  193.1 0.1 reshape.137
  193.2 9.0 %all-to-all-done.2 = f32[128,1,8]{2,1,0:T(1,128)S(1)} async-done(((f32[128,1,8]{2,1,0:T(1,128)}), f32[128,1,8]{2,1,0:T(1,128)S(1)}, u32[]{:S(2)}, u32[]{:S(2)}) %all-to-all-start.2) | async-done | bytes 4128 | tf_op jit(solution)/shard_map/all_to_all | solution.py:46
  202.2 0.5 broadcast.108
  202.7 0.8 reduce.5
  203.5 0.1 reshape.118
  203.6 3.2 gather_fusion.1
  206.8 0.1 broadcast_in_dim.50
  207.0 0.1 copy.67
  207.0 0.3 select_reduce_fusion
  207.3 0.1 copy.68
  207.5 5.1 %gather_fusion.2 = f32[768]{0:T(1024)S(1)} fusion(f32[128,128]{0,1:T(8,128)S(1)} %get-tuple-element.25, s32[768]{0:T(1024)S(1)} %reshape.137), kind=kCustom, calls=%fused_computation.2 | custom fusion | bytes 12288 | tf_op jit(solution)/shard_map/jit(take_along_axis)/gather | solution.py:20
  212.6 0.1 reshape.140
  212.8 0.1 copy.64
  213.0 0.2 reshape.147
  213.1 8.6 %scatter_custom_fusion = bf16[1024]{0:T(1024)(128)(2,1)S(1)} fusion(s32[768]{0:T(1024)S(1)} %fusion.39, bf16[768]{0:T(1024)(128)(2,1)S(1)} %reshape.147, bf16[]{:T(256)} %constant.14.clone.1), kind=kCustom, calls=%fused_computation.58 | custom fusion | bytes 2050 | tf_op jit(solution)/shard_map/scatter | solution.py:30
  221.7 0.7 all_to_all.20
  222.5 4.8 %all-to-all-start = ((bf16[128,1,8]{2,1,0:T(2,128)(2,1)}), bf16[128,1,8]{2,1,0:T(2,128)(2,1)S(1)}, u32[]{:S(2)}, u32[]{:S(2)}) async-start(bf16[128,1,8]{2,1,0:T(2,128)(2,1)} %all_to_all.20), calls=%async_computation | async-start | bytes 131072 | tf_op jit(solution)/shard_map/all_to_all | solution.py:38
  227.3 0.3 all-reduce.4.cloned.1.call-start
  227.5 2.0 convolution_bitcast_fusion
  229.5 2.9 convolution_convert_fusion
  232.5 4.1 %all-to-all-done = bf16[128,1,8]{2,1,0:T(2,128)(2,1)S(1)} async-done(((bf16[128,1,8]{2,1,0:T(2,128)(2,1)}), bf16[128,1,8]{2,1,0:T(2,128)(2,1)S(1)}, u32[]{:S(2)}, u32[]{:S(2)}) %all-to-all-start) | async-done | bytes 2080 | tf_op jit(solution)/shard_map/all_to_all | solution.py:38
  236.5 0.1 convert_element_type.73
  236.6 16.9 %fusion.13 = bf16[1,768,5120]{1,2,0:T(8,128)(2,1)} fusion(bf16[128,8,5120]{2,1,0:T(8,128)(2,1)} %all-to-all-done.1, f32[128,8]{1,0:T(8,128)S(1)} %bitcast.69, bf16[1,1024,768]{2,1,0:T(8,128)(2,1)S(1)} %copy-done), kind=kOutput, calls=%fused_computation.16 | convolution fusion | flops 8072724480 | bytes 19927040 | tf_op jit(solution)/shard_map/dot_general | solution.py:56
  253.5 10.7 %copy.69 = bf16[1,768,5120]{2,1,0:T(8,128)(2,1)} copy(bf16[1,768,5120]{1,2,0:T(8,128)(2,1)} %fusion.13) | data formatting | bytes 15728640
  264.2 14.4 %fusion.23 = bf16[1,1024,768]{2,1,0:T(8,128)(2,1)} fusion(bf16[1,768,5120]{2,1,0:T(8,128)(2,1)} %param.11, bf16[128,8,5120]{2,1,0:T(8,128)(2,1)} %all-to-all-done.1, f32[128,8]{1,0:T(8,128)S(1)} %bitcast.70), kind=kOutput, calls=%fused_computation.22 | convolution fusion | flops 8069578752 | bytes 19927040 | tf_op jit(solution)/shard_map/dot_general | solution.py:53
  278.6 107.8 %all-reduce.4.cloned.1.call-done = f32[5120,128]{0,1:T(8,128)} async-done(((f32[5120,128]{0,1:T(8,128)}), f32[5120,128]{0,1:T(8,128)}) %all-reduce.4.cloned.1.call-update) | async-done | bytes 2621456
  386.4 1.0 constant_dynamic-slice_fusion
  387.3 0.7 copy.70
  (20 shorter events, 0.3 us)
Async XLA Ops:
  7.2 157.3 %copy-start = (bf16[1,1024,768]{2,1,0:T(8,128)(2,1)S(1)}, bf16[1,1024,768]{2,1,0:T(8,128)(2,1)}, u32[]{:S(2)}) copy-start(bf16[1,1024,768]{2,1,0:T(8,128)(2,1)} %param.10) | copy-start | bytes 4718596
  23.7 11.9 %copy-start.1 = (bf16[128,5120]{1,0:T(8,128)(2,1)S(1)}, bf16[128,5120]{1,0:T(8,128)(2,1)}, u32[]{:S(2)}) copy-start(bf16[128,5120]{1,0:T(8,128)(2,1)} %param.7) | copy-start | bytes 3932164
  23.7 13.9 %copy-start.2 = (s32[128,6]{0,1:T(8,128)S(1)}, s32[128,6]{0,1:T(8,128)}, u32[]{:S(2)}) copy-start(s32[128,6]{0,1:T(8,128)} %param.9) | copy-start | bytes 9220
  23.7 140.8 %all-to-all-start.1 = ((bf16[128,8,5120]{2,1,0:T(8,128)(2,1)}), bf16[128,8,5120]{2,1,0:T(8,128)(2,1)}, u32[]{:S(2)}, u32[]{:S(2)}) async-start(bf16[128,8,5120]{2,1,0:T(8,128)(2,1)} %bitcast.68), calls=%async_computation.1 | async-start | bytes 20971520 | tf_op jit(solution)/shard_map/all_to_all | solution.py:37
  178.7 23.6 %all-to-all-start.2 = ((f32[128,1,8]{2,1,0:T(1,128)}), f32[128,1,8]{2,1,0:T(1,128)S(1)}, u32[]{:S(2)}, u32[]{:S(2)}) async-start(f32[128,1,8]{2,1,0:T(1,128)} %bitcast.13), calls=%async_computation.2 | async-start | bytes 131072 | tf_op jit(solution)/shard_map/all_to_all | solution.py:46
  222.5 14.1 %all-to-all-start = ((bf16[128,1,8]{2,1,0:T(2,128)(2,1)}), bf16[128,1,8]{2,1,0:T(2,128)(2,1)S(1)}, u32[]{:S(2)}, u32[]{:S(2)}) async-start(bf16[128,1,8]{2,1,0:T(2,128)(2,1)} %all_to_all.20), calls=%async_computation | async-start | bytes 131072 | tf_op jit(solution)/shard_map/all_to_all | solution.py:38
  227.3 159.1 %all-reduce.4.cloned.1.call-start = ((), (), s32[]{:S(2)}) async-start(), calls=%async_computation.3 | async-start | bytes 5242880
Sparse Core Ops, SparseCore 0:
  232.9 153.3 all-reduce.3
where the time goes:
time: 396 us; the launch traced here: 395 us
  waiting for transfers between devices  248 us (63%)
  matrix products  51.7 us (13%)
  local copies, waits for them, and re-layouts  47.4 us (12%)
  starting transfers between devices  31.2 us (8%)
  between operations  14.3 us (4%)
    all_to_all x1, waiting for transfers between devices, body(): lax.all_to_all(send_rows, ('dp', 'tensor'), split_axis=0, concat_axis=0,...  127 us
    unnamed x2, waiting for transfers between devices  108 us
    dot_general x1, matrix products, body(): lax.dot_general(hidden_rows, local_grad, (((0,), (0,)), ((), ())), prefer...  16.9 us
    dot_general x1, matrix products, body(): lax.dot_general(local_grad, weight, (((1,), (1,)), ((), ())), preferred_e...  14.4 us
    all_to_all x1, starting transfers between devices, body(): lax.all_to_all(slot_score.reshape(groups, capacity), ('dp', 'tensor'), sp...  14.3 us
    dot_general x1, matrix products, body(): jnp.dot(hidden_rows, weight, preferred_element_type=jnp.float32)  13.5 us
    unnamed x10, local copies, waits for them, and re-layouts  13.1 us
    all_to_all x1, starting transfers between devices, body(): lax.all_to_all(send_rows, ('dp', 'tensor'), split_axis=0, concat_axis=0,...  11.9 us
  transfers between devices with their start and end apart: 4, of which 4 were waited for; matrix products, arithmetic and copies ran while one was open for 12% of the time, Pallas kernels for 0%

commit v1 on v0

v1 whole, which is shorter than its diff:
```python
import functools

import jax
import jax.numpy as jnp
from jax import lax
from jax.experimental import pallas as pl
from jax.experimental.pallas import tpu as pltpu
from jax.sharding import Mesh, PartitionSpec as P

route_scale = 16.0
ALL = ("dp", "z", "c")
CHIPS = ("dp", "z")
MIB = 1 << 20
NT = (((1,), (1,)), ((), ()))


def tile(size, best):
    return best if size % best == 0 else size


def route_kernel(capacity, ids_ref, grad_ref, rows_ref, code_ref, pick):
    @pl.when(pl.program_id(0) == 0)
    def _():
        experts, tokens = code_ref.shape
        expert = lax.broadcasted_iota(jnp.int32, (experts, tokens), 0)
        hit = ids_ref[0:1, :] == expert
        for k in range(1, ids_ref.shape[0]):
            hit = hit | (ids_ref[k : k + 1, :] == expert)
        earlier = lax.broadcasted_iota(jnp.int32, (tokens, tokens), 0)
        later = lax.broadcasted_iota(jnp.int32, (tokens, tokens), 1)
        before = jnp.where(earlier < later, 1.0, 0.0).astype(jnp.bfloat16)
        chosen = jnp.where(hit, 1.0, 0.0).astype(jnp.bfloat16)
        rank = jnp.dot(chosen, before, preferred_element_type=jnp.float32)
        code = jnp.where(hit, rank, -1.0)
        code_ref[...] = code
        slot = lax.broadcasted_iota(jnp.int32, (experts, capacity, tokens), 1).astype(jnp.float32)
        one = jnp.where(code[:, None, :] == slot, 1.0, 0.0)
        pick[...] = one.reshape(experts * capacity, tokens).astype(jnp.bfloat16)

    rows_ref[...] = jnp.dot(
        pick[...], grad_ref[...], preferred_element_type=jnp.float32
    ).astype(rows_ref.dtype)


def route(ids_t, out_grad, experts, capacity):
    tokens, width = out_grad.shape
    step = tile(width, 640)
    slots = experts * capacity
    return pl.pallas_call(
        functools.partial(route_kernel, capacity),
        grid=(width // step,),
        in_specs=[
            pl.BlockSpec(ids_t.shape, lambda i: (0, 0)),
            pl.BlockSpec((tokens, step), lambda i: (0, i)),
        ],
        out_specs=[
            pl.BlockSpec((slots, step), lambda i: (0, i)),
            pl.BlockSpec((experts, tokens), lambda i: (0, 0)),
        ],
        out_shape=[
            jax.ShapeDtypeStruct((slots, width), out_grad.dtype),
            jax.ShapeDtypeStruct((experts, tokens), jnp.float32),
        ],
        scratch_shapes=[pltpu.VMEM((slots, tokens), jnp.bfloat16)],
        compiler_params=pltpu.CompilerParams(vmem_limit_bytes=24 * MIB),
        cost_estimate=pl.CostEstimate(
            flops=2 * slots * tokens * width,
            bytes_accessed=2 * (slots + tokens) * width,
            transcendentals=0,
        ),
        name="route_rows",
    )(ids_t, out_grad)


def score_kernel(capacity, rows_ref, weight_ref, hidden_ref, gate_ref, dh_ref, score_ref, acc):
    step = pl.program_id(0)
    part = lax.dot_general(
        rows_ref[...], weight_ref[...], NT, preferred_element_type=jnp.float32
    )

    @pl.when(step == 0)
    def _():
        acc[...] = part

    @pl.when(step > 0)
    def _():
        acc[...] += part

    @pl.when(step == pl.num_programs(0) - 1)
    def _():
        slots = acc.shape[0]
        group = 2 * capacity
        total = acc[...]
        dh_ref[...] = (total * gate_ref[...]).astype(dh_ref.dtype)
        score = jnp.sum(total * hidden_ref[...].astype(jnp.float32), axis=1, keepdims=True)
        row = lax.broadcasted_iota(jnp.int32, (slots, 128), 0) % group
        lane = lax.broadcasted_iota(jnp.int32, (slots, 128), 1)
        spread = jnp.where(row == lane, score, 0.0)
        score_ref[...] = jnp.sum(spread.reshape(slots // group, group, 128), axis=1)


def scores(rows, weight, hidden, gate, capacity):
    slots, width = rows.shape
    units = weight.shape[0]
    step = tile(width, 512)
    return pl.pallas_call(
        functools.partial(score_kernel, capacity),
        grid=(width // step,),
        in_specs=[
            pl.BlockSpec((slots, step), lambda i: (0, i)),
            pl.BlockSpec((units, step), lambda i: (0, i)),
            pl.BlockSpec((slots, units), lambda i: (0, 0)),
            pl.BlockSpec((slots, 1), lambda i: (0, 0)),
        ],
        out_specs=[
            pl.BlockSpec((slots, units), lambda i: (0, 0)),
            pl.BlockSpec((slots // (2 * capacity), 128), lambda i: (0, 0)),
        ],
        out_shape=[
            jax.ShapeDtypeStruct((slots, units), jnp.bfloat16),
            jax.ShapeDtypeStruct((slots // (2 * capacity), 128), jnp.float32),
        ],
        scratch_shapes=[pltpu.VMEM((slots, units), jnp.float32)],
        compiler_params=pltpu.CompilerParams(vmem_limit_bytes=40 * MIB),
        cost_estimate=pl.CostEstimate(
            flops=2 * slots * units * width,
            bytes_accessed=2 * (slots + units) * width + 4 * slots * units,
            transcendentals=0,
        ),
        name="score_rows",
    )(rows, weight, hidden, gate)


def product_kernel(left_ref, right_ref, out_ref):
    out_ref[...] = jnp.dot(
        left_ref[...], right_ref[...], preferred_element_type=jnp.float32
    ).astype(out_ref.dtype)


def product(left, right, name):
    m, k = left.shape
    n = right.shape[1]
    step = tile(n, 512)
    return pl.pallas_call(
        product_kernel,
        grid=(n // step,),
        in_specs=[
            pl.BlockSpec((m, k), lambda i: (0, 0)),
            pl.BlockSpec((k, step), lambda i: (0, i)),
        ],
        out_specs=pl.BlockSpec((m, step), lambda i: (0, i)),
        out_shape=jax.ShapeDtypeStruct((m, n), jnp.bfloat16),
        compiler_params=pltpu.CompilerParams(vmem_limit_bytes=32 * MIB),
        cost_estimate=pl.CostEstimate(
            flops=2 * m * n * k, bytes_accessed=2 * (m * k + k * n + m * n), transcendentals=0
        ),
        name=name,
    )(left, right)


def router_kernel(capacity, back_ref, code_ref, prob_ref, normed_ref, terms_ref, grad_ref):
    halves, experts, tokens = code_ref.shape
    parts = []
    for half in range(halves):
        code = code_ref[half]
        prob = prob_ref[half]
        gate_grad = jnp.zeros((experts, tokens), jnp.float32)
        for r in range(capacity):
            at = half * capacity + r
            gate_grad = jnp.where(code == r, back_ref[:, at : at + 1], gate_grad)
        prob_grad = route_scale * gate_grad
        mean = jnp.sum(prob * prob_grad, axis=0, keepdims=True)
        parts.append(prob * (prob_grad - mean))
    grad = jnp.concatenate(parts, axis=1).astype(jnp.bfloat16)
    grad_ref[...] = grad
    terms_ref[...] = lax.dot_general(
        normed_ref[...], grad, NT, preferred_element_type=jnp.float32
    ).astype(terms_ref.dtype)


def router_terms(back, code, prob, normed_t, capacity):
    experts = back.shape[0]
    columns, tokens = normed_t.shape
    return pl.pallas_call(
        functools.partial(router_kernel, capacity),
        out_shape=[
            jax.ShapeDtypeStruct((columns, experts), jnp.bfloat16),
            jax.ShapeDtypeStruct((experts, tokens), jnp.bfloat16),
        ],
        compiler_params=pltpu.CompilerParams(vmem_limit_bytes=32 * MIB),
        cost_estimate=pl.CostEstimate(
            flops=2 * columns * experts * tokens,
            bytes_accessed=2 * columns * (experts + tokens),
            transcendentals=0,
        ),
        name="router_terms",
    )(back, code, prob, normed_t)


def all_to_all(x, axes):
    return lax.all_to_all(x, axes, split_axis=0, concat_axis=0, tiled=True)


def body(out_grad, normed, router, expert_ids, hidden_act, down_weight):
    groups = lax.axis_size(ALL)
    core = lax.axis_index("c")
    me = lax.axis_index(ALL)
    tokens, width = out_grad.shape
    experts = router.shape[1]
    hidden = hidden_act[0]
    weight = down_weight[0]
    capacity = hidden.shape[0] // groups
    slots = groups * capacity
    swap = [(0, 1), (1, 0)]

    send_rows, code_t = route(expert_ids.T, out_grad, experts, capacity)
    rows = all_to_all(send_rows.reshape(experts, capacity, width), ALL)
    rows = rows.reshape(slots, width)

    logits = jnp.dot(normed, router, preferred_element_type=jnp.float32)
    prob = jax.nn.softmax(logits, axis=-1)
    gates = (route_scale * prob).astype(jnp.bfloat16)
    code = code_t.T
    slot = jnp.arange(capacity, dtype=jnp.int32).astype(jnp.float32)
    slot_gate = jnp.sum(
        jnp.where(code[None] == slot[:, None, None], gates[None].astype(jnp.float32), 0.0), axis=1
    ).astype(jnp.bfloat16)
    all_gates = lax.all_gather(slot_gate, ALL, axis=0, tiled=False)
    mine = jnp.arange(experts, dtype=jnp.int32) == me
    gate = jnp.sum(jnp.where(mine, all_gates.astype(jnp.float32), 0.0), axis=2)
    gate = gate.reshape(slots, 1)
    gated_hidden_t = (gate * hidden.astype(jnp.float32)).astype(jnp.bfloat16).T

    own = jnp.stack([code_t, prob.T])
    other = lax.ppermute(own, "c", swap)
    first = core == 0
    pair = jnp.stack([jnp.where(first, own, other), jnp.where(first, other, own)], axis=1)
    halves = normed.T.reshape(groups // 2, 2, width // groups, tokens)
    keep = lax.dynamic_index_in_dim(halves, core, 1, keepdims=False)
    give = lax.dynamic_index_in_dim(halves, 1 - core, 1, keepdims=False)
    taken = lax.ppermute(give, "c", swap)
    pair_normed = jnp.where(
        first,
        jnp.concatenate([keep, taken], axis=2),
        jnp.concatenate([taken, keep], axis=2),
    ).reshape(width // 2, 2 * tokens)

    d_hidden, score = scores(rows, weight, hidden, gate, capacity)
    score = jnp.broadcast_to(score[:, None, :], (groups // 2, 2, 128)).reshape(groups, 128)
    back = all_to_all(score, ALL)
    d_down = product(gated_hidden_t, rows, "down_grad")

    terms, logit_grad_t = router_terms(back, pair[0], pair[1], pair_normed, capacity)
    got = all_to_all(terms.reshape(groups // 2, width // groups, experts), CHIPS)
    logit_grad = lax.dynamic_slice_in_dim(logit_grad_t, core * tokens, tokens, 1).T
    d_normed = lax.dot_general(
        logit_grad, router, NT, preferred_element_type=jnp.float32
    ).astype(jnp.bfloat16)
    d_router = jnp.sum(got.astype(jnp.float32), axis=0)
    return d_down[None], d_hidden[None], d_router, d_normed


def solution(mesh):
    dp, tensor = mesh.devices.shape
    fine = Mesh(mesh.devices.reshape(dp, tensor // 2, 2), ALL)
    in_specs = (
        P(ALL, None),
        P(ALL, None),
        P(),
        P(ALL, None),
        P(ALL, None, None),
        P(ALL, None, None),
    )
    out_specs = (P(ALL, None, None), P(ALL, None, None), P(ALL, None), P(ALL, None))
    return jax.shard_map(body, mesh=fine, in_specs=in_specs, out_specs=out_specs, check_vma=False)
```

time: 396 us -> 254 us (0.64)
  waiting for transfers between devices: 248 us -> 7.22 us
  blocking collectives: 0 us -> 155 us
  matrix products: 51.7 us -> 2.22 us
  Pallas kernels: 0 us -> 38.3 us
  local copies, waits for them, and re-layouts: 47.4 us -> 18.9 us
  between operations: 14.3 us -> 0.85 us
  starting transfers between devices: 31.2 us -> 24 us
  other arithmetic: 2.7 us -> 7.03 us
    all_gather x0 -> x1, blocking collectives: none -> 155 us  [body(): all_gates = lax.all_gather(slot_gate, ALL, axis=0, tiled=False)]
    all_to_all x3, waiting for transfers between devices: 140 us -> 7.22 us  [all_to_all(): return lax.all_to_all(x, axes, split_axis=0, concat_axis=0, tiled=True)]
    unnamed x2 -> x0, waiting for transfers between devices: 108 us -> none
    dot_general x5 -> x1, matrix products: 49.7 us -> 1.59 us  [body(): lax.dot_general(logit_grad, router, NT, preferred_element_type=jnp.float32)]
    pallas_call x0 -> x4, Pallas kernels: none -> 38.3 us  [the longest x1 16.6 us: scores(): pl.pallas_call(functools.partial(score_kernel, capacity), grid=(width //...]
    gather x7 -> x0, local copies, waits for them, and re-layouts: 17.4 us -> none  [the longest x1 8.69 us: body(): send_rows = padded[token_of_row].reshape(groups, capacity, model_width)]
    scatter x2 -> x0, local copies, waits for them, and re-layouts: 12 us -> none  [the longest x1 8.61 us: body(): jnp.zeros((groups * capacity,), jnp.bfloat16).at[slot_rows]]
    all_to_all x3, starting transfers between devices: 30.9 us -> 22.9 us  [all_to_all(): return lax.all_to_all(x, axes, split_axis=0, concat_axis=0, tiled=True)]
  transfers between devices with their start and end apart: 4 -> 5, of which waited for: 4 -> 1; matrix products, arithmetic and copies ran while one was open for 12% -> 6% of each run, Pallas kernels for 0% -> 12%
where the time goes in v1:
time: 254 us; the launch traced here: 253 us
  blocking collectives  155 us (61%)
  Pallas kernels  38.3 us (15%)
  starting transfers between devices  24 us (9%)
  local copies, waits for them, and re-layouts  18.9 us (7%)
  waiting for transfers between devices  7.22 us (3%)
  other arithmetic  7.03 us (3%)
    all_gather x1, blocking collectives, body(): all_gates = lax.all_gather(slot_gate, ALL, axis=0, tiled=False)  155 us
    all_to_all x3, starting transfers between devices, all_to_all(): return lax.all_to_all(x, axes, split_axis=0, concat_axis=0, tiled=True)  22.9 us
    pallas_call x1, Pallas kernels, scores(): pl.pallas_call(functools.partial(score_kernel, capacity), grid=(width //...  16.6 us
    pallas_call x1, Pallas kernels, product(): pl.pallas_call(product_kernel, grid=(n // step,), in_specs=[pl.BlockSpec(...  14.4 us
    unnamed x25, local copies, waits for them, and re-layouts  12.6 us
    all_to_all x3, waiting for transfers between devices, all_to_all(): return lax.all_to_all(x, axes, split_axis=0, concat_axis=0, tiled=True)  7.22 us
    pallas_call x1, Pallas kernels, route(): pl.pallas_call(functools.partial(route_kernel, capacity), grid=(width //...  5.5 us
  transfers between devices with their start and end apart: 5, of which 1 were waited for; matrix products, arithmetic and copies ran while one was open for 6% of the time, Pallas kernels for 12%

profile of v1, /device:TPU:1, one launch (start us, length us, event | category | flops | bytes accessed | tf_op | source)
XLA Modules:
  0.0 253.5 jit_solution(14084150130595798479)
XLA Ops:
  0.6 0.0 copy-start
  0.6 0.0 copy-start.7
  0.7 1.4 copy-done.7
  2.1 0.7 copy-done.8
  2.8 5.5 %route_rows.1 = (bf16[1024,5120]{1,0:T(8,128)(2,1)S(1)}, f32[128,128]{1,0:T(8,128)S(1)}) custom-call(s32[6,128]{1,0:T(8,128)S(1)} %bitcast.49, bf16[128,5120]{1,0:T(8,128)(2,1)S(1)} %copy-done.7), custom_call_target="tpu_custom_call" | custom-call | flops 1342177280 | bytes 11796480 | tf_op jit(solution)/shard_map/route_rows/pallas_call | solution.py:49
  8.3 0.0 copy-start.1
  8.3 3.8 %copy-done.1 = bf16[1024,5120]{1,0:T(8,128)(2,1)} copy-done((bf16[1024,5120]{1,0:T(8,128)(2,1)}, bf16[1024,5120]{1,0:T(8,128)(2,1)S(1)}, u32[]{:S(2)}) %copy-start.1) | copy-done | bytes 10485784
  12.1 11.9 %all-to-all-start = ((bf16[128,8,5120]{2,1,0:T(8,128)(2,1)}), bf16[128,8,5120]{2,1,0:T(8,128)(2,1)}, u32[]{:S(2)}, u32[]{:S(2)}) async-start(bf16[128,8,5120]{2,1,0:T(8,128)(2,1)} %bitcast.42), calls=%async_computation | async-start | bytes 20971520 | tf_op jit(solution)/shard_map/all_to_all | solution.py:201
  24.0 0.0 copy-done
  24.0 0.0 copy-done.9
  24.0 0.6 fusion.11
  24.7 0.0 copy-start.10
  24.7 0.6 copy-done.10
  25.3 0.7 pad_maximum_fusion.1
  26.0 1.1 collective-permute-start
  27.1 1.4 copy.33
  28.6 2.6 %constant_dynamic-slice_fusion = (bf16[64,1,40,128]{3,2,1,0:T(8,128)(2,1)}, bf16[64,40,128]{2,1,0:T(8,128)(2,1)}) fusion(bf16[64,2,40,128]{3,2,1,0:T(8,128)(2,1)} %bitcast.50, s32[]{:T(128)S(6)} %select_n.45, s32[]{:T(128)S(6)} %select_n.46), kind=kLoop, calls=%fused_computation.26 | loop fusion | bytes 2621448 | tf_op jit(solution)/shard_map/jit(dynamic_index_in_dim)/dynamic_slice | solution.py:239
  31.2 0.0 collective-permute-start.1
  31.2 0.1 copy.29
  31.3 0.1 copy.28
  31.4 0.1 select_reduce_fusion
  31.6 154.9 %all-gather = bf16[1024,128]{1,0:T(8,128)(2,1)S(1)} all-gather(bf16[8,128]{1,0:T(8,128)(2,1)S(1)} %select_reduce_fusion), channel_id=2, replica_groups=mesh['dp'=16,'z'=4,'c'=2] {'dp','z','c'}, dimensions={0}, use_global_device_ids=true | all-gather | bytes 264192 | tf_op jit(solution)/shard_map/all_gather | solution.py:228
  186.5 0.2 fusion.1
  186.7 0.1 mul.29
  186.8 0.0 copy-done.2
  186.8 1.5 fusion
  188.3 0.2 reshape.60.gate_ref
  188.5 2.6 %copy.30.left_ref = bf16[768,1024]{1,0:T(8,128)(2,1)} copy(bf16[768,1024]{0,1:T(8,128)(2,1)} %fusion) | data formatting | bytes 3145728 | tf_op jit(solution)/shard_map/transpose | solution.py:232
  191.1 0.0 collective-permute-done
  191.1 0.9 select_bitcast_fusion
  192.0 0.7 fusion.4
  192.7 0.0 all-to-all-done
  192.7 3.2 %copy-done.6 = bf16[1,768,5120]{2,1,0:T(8,128)(2,1)S(1)} copy-done((bf16[1,768,5120]{2,1,0:T(8,128)(2,1)S(1)}, bf16[1,768,5120]{2,1,0:T(8,128)(2,1)}, u32[]{:S(2)}) %copy-start.6) | copy-done | bytes 7864344
  196.0 16.6 %score_rows.1 = (bf16[1024,768]{1,0:T(8,128)(2,1)}, f32[64,128]{1,0:T(8,128)S(1)}) custom-call(bf16[1024,5120]{1,0:T(8,128)(2,1)} %bitcast.6.right_ref.rows_ref, bf16[768,5120]{1,0:T(8,128)(2,1)S(1)} %bitcast.48, bf16[1024,768]{1,0:T(8,128)(2,1)S(1)} %bitcast.43, f32[1024,1]{1,0:T(8,128)S(1)} %reshape.60.gate_ref), custom_call_target="tpu_custom_call" | custom-call | flops 8053063680 | bytes 21495808 | tf_op jit(solution)/shard_map/score_rows/pallas_call | solution.py:106
  212.5 0.6 broadcast_in_dim.43
  213.2 6.0 %all-to-all-start.1 = ((f32[128,1,128]{2,1,0:T(1,128)}), f32[128,1,128]{2,1,0:T(1,128)S(1)}, u32[]{:S(2)}, u32[]{:S(2)}) async-start(f32[128,1,128]{2,1,0:T(1,128)} %bitcast.10), calls=%async_computation.1 | async-start | bytes 131072 | tf_op jit(solution)/shard_map/all_to_all | solution.py:201
  219.1 0.0 collective-permute-done.1
  219.1 0.0 copy-start.4
  219.2 2.1 maximum_select_fusion.normed_ref
  221.3 7.2 %all-to-all-done.1 = f32[128,1,128]{2,1,0:T(1,128)S(1)} async-done(((f32[128,1,128]{2,1,0:T(1,128)}), f32[128,1,128]{2,1,0:T(1,128)S(1)}, u32[]{:S(2)}, u32[]{:S(2)}) %all-to-all-start.1) | async-done | bytes 65568 | tf_op jit(solution)/shard_map/all_to_all | solution.py:201
  228.5 1.9 router_terms.1
  230.4 5.0 %all-to-all-start.2 = ((bf16[64,40,128]{2,1,0:T(8,128)(2,1)}), bf16[64,40,128]{2,1,0:T(8,128)(2,1)S(1)}, u32[]{:S(2)}, u32[]{:S(2)}) async-start(bf16[64,40,128]{2,1,0:T(8,128)(2,1)} %bitcast.26), calls=%async_computation.2 | async-start | bytes 1310720 | tf_op jit(solution)/shard_map/all_to_all | solution.py:201
  235.4 0.0 copy-start.3
  235.4 1.4 copy-done.3
  236.8 14.4 %down_grad.1 = bf16[768,5120]{1,0:T(8,128)(2,1)} custom-call(bf16[768,1024]{1,0:T(8,128)(2,1)S(1)} %copy-done.3, bf16[1024,5120]{1,0:T(8,128)(2,1)} %bitcast.6.right_ref.rows_ref), custom_call_target="tpu_custom_call" | custom-call | flops 8053063680 | bytes 19922944 | tf_op jit(solution)/shard_map/down_grad/pallas_call | solution.py:144
  251.2 1.6 convolution_convert_fusion
  252.7 0.0 all-to-all-done.2
  252.7 0.7 convert_reduce_fusion
  (13 shorter events, 0.1 us)
Async XLA Ops:
  0.6 23.4 %copy-start = (bf16[5120,128]{1,0:T(8,128)(2,1)S(1)}, bf16[5120,128]{1,0:T(8,128)(2,1)}, u32[]{:S(2)}) copy-start(bf16[5120,128]{1,0:T(8,128)(2,1)} %param.8) | copy-start | bytes 3932164
  0.6 1.4 copy-start.7
  2.1 0.7 copy-start.8
  8.3 3.8 %copy-start.1 = (bf16[1024,5120]{1,0:T(8,128)(2,1)}, bf16[1024,5120]{1,0:T(8,128)(2,1)S(1)}, u32[]{:S(2)}) copy-start(bf16[1024,5120]{1,0:T(8,128)(2,1)S(1)} %get-tuple-element.11) | copy-start | bytes 31457284
  12.1 11.9 %copy-start.9 = (bf16[128,5120]{1,0:T(8,128)(2,1)S(1)}, bf16[128,5120]{1,0:T(8,128)(2,1)}, u32[]{:S(2)}) copy-start(bf16[128,5120]{1,0:T(8,128)(2,1)} %param.7) | copy-start | bytes 3932164
  12.1 180.6 %all-to-all-start = ((bf16[128,8,5120]{2,1,0:T(8,128)(2,1)}), bf16[128,8,5120]{2,1,0:T(8,128)(2,1)}, u32[]{:S(2)}, u32[]{:S(2)}) async-start(bf16[128,8,5120]{2,1,0:T(8,128)(2,1)} %bitcast.42), calls=%async_computation | async-start | bytes 20971520 | tf_op jit(solution)/shard_map/all_to_all | solution.py:201
  24.7 0.6 copy-start.10
  26.0 165.1 %collective-permute-start = (f32[2,128,128]{2,1,0:T(8,128)}, f32[2,128,128]{2,1,0:T(8,128)}, u32[]{:S(2)}, u32[]{:S(2)}) collective-permute-start(f32[2,128,128]{2,1,0:T(8,128)} %pad_maximum_fusion.1), channel_id=1, source_target_pairs={{0,1},{1,0},{2,3},{3,2},{4,5},{5,4},{6,7},{7,6},{8,9},{9,8},{10,11... | collective-permute-start | bytes 393224 | tf_op jit(solution)/shard_map/ppermute | solution.py:235
  28.6 158.2 %copy-start.2 = (bf16[1,1024,768]{2,1,0:T(8,128)(2,1)S(1)}, bf16[1,1024,768]{2,1,0:T(8,128)(2,1)}, u32[]{:S(2)}) copy-start(bf16[1,1024,768]{2,1,0:T(8,128)(2,1)} %param.10) | copy-start | bytes 4718596
  31.2 187.9 %collective-permute-start.1 = (bf16[64,40,128]{2,1,0:T(8,128)(2,1)}, bf16[64,40,128]{2,1,0:T(8,128)(2,1)}, u32[]{:S(2)}, u32[]{:S(2)}) collective-permute-start(bf16[64,40,128]{2,1,0:T(8,128)(2,1)} %get-tuple-element.17), channel_id=1, source_target_pairs={{0,1},{1,0},{2,3},{3,2},{4,5},{5,4},{6,7},{7,6},{8,9},{9,8},{10,11... | collective-permute-start | bytes 1966088 | tf_op jit(solution)/shard_map/ppermute | solution.py:241
  188.5 2.6 %copy-start.11 = (f32[1,128,128]{2,1,0:T(8,128)S(1)}, f32[1,128,128]{2,1,0:T(8,128)}, u32[]{:S(2)}) copy-start(f32[1,128,128]{2,1,0:T(8,128)} %copy-done.10) | copy-start | bytes 196612
  192.7 3.2 %copy-start.6 = (bf16[1,768,5120]{2,1,0:T(8,128)(2,1)S(1)}, bf16[1,768,5120]{2,1,0:T(8,128)(2,1)}, u32[]{:S(2)}) copy-start(bf16[1,768,5120]{2,1,0:T(8,128)(2,1)} %param.11) | copy-start | bytes 23592964
  213.2 15.3 %all-to-all-start.1 = ((f32[128,1,128]{2,1,0:T(1,128)}), f32[128,1,128]{2,1,0:T(1,128)S(1)}, u32[]{:S(2)}, u32[]{:S(2)}) async-start(f32[128,1,128]{2,1,0:T(1,128)} %bitcast.10), calls=%async_computation.1 | async-start | bytes 131072 | tf_op jit(solution)/shard_map/all_to_all | solution.py:201
  219.1 9.3 %copy-start.4 = (f32[2,128,128]{2,1,0:T(8,128)S(1)}, f32[2,128,128]{2,1,0:T(8,128)}, u32[]{:S(2)}) copy-start(f32[2,128,128]{2,1,0:T(8,128)} %get-tuple-element.18.prob_ref) | copy-start | bytes 393220
  219.2 9.3 %copy-start.5 = (f32[2,128,128]{2,1,0:T(8,128)S(1)}, f32[2,128,128]{2,1,0:T(8,128)}, u32[]{:S(2)}) copy-start(f32[2,128,128]{2,1,0:T(8,128)} %get-tuple-element.19.code_ref) | copy-start | bytes 393220
  230.4 22.4 %all-to-all-start.2 = ((bf16[64,40,128]{2,1,0:T(8,128)(2,1)}), bf16[64,40,128]{2,1,0:T(8,128)(2,1)S(1)}, u32[]{:S(2)}, u32[]{:S(2)}) async-start(bf16[64,40,128]{2,1,0:T(8,128)(2,1)} %bitcast.26), calls=%async_computation.2 | async-start | bytes 1310720 | tf_op jit(solution)/shard_map/all_to_all | solution.py:201
  235.4 1.4 copy-start.3

commit v2 on v1

v2 whole, which is shorter than its diff:
```python
import functools

import jax
import jax.numpy as jnp
from jax import lax
from jax.experimental import pallas as pl
from jax.experimental.pallas import tpu as pltpu
from jax.sharding import Mesh, PartitionSpec as P

route_scale = 16.0
ALL = ("dp", "z", "c")
CHIPS = ("dp", "z")
MIB = 1 << 20
NT = (((1,), (1,)), ((), ()))
TN = (((0,), (0,)), ((), ()))


def cut(size, best):
    return best if size % best == 0 else size


def spread_columns(pick_ref, grad_ref, rows_hbm, rows, sem):
    width = rows.shape[1]
    step = cut(width, 512)
    copies = []
    for n in range(0, width, step):
        rows[:, n : n + step] = jnp.dot(
            pick_ref[...], grad_ref[:, n : n + step], preferred_element_type=jnp.float32
        ).astype(rows.dtype)
        columns = (slice(None), pl.ds(n, step))
        copy = pltpu.make_async_copy(rows.at[columns], rows_hbm.at[columns], sem.at[n // step])
        copy.start()
        copies.append(copy)
    for copy in copies:
        copy.wait()


def route_kernel(capacity, ids_ref, grad_ref, rows_hbm, code_ref, pick_ref, rows, sem):
    experts, tokens = code_ref.shape
    expert = lax.broadcasted_iota(jnp.int32, (experts, tokens), 0)
    hit = ids_ref[0:1, :] == expert
    for k in range(1, ids_ref.shape[0]):
        hit = hit | (ids_ref[k : k + 1, :] == expert)
    earlier = lax.broadcasted_iota(jnp.int32, (tokens, tokens), 0)
    later = lax.broadcasted_iota(jnp.int32, (tokens, tokens), 1)
    before = jnp.where(earlier < later, 1.0, 0.0).astype(jnp.bfloat16)
    chosen = jnp.where(hit, 1.0, 0.0).astype(jnp.bfloat16)
    rank = jnp.dot(chosen, before, preferred_element_type=jnp.float32)
    code = jnp.where(hit, rank, -1.0)
    code_ref[...] = code
    slot = lax.broadcasted_iota(jnp.int32, (experts, capacity, tokens), 1).astype(jnp.float32)
    one = jnp.where(code[:, None, :] == slot, 1.0, 0.0)
    pick_ref[...] = one.reshape(experts * capacity, tokens).astype(jnp.bfloat16)
    spread_columns(pick_ref, grad_ref, rows_hbm, rows, sem)


def route(ids_t, out_grad, experts, capacity, first, width):
    tokens = out_grad.shape[0]
    slots = experts * capacity
    return pl.pallas_call(
        functools.partial(route_kernel, capacity),
        grid=(1,),
        in_specs=[
            pl.BlockSpec(ids_t.shape, lambda i: (0, 0)),
            pl.BlockSpec((tokens, width), lambda i: (0, first // width)),
        ],
        out_specs=[
            pl.BlockSpec(memory_space=pl.ANY),
            pl.BlockSpec((experts, tokens), lambda i: (0, 0)),
            pl.BlockSpec((slots, tokens), lambda i: (0, 0)),
        ],
        out_shape=[
            jax.ShapeDtypeStruct((slots, width), out_grad.dtype),
            jax.ShapeDtypeStruct((experts, tokens), jnp.float32),
            jax.ShapeDtypeStruct((slots, tokens), jnp.bfloat16),
        ],
        scratch_shapes=[
            pltpu.VMEM((slots, width), out_grad.dtype),
            pltpu.SemaphoreType.DMA((width // cut(width, 512),)),
        ],
        compiler_params=pltpu.CompilerParams(vmem_limit_bytes=56 * MIB),
        cost_estimate=pl.CostEstimate(
            flops=2 * slots * tokens * width,
            bytes_accessed=2 * (slots + tokens) * width,
            transcendentals=0,
        ),
        name="route_rows",
    )(ids_t, out_grad)


def route_rest(pick, out_grad, first, width):
    slots, tokens = pick.shape
    return pl.pallas_call(
        spread_columns,
        grid=(1,),
        in_specs=[
            pl.BlockSpec((slots, tokens), lambda i: (0, 0)),
            pl.BlockSpec((tokens, width), lambda i: (0, first // width)),
        ],
        out_specs=pl.BlockSpec(memory_space=pl.ANY),
        out_shape=jax.ShapeDtypeStruct((slots, width), out_grad.dtype),
        scratch_shapes=[
            pltpu.VMEM((slots, width), out_grad.dtype),
            pltpu.SemaphoreType.DMA((width // cut(width, 512),)),
        ],
        compiler_params=pltpu.CompilerParams(vmem_limit_bytes=56 * MIB),
        cost_estimate=pl.CostEstimate(
            flops=2 * slots * tokens * width,
            bytes_accessed=2 * (slots + tokens) * width,
            transcendentals=0,
        ),
        name="route_rest",
    )(pick, out_grad)


def first_half_kernel(rows_ref, weight_ref, out_ref):
    part = lax.dot_general(
        rows_ref[...], weight_ref[...], NT, preferred_element_type=jnp.float32
    )

    @pl.when(pl.program_id(0) == 0)
    def _():
        out_ref[...] = part

    @pl.when(pl.program_id(0) > 0)
    def _():
        out_ref[...] += part


def first_half(rows, weight):
    slots, width = rows.shape
    units = weight.shape[0]
    step = cut(width, 1280)
    return pl.pallas_call(
        first_half_kernel,
        grid=(width // step,),
        in_specs=[
            pl.BlockSpec((slots, step), lambda i: (0, i)),
            pl.BlockSpec((units, step), lambda i: (0, i)),
        ],
        out_specs=pl.BlockSpec((slots, units), lambda i: (0, 0)),
        out_shape=jax.ShapeDtypeStruct((slots, units), jnp.float32),
        compiler_params=pltpu.CompilerParams(vmem_limit_bytes=40 * MIB),
        cost_estimate=pl.CostEstimate(
            flops=2 * slots * units * width,
            bytes_accessed=2 * (slots + units) * width + 4 * slots * units,
            transcendentals=0,
        ),
        name="first_half",
    )(rows, weight)


def score_kernel(
    capacity, rows_hbm, weight_hbm, hidden_hbm, half_hbm, gates_ref, proj_hbm, back_ref,
    rows, weight, hidden, half, proj, total, score, row_sem, weight_sem, proj_sem,
):
    slots, units = hidden.shape
    group = 2 * capacity
    width = rows.shape[1]
    bm, bn = cut(slots, 256), cut(units, 256)
    tall, wide = slots // bm, units // bn
    rest = pl.ds(weight_hbm.shape[1] - width, width)

    def load_rows(i):
        at = pl.ds(i * bm, bm)
        return [
            pltpu.make_async_copy(rows_hbm.at[at], rows.at[at], row_sem.at[0, i]),
            pltpu.make_async_copy(half_hbm.at[at], half.at[at], row_sem.at[1, i]),
            pltpu.make_async_copy(hidden_hbm.at[at], hidden.at[at], row_sem.at[2, i]),
        ]

    def load_weight(j):
        at = pl.ds(j * bn, bn)
        return [pltpu.make_async_copy(weight_hbm.at[at, rest], weight.at[at], weight_sem.at[j])]

    blocks = [(i / tall, 0, i) for i in range(tall)] + [(j / wide, 1, j) for j in range(wide)]
    blocks = sorted(blocks)
    loads = [load_weight(k) if kind else load_rows(k) for _, kind, k in blocks]
    for copies in loads[:3]:
        for copy in copies:
            copy.start()

    row = lax.broadcasted_iota(jnp.int32, (bm, 128), 0) % group
    lane = lax.broadcasted_iota(jnp.int32, (bm, 128), 1)
    stores = []
    have = ([], [])
    for step, (_, kind, k) in enumerate(blocks):
        for copy in loads[step]:
            copy.wait()
        if step + 3 < len(loads):
            for copy in loads[step + 3]:
                copy.start()
        have[kind].append(k)
        tiles = [(i, k) for i in have[0]] if kind else [(k, j) for j in have[1]]
        for i, j in tiles:
            at, to = slice(i * bm, (i + 1) * bm), slice(j * bn, (j + 1) * bn)
            part = half[at, to] + lax.dot_general(
                rows[at, :], weight[to, :], NT, preferred_element_type=jnp.float32
            )
            proj[at, to] = part.astype(proj.dtype)
            saved = hidden[at, to].astype(jnp.float32)
            part = jnp.sum(part * saved, axis=1, keepdims=True)
            total[at, :] = part if j == 0 else total[at, :] + part
            if j == wide - 1:
                block = pl.ds(i * bm, bm)
                store = pltpu.make_async_copy(proj.at[block], proj_hbm.at[block], proj_sem.at[i])
                store.start()
                stores.append(store)
                laid = jnp.where(row == lane, total[at, :], 0.0)
                score[i * bm // group : (i + 1) * bm // group, :] = jnp.sum(
                    laid.reshape(bm // group, group, 128), axis=1
                )
    both = score[...]
    chips = slots // group
    back_ref[pl.ds(0, chips, stride=2), :] = both
    back_ref[pl.ds(1, chips, stride=2), :] = both
    back_ref[...] += gates_ref[...]
    for store in stores:
        store.wait()


def scores(rows, weight, hidden, half, gates, capacity):
    slots, width = rows.shape
    units = weight.shape[0]
    bm, bn = cut(slots, 256), cut(units, 256)
    anywhere = pl.BlockSpec(memory_space=pl.ANY)
    inside = pl.BlockSpec(memory_space=pltpu.VMEM)
    return pl.pallas_call(
        functools.partial(score_kernel, capacity),
        in_specs=[anywhere, anywhere, anywhere, anywhere, inside],
        out_specs=[anywhere, inside],
        out_shape=[
            jax.ShapeDtypeStruct((slots, units), jnp.bfloat16),
            jax.ShapeDtypeStruct((slots // capacity, 128), jnp.float32),
        ],
        scratch_shapes=[
            pltpu.VMEM((slots, width), jnp.bfloat16),
            pltpu.VMEM((units, width), jnp.bfloat16),
            pltpu.VMEM((slots, units), jnp.bfloat16),
            pltpu.VMEM((slots, units), jnp.float32),
            pltpu.VMEM((slots, units), jnp.bfloat16),
            pltpu.VMEM((slots, 1), jnp.float32),
            pltpu.VMEM((slots // (2 * capacity), 128), jnp.float32),
            pltpu.SemaphoreType.DMA((3, slots // bm)),
            pltpu.SemaphoreType.DMA((units // bn,)),
            pltpu.SemaphoreType.DMA((slots // bm,)),
        ],
        compiler_params=pltpu.CompilerParams(vmem_limit_bytes=56 * MIB),
        cost_estimate=pl.CostEstimate(
            flops=2 * slots * units * width,
            bytes_accessed=2 * (slots + units) * width + 8 * slots * units,
            transcendentals=0,
        ),
        name="score_rows",
    )(rows, weight, hidden, half, gates)


def down_kernel(
    capacity, split, back_ref, hidden_ref, proj_ref, first_ref, second_ref, dw_ref, dh_ref, gated
):
    @pl.when(pl.program_id(0) == 0)
    def _():
        slots = hidden_ref.shape[0]
        groups = slots // capacity
        back = back_ref[...]
        slot = lax.broadcasted_iota(jnp.int32, (groups, capacity, 128), 1)
        lane = lax.broadcasted_iota(jnp.int32, (groups, capacity, 128), 2)
        own = jnp.where(lane == slot + 2 * capacity, back[:, None, :], 0.0)
        gate = jnp.sum(own.reshape(slots, 128), axis=1, keepdims=True)
        gated[...] = (gate * hidden_ref[...].astype(jnp.float32)).astype(gated.dtype)
        dh_ref[...] = (gate * proj_ref[...].astype(jnp.float32)).astype(dh_ref.dtype)

    def tile_of(rows_ref):
        dw_ref[...] = lax.dot_general(
            gated[...], rows_ref[...], TN, preferred_element_type=jnp.float32
        ).astype(dw_ref.dtype)

    @pl.when(pl.program_id(0) < split)
    def _():
        tile_of(first_ref)

    @pl.when(pl.program_id(0) >= split)
    def _():
        tile_of(second_ref)


def down_grads(back, hidden, proj, first, second, capacity):
    slots, units = hidden.shape
    width = first.shape[1] + second.shape[1]
    step = cut(first.shape[1], 1280)
    split = first.shape[1] // step
    whole = lambda i: (0, 0)
    return pl.pallas_call(
        functools.partial(down_kernel, capacity, split),
        grid=(width // step,),
        in_specs=[
            pl.BlockSpec(back.shape, whole),
            pl.BlockSpec(hidden.shape, whole),
            pl.BlockSpec(proj.shape, whole),
            pl.BlockSpec((slots, step), lambda i: (0, jnp.minimum(i, split - 1))),
            pl.BlockSpec((slots, step), lambda i: (0, jnp.maximum(i - split, 0))),
        ],
        out_specs=[
            pl.BlockSpec((units, step), lambda i: (0, i)),
            pl.BlockSpec((slots, units), whole),
        ],
        out_shape=[
            jax.ShapeDtypeStruct((units, width), jnp.bfloat16),
            jax.ShapeDtypeStruct((slots, units), jnp.bfloat16),
        ],
        scratch_shapes=[pltpu.VMEM((slots, units), jnp.bfloat16)],
        compiler_params=pltpu.CompilerParams(vmem_limit_bytes=56 * MIB),
        cost_estimate=pl.CostEstimate(
            flops=2 * slots * units * width,
            bytes_accessed=2 * (slots + units) * width + 6 * slots * units,
            transcendentals=0,
        ),
        name="down_grads",
    )(back, hidden, proj, first, second)


def router_kernel(capacity, back_ref, code_ref, prob_ref, normed_ref, terms_ref, grad_ref):
    halves, experts, tokens = code_ref.shape
    parts = []
    for half in range(halves):
        code = code_ref[half]
        prob = prob_ref[half]
        gate_grad = jnp.zeros((experts, tokens), jnp.float32)
        for r in range(capacity):
            at = half * capacity + r
            gate_grad = jnp.where(code == r, back_ref[:, at : at + 1], gate_grad)
        prob_grad = route_scale * gate_grad
        mean = jnp.sum(prob * prob_grad, axis=0, keepdims=True)
        parts.append(prob * (prob_grad - mean))
    grad = jnp.concatenate(parts, axis=1).astype(jnp.bfloat16)
    grad_ref[...] = grad
    terms_ref[...] = lax.dot_general(
        normed_ref[...], grad, NT, preferred_element_type=jnp.float32
    ).astype(terms_ref.dtype)


def router_terms(back, code, prob, normed_t, capacity):
    experts = back.shape[0]
    columns, tokens = normed_t.shape
    return pl.pallas_call(
        functools.partial(router_kernel, capacity),
        out_shape=[
            jax.ShapeDtypeStruct((columns, experts), jnp.bfloat16),
            jax.ShapeDtypeStruct((experts, tokens), jnp.bfloat16),
        ],
        compiler_params=pltpu.CompilerParams(vmem_limit_bytes=32 * MIB),
        cost_estimate=pl.CostEstimate(
            flops=2 * columns * experts * tokens,
            bytes_accessed=2 * columns * (experts + tokens),
            transcendentals=0,
        ),
        name="router_terms",
    )(back, code, prob, normed_t)


def all_to_all(x, axes):
    return lax.all_to_all(x, axes, split_axis=0, concat_axis=0, tiled=True)


def body(out_grad, normed, router, expert_ids, hidden_act, down_weight):
    groups = lax.axis_size(ALL)
    core = lax.axis_index("c")
    tokens, width = out_grad.shape
    experts = router.shape[1]
    hidden = hidden_act[0]
    weight = down_weight[0]
    capacity = hidden.shape[0] // groups
    slots = groups * capacity
    swap = [(0, 1), (1, 0)]

    part = width // 2
    send, code_t, pick = route(expert_ids.T, out_grad, experts, capacity, 0, part)
    first = all_to_all(send.reshape(experts, capacity, part), ALL).reshape(slots, part)
    send = route_rest(pick, out_grad, part, part)
    second = all_to_all(send.reshape(experts, capacity, part), ALL).reshape(slots, part)
    half = first_half(first, weight)

    logits = jnp.dot(normed, router, preferred_element_type=jnp.float32)
    prob = jax.nn.softmax(logits, axis=-1)
    gates = (route_scale * prob).astype(jnp.bfloat16)
    code = code_t.T
    slot = jnp.arange(capacity, dtype=jnp.int32).astype(jnp.float32)
    slot_gate = jnp.sum(
        jnp.where(code[None] == slot[:, None, None], gates[None].astype(jnp.float32), 0.0), axis=1
    ).astype(jnp.bfloat16)
    lanes = ((0, 0), (2 * capacity, 128 - 3 * capacity))
    gate_lanes = jnp.pad(slot_gate.astype(jnp.float32).T, lanes)

    own = jnp.stack([code_t, prob.T])
    other = lax.ppermute(own, "c", swap)
    even = core == 0
    pair = jnp.stack([jnp.where(even, own, other), jnp.where(even, other, own)], axis=1)
    halves = normed.T.reshape(groups // 2, 2, width // groups, tokens)
    keep = lax.dynamic_index_in_dim(halves, core, 1, keepdims=False)
    give = lax.dynamic_index_in_dim(halves, 1 - core, 1, keepdims=False)
    taken = lax.ppermute(give, "c", swap)
    pair_normed = jnp.where(
        even,
        jnp.concatenate([keep, taken], axis=2),
        jnp.concatenate([taken, keep], axis=2),
    ).reshape(width // 2, 2 * tokens)

    proj, score = scores(second, weight, hidden, half, gate_lanes, capacity)
    back = all_to_all(score, ALL)

    terms, logit_grad_t = router_terms(back, pair[0], pair[1], pair_normed, capacity)
    got = all_to_all(terms.reshape(groups // 2, width // groups, experts), CHIPS)
    d_down, d_hidden = down_grads(back, hidden, proj, first, second, capacity)
    logit_grad = lax.dynamic_slice_in_dim(logit_grad_t, core * tokens, tokens, 1).T
    d_normed = lax.dot_general(
        logit_grad, router, NT, preferred_element_type=jnp.float32
    ).astype(jnp.bfloat16)
    d_router = jnp.sum(got.astype(jnp.float32), axis=0)
    return d_down[None], d_hidden[None], d_router, d_normed


def solution(mesh):
    dp, tensor = mesh.devices.shape
    fine = Mesh(mesh.devices.reshape(dp, tensor // 2, 2), ALL)
    in_specs = (
        P(ALL, None),
        P(ALL, None),
        P(),
        P(ALL, None),
        P(ALL, None, None),
        P(ALL, None, None),
    )
    out_specs = (P(ALL, None, None), P(ALL, None, None), P(ALL, None), P(ALL, None))
    return jax.shard_map(body, mesh=fine, in_specs=in_specs, out_specs=out_specs, check_vma=False)
```

time: 254 us -> 207 us (0.81)
  blocking collectives: 155 us -> 0 us
  waiting for transfers between devices: 7.22 us -> 114 us
  local copies, waits for them, and re-layouts: 18.9 us -> 6.6 us
  starting transfers between devices: 24 us -> 32.7 us
  Pallas kernels: 38.3 us -> 45.4 us
  other arithmetic: 7.03 us -> 3.99 us
    all_gather x1 -> x0, blocking collectives: 155 us -> none  [body(): all_gates = lax.all_gather(slot_gate, ALL, axis=0, tiled=False)]
    all_to_all x3 -> x4, waiting for transfers between devices: 7.22 us -> 114 us  [all_to_all(): return lax.all_to_all(x, axes, split_axis=0, concat_axis=0, tiled=True)]
    unnamed x25 -> x13, local copies, waits for them, and re-layouts: 12.6 us -> 4.06 us
    all_to_all x3 -> x4, starting transfers between devices: 22.9 us -> 31.4 us  [all_to_all(): return lax.all_to_all(x, axes, split_axis=0, concat_axis=0, tiled=True)]
    pallas_call x3 -> x5, Pallas kernels: 36.4 us -> 43.5 us  [the longest x1 15.1 us: down_grads(): pl.pallas_call(functools.partial(down_kernel, capacity, split), grid=(wid...]
    transpose x1 -> x0, local copies, waits for them, and re-layouts: 2.61 us -> none  [body(): gated_hidden_t = (gate * hidden.astype(jnp.float32)).astype(jnp.bfloat16).T]
  transfers between devices with their start and end apart: 5 -> 6, of which waited for: 1 -> 3; matrix products, arithmetic and copies ran while one was open for 6% -> 5% of each run, Pallas kernels for 12% -> 19%
where the time goes in v2:
time: 207 us; the launch traced here: 206 us
  waiting for transfers between devices  114 us (55%)
  Pallas kernels  45.4 us (22%)
  starting transfers between devices  32.7 us (16%)
  local copies, waits for them, and re-layouts  6.6 us (3%)
  other arithmetic  3.99 us (2%)
  matrix products  2.23 us (1%)
    all_to_all x4, waiting for transfers between devices, all_to_all(): return lax.all_to_all(x, axes, split_axis=0, concat_axis=0, tiled=True)  114 us
    all_to_all x4, starting transfers between devices, all_to_all(): return lax.all_to_all(x, axes, split_axis=0, concat_axis=0, tiled=True)  31.4 us
    pallas_call x1, Pallas kernels, down_grads(): pl.pallas_call(functools.partial(down_kernel, capacity, split), grid=(wid...  15.1 us
    pallas_call x1, Pallas kernels, scores(): pl.pallas_call(functools.partial(score_kernel, capacity), in_specs=[anywh...  12.3 us
    pallas_call x1, Pallas kernels, first_half(): pl.pallas_call(first_half_kernel, grid=(width // step,), in_specs=[pl.Blo...  7.22 us
    pallas_call x1, Pallas kernels, route(): pl.pallas_call(functools.partial(route_kernel, capacity), grid=(1,), in_s...  4.89 us
  transfers between devices with their start and end apart: 6, of which 3 were waited for; matrix products, arithmetic and copies ran while one was open for 5% of the time, Pallas kernels for 19%

profile of v2, /device:TPU:1, one launch (start us, length us, event | category | flops | bytes accessed | tf_op | source)
XLA Modules:
  0.0 206.0 jit_solution(17153830543785448154)
XLA Ops:
  0.6 0.0 copy-start
  0.6 4.9 %route_rows.1 = (bf16[1024,2560]{1,0:T(8,128)(2,1)}, f32[128,128]{1,0:T(8,128)}, bf16[1024,128]{1,0:T(8,128)(2,1)}) custom-call(s32[6,128]{1,0:T(8,128)} %bitcast.57, bf16[128,5120]{1,0:T(8,128)(2,1)} %grad_ref.3), custom_call_target="tpu_custom_call" | custom-call | flops 671088640 | bytes 5898240 | tf_op jit(solution)/shard_map/route_rows/pallas_call | solution.py:60
  5.5 11.9 %all-to-all-start.1 = ((bf16[128,8,2560]{2,1,0:T(8,128)(2,1)}), bf16[128,8,2560]{2,1,0:T(8,128)(2,1)}, u32[]{:S(2)}, u32[]{:S(2)}) async-start(bf16[128,8,2560]{2,1,0:T(8,128)(2,1)} %bitcast.46), calls=%async_computation.1 | async-start | bytes 10485760 | tf_op jit(solution)/shard_map/all_to_all | solution.py:362
  17.5 4.0 %route_rest.1 = bf16[1024,2560]{1,0:T(8,128)(2,1)} custom-call(bf16[1024,128]{1,0:T(8,128)(2,1)} %get-tuple-element.13.pick_ref, bf16[128,5120]{1,0:T(8,128)(2,1)} %grad_ref.3), custom_call_target="tpu_custom_call" | custom-call | flops 671088640 | bytes 5898240 | tf_op jit(solution)/shard_map/route_rest/pallas_call | solution.py:93
  21.5 60.0 %all-to-all-done.1 = bf16[128,8,2560]{2,1,0:T(8,128)(2,1)} async-done(((bf16[128,8,2560]{2,1,0:T(8,128)(2,1)}), bf16[128,8,2560]{2,1,0:T(8,128)(2,1)}, u32[]{:S(2)}, u32[]{:S(2)}) %all-to-all-start.1) | async-done | bytes 5242912 | tf_op jit(solution)/shard_map/all_to_all | solution.py:362
  81.5 0.0 copy-start.3
  81.5 7.4 %all-to-all-start = ((bf16[128,8,2560]{2,1,0:T(8,128)(2,1)}), bf16[128,8,2560]{2,1,0:T(8,128)(2,1)}, u32[]{:S(2)}, u32[]{:S(2)}) async-start(bf16[128,8,2560]{2,1,0:T(8,128)(2,1)} %bitcast.45), calls=%async_computation | async-start | bytes 10485760 | tf_op jit(solution)/shard_map/all_to_all | solution.py:362
  88.9 0.0 copy-done
  88.9 0.0 copy-done.3
  88.9 0.0 copy-start.5
  89.0 0.6 fusion.9
  89.7 0.1 copy-done.5
  89.8 1.2 collective-permute-start
  91.0 1.4 copy.29
  92.4 2.2 %constant_dynamic-slice_fusion = (bf16[64,1,40,128]{3,2,1,0:T(8,128)(2,1)}, bf16[64,40,128]{2,1,0:T(8,128)(2,1)S(1)}) fusion(bf16[64,2,40,128]{3,2,1,0:T(8,128)(2,1)} %bitcast.47, s32[]{:T(128)S(6)} %select_n.40, s32[]{:T(128)S(6)} %select_n.41), kind=kLoop, calls=%fused_computation.23 | loop fusion | bytes 2621448 | tf_op jit(solution)/shard_map/jit(dynamic_index_in_dim)/dynamic_slice | solution.py:399
  94.7 0.0 collective-permute-start.1
  94.7 0.1 copy.25
  94.8 0.1 copy.24
  94.9 0.1 select_reduce_fusion
  95.1 0.1 copy.26
  95.2 0.7 pad_convert_fusion.gates_ref
  95.9 0.0 collective-permute-done
  96.0 7.2 %first_half.1.half_hbm = f32[1024,768]{1,0:T(8,128)S(1)} custom-call(bf16[1024,2560]{1,0:T(8,128)(2,1)} %bitcast.6.rows_ref.first_ref, bf16[768,5120]{1,0:T(8,128)(2,1)} %bitcast.43), custom_call_target="tpu_custom_call" | custom-call | flops 4026531840 | bytes 12320768 | tf_op jit(solution)/shard_map/first_half/pallas_call | solution.py:134
  103.2 0.0 copy-start.1
  103.2 1.7 copy-done.1
  104.9 48.1 %all-to-all-done = bf16[128,8,2560]{2,1,0:T(8,128)(2,1)} async-done(((bf16[128,8,2560]{2,1,0:T(8,128)(2,1)}), bf16[128,8,2560]{2,1,0:T(8,128)(2,1)}, u32[]{:S(2)}, u32[]{:S(2)}) %all-to-all-start) | async-done | bytes 5242912 | tf_op jit(solution)/shard_map/all_to_all | solution.py:362
  152.9 12.3 %score_rows.1 = (bf16[1024,768]{1,0:T(8,128)(2,1)}, f32[128,128]{1,0:T(8,128)}) custom-call(bf16[1024,2560]{1,0:T(8,128)(2,1)} %bitcast.2.rows_hbm.second_ref, bf16[768,5120]{1,0:T(8,128)(2,1)} %bitcast.44, bf16[1024,768]{1,0:T(8,128)(2,1)} %bitcast.49, f32[1024,768]{1,0:T(8,128)} %copy-done.1, f32[128,128]{1,0:T(8,128)} %pad_convert_fusion.gates_ref), custom_call_target="tpu_custom_call" | custom-call | flops 4026531840 | bytes 15466496 | tf_op jit(solution)/shard_map/score_rows/pallas_call | solution.py:228
  165.2 7.0 %all-to-all-start.2 = ((f32[128,1,128]{2,1,0:T(1,128)}), f32[128,1,128]{2,1,0:T(1,128)S(1)}, u32[]{:S(2)}, u32[]{:S(2)}) async-start(f32[128,1,128]{2,1,0:T(1,128)} %bitcast.56), calls=%async_computation.2 | async-start | bytes 131072 | tf_op jit(solution)/shard_map/all_to_all | solution.py:362
  172.3 0.0 collective-permute-done.1
  172.3 0.0 copy-start.4
  172.3 0.8 copy-done.4
  173.1 2.3 %maximum_select_fusion.normed_ref = bf16[2560,256]{1,0:T(8,128)(2,1)S(1)} fusion(bf16[2560,128]{1,0:T(8,128)(2,1)} %bitcast.51, bf16[2560,128]{1,0:T(8,128)(2,1)} %bitcast.48, pred[]{:T(512)S(6)} %eq.19), kind=kLoop, calls=%fused_computation.1 | loop fusion | flops 5898240 | bytes 2621441 | tf_op jit(solution)/shard_map/jit(_where)/select_n | solution.py:402
  175.4 6.2 %all-to-all-done.2 = f32[128,1,128]{2,1,0:T(1,128)S(1)} async-done(((f32[128,1,128]{2,1,0:T(1,128)}), f32[128,1,128]{2,1,0:T(1,128)S(1)}, u32[]{:S(2)}, u32[]{:S(2)}) %all-to-all-start.2) | async-done | bytes 65568 | tf_op jit(solution)/shard_map/all_to_all | solution.py:362
  181.7 0.0 copy-start.2
  181.7 1.9 router_terms.1
  183.5 0.0 copy-done.2
  183.5 5.0 %all-to-all-start.3 = ((bf16[64,40,128]{2,1,0:T(8,128)(2,1)}), bf16[64,40,128]{2,1,0:T(8,128)(2,1)S(1)}, u32[]{:S(2)}, u32[]{:S(2)}) async-start(bf16[64,40,128]{2,1,0:T(8,128)(2,1)} %bitcast.28), calls=%async_computation.3 | async-start | bytes 1310720 | tf_op jit(solution)/shard_map/all_to_all | solution.py:362
  188.6 1.6 convolution_convert_fusion
  190.2 15.1 %down_grads.1 = (bf16[768,5120]{1,0:T(8,128)(2,1)}, bf16[1024,768]{1,0:T(8,128)(2,1)}) custom-call(f32[128,128]{1,0:T(8,128)} %bitcast.42, bf16[1024,768]{1,0:T(8,128)(2,1)} %bitcast.50, bf16[1024,768]{1,0:T(8,128)(2,1)} %get-tuple-element.17.proj_ref, bf16[1024,2560]{1,0:T(8,128)(2,1)} %bitcast.6.rows_ref.first_ref, ...), custom_call_target="tpu_custom_call" | custom-call | flops 8053063680 | bytes 23068672 | tf_op jit(solution)/shard_map/down_grads/pallas_call | solution.py:293
  205.3 0.0 all-to-all-done.3
  205.3 0.7 convert_reduce_fusion
  (6 shorter events, 0.1 us)
Async XLA Ops:
  0.6 88.3 %copy-start = (bf16[5120,128]{1,0:T(8,128)(2,1)S(1)}, bf16[5120,128]{1,0:T(8,128)(2,1)}, u32[]{:S(2)}) copy-start(bf16[5120,128]{1,0:T(8,128)(2,1)} %param.8) | copy-start | bytes 3932164
  5.5 75.9 %all-to-all-start.1 = ((bf16[128,8,2560]{2,1,0:T(8,128)(2,1)}), bf16[128,8,2560]{2,1,0:T(8,128)(2,1)}, u32[]{:S(2)}, u32[]{:S(2)}) async-start(bf16[128,8,2560]{2,1,0:T(8,128)(2,1)} %bitcast.46), calls=%async_computation.1 | async-start | bytes 10485760 | tf_op jit(solution)/shard_map/all_to_all | solution.py:362
  81.5 7.5 %copy-start.3 = (bf16[128,5120]{1,0:T(8,128)(2,1)S(1)}, bf16[128,5120]{1,0:T(8,128)(2,1)}, u32[]{:S(2)}) copy-start(bf16[128,5120]{1,0:T(8,128)(2,1)} %param.7) | copy-start | bytes 3932164
  81.5 71.5 %all-to-all-start = ((bf16[128,8,2560]{2,1,0:T(8,128)(2,1)}), bf16[128,8,2560]{2,1,0:T(8,128)(2,1)}, u32[]{:S(2)}, u32[]{:S(2)}) async-start(bf16[128,8,2560]{2,1,0:T(8,128)(2,1)} %bitcast.45), calls=%async_computation | async-start | bytes 10485760 | tf_op jit(solution)/shard_map/all_to_all | solution.py:362
  88.9 0.8 copy-start.5
  89.8 6.1 %collective-permute-start = (f32[2,128,128]{2,1,0:T(8,128)S(1)}, f32[2,128,128]{2,1,0:T(8,128)S(1)}, u32[]{:S(2)}, u32[]{:S(2)}) collective-permute-start(f32[2,128,128]{2,1,0:T(8,128)S(1)} %pad_maximum_fusion.1), channel_id=1, source_target_pairs={{0,1},{1,0},{2,3},{3,2},{4,5},{5,4},{6,7},{7,6},{8,9},{9,8},{10,11... | collective-permute-start | bytes 393224 | tf_op jit(solution)/shard_map/ppermute | solution.py:395
  94.7 77.6 %collective-permute-start.1 = (bf16[64,40,128]{2,1,0:T(8,128)(2,1)S(1)}, bf16[64,40,128]{2,1,0:T(8,128)(2,1)S(1)}, u32[]{:S(2)}, u32[]{:S(2)}) collective-permute-start(bf16[64,40,128]{2,1,0:T(8,128)(2,1)S(1)} %get-tuple-element.23), channel_id=1, source_target_pairs={{0,1},{1,0},{2,3},{3,2},{4,5},{5,4},{6,7},{7,6},{8,9},{9,8},{10,11... | collective-permute-start | bytes 1966088 | tf_op jit(solution)/shard_map/ppermute | solution.py:401
  103.2 1.7 copy-start.1
  165.2 16.4 %all-to-all-start.2 = ((f32[128,1,128]{2,1,0:T(1,128)}), f32[128,1,128]{2,1,0:T(1,128)S(1)}, u32[]{:S(2)}, u32[]{:S(2)}) async-start(f32[128,1,128]{2,1,0:T(1,128)} %bitcast.56), calls=%async_computation.2 | async-start | bytes 131072 | tf_op jit(solution)/shard_map/all_to_all | solution.py:362
  172.3 0.8 copy-start.4
  181.7 1.9 copy-start.2
  183.5 21.7 %all-to-all-start.3 = ((bf16[64,40,128]{2,1,0:T(8,128)(2,1)}), bf16[64,40,128]{2,1,0:T(8,128)(2,1)S(1)}, u32[]{:S(2)}, u32[]{:S(2)}) async-start(bf16[64,40,128]{2,1,0:T(8,128)(2,1)} %bitcast.28), calls=%async_computation.3 | async-start | bytes 1310720 | tf_op jit(solution)/shard_map/all_to_all | solution.py:362

commit v3 on v2

v3 whole, which is shorter than its diff:
```python
import functools
import math

import jax
import jax.numpy as jnp
from jax import lax
from jax.experimental import pallas as pl
from jax.experimental.pallas import tpu as pltpu
from jax.sharding import Mesh, PartitionSpec as P

route_scale = 16.0
ALL = ("dp", "z", "c")
CHIPS = ("dp", "z")
MIB = 1 << 20
NT = (((1,), (1,)), ((), ()))


def cut(size, best):
    return best if size % best == 0 else size


def spread_columns(pick_ref, grad_ref, rows_hbm, rows, sem):
    width = rows.shape[1]
    step = cut(width, 256)
    copies = []
    for n in range(0, width, step):
        rows[:, n : n + step] = jnp.dot(
            pick_ref[...], grad_ref[:, n : n + step], preferred_element_type=jnp.float32
        ).astype(rows.dtype)
        columns = (slice(None), pl.ds(n, step))
        copy = pltpu.make_async_copy(rows.at[columns], rows_hbm.at[columns], sem.at[n // step])
        copy.start()
        copies.append(copy)
    for copy in copies:
        copy.wait()


def route_kernel(capacity, ids_ref, grad_ref, rows_hbm, code_ref, pick_ref, rows, sem):
    experts, tokens = code_ref.shape
    expert = lax.broadcasted_iota(jnp.int32, (experts, tokens), 0)
    hit = ids_ref[0:1, :] == expert
    for k in range(1, ids_ref.shape[0]):
        hit = hit | (ids_ref[k : k + 1, :] == expert)
    earlier = lax.broadcasted_iota(jnp.int32, (tokens, tokens), 0)
    later = lax.broadcasted_iota(jnp.int32, (tokens, tokens), 1)
    before = jnp.where(earlier < later, 1.0, 0.0).astype(jnp.bfloat16)
    chosen = jnp.where(hit, 1.0, 0.0).astype(jnp.bfloat16)
    rank = jnp.dot(chosen, before, preferred_element_type=jnp.float32)
    code = jnp.where(hit, rank, -1.0)
    code_ref[...] = code
    slot = lax.broadcasted_iota(jnp.int32, (experts, capacity, tokens), 1).astype(jnp.float32)
    one = jnp.where(code[:, None, :] == slot, 1.0, 0.0)
    pick_ref[...] = one.reshape(experts * capacity, tokens).astype(jnp.bfloat16)
    spread_columns(pick_ref, grad_ref, rows_hbm, rows, sem)


def route(ids_t, out_grad, experts, capacity, first, width):
    tokens = out_grad.shape[0]
    slots = experts * capacity
    return pl.pallas_call(
        functools.partial(route_kernel, capacity),
        grid=(1,),
        in_specs=[
            pl.BlockSpec(ids_t.shape, lambda i: (0, 0)),
            pl.BlockSpec((tokens, width), lambda i: (0, first // width)),
        ],
        out_specs=[
            pl.BlockSpec(memory_space=pl.ANY),
            pl.BlockSpec((experts, tokens), lambda i: (0, 0)),
            pl.BlockSpec((slots, tokens), lambda i: (0, 0)),
        ],
        out_shape=[
            jax.ShapeDtypeStruct((slots, width), out_grad.dtype),
            jax.ShapeDtypeStruct((experts, tokens), jnp.float32),
            jax.ShapeDtypeStruct((slots, tokens), jnp.bfloat16),
        ],
        scratch_shapes=[
            pltpu.VMEM((slots, width), out_grad.dtype),
            pltpu.SemaphoreType.DMA((width // cut(width, 256),)),
        ],
        compiler_params=pltpu.CompilerParams(vmem_limit_bytes=56 * MIB),
        cost_estimate=pl.CostEstimate(
            flops=2 * slots * tokens * width,
            bytes_accessed=2 * (slots + tokens) * width,
            transcendentals=0,
        ),
        name="route_rows",
    )(ids_t, out_grad)


def route_rest(pick, out_grad):
    slots, tokens = pick.shape
    width = out_grad.shape[1]
    return pl.pallas_call(
        spread_columns,
        grid=(1,),
        in_specs=[
            pl.BlockSpec((slots, tokens), lambda i: (0, 0)),
            pl.BlockSpec((tokens, width), lambda i: (0, 0)),
        ],
        out_specs=pl.BlockSpec(memory_space=pl.ANY),
        out_shape=jax.ShapeDtypeStruct((slots, width), out_grad.dtype),
        scratch_shapes=[
            pltpu.VMEM((slots, width), out_grad.dtype),
            pltpu.SemaphoreType.DMA((width // cut(width, 256),)),
        ],
        compiler_params=pltpu.CompilerParams(vmem_limit_bytes=56 * MIB),
        cost_estimate=pl.CostEstimate(
            flops=2 * slots * tokens * width,
            bytes_accessed=2 * (slots + tokens) * width,
            transcendentals=0,
        ),
        name="route_rest",
    )(pick, out_grad)


def project_kernel(start, rows_ref, weight_ref, *refs):
    out_ref, total = refs[-2:]
    part = lax.dot_general(
        rows_ref[...], weight_ref[...], NT, preferred_element_type=jnp.float32
    )

    @pl.when(pl.program_id(0) == 0)
    def _():
        total[...] = part + refs[0][...] if start else part

    @pl.when(pl.program_id(0) > 0)
    def _():
        total[...] += part

    @pl.when(pl.program_id(0) == pl.num_programs(0) - 1)
    def _():
        out_ref[...] = total[...].astype(out_ref.dtype)


def project(rows, weight, first, half, dtype, name):
    slots, width = rows.shape
    units = weight.shape[0]
    step = cut(math.gcd(width, first) if first else width, 1024)
    start = [] if half is None else [half]
    whole = lambda i: (0, 0)
    return pl.pallas_call(
        functools.partial(project_kernel, half is not None),
        grid=(width // step,),
        in_specs=[
            pl.BlockSpec((slots, step), lambda i: (0, i)),
            pl.BlockSpec((units, step), lambda i: (0, i + first // step)),
        ]
        + [pl.BlockSpec((slots, units), whole)] * len(start),
        out_specs=pl.BlockSpec((slots, units), whole),
        out_shape=jax.ShapeDtypeStruct((slots, units), dtype),
        scratch_shapes=[pltpu.VMEM((slots, units), jnp.float32)],
        compiler_params=pltpu.CompilerParams(vmem_limit_bytes=56 * MIB),
        cost_estimate=pl.CostEstimate(
            flops=2 * slots * units * width,
            bytes_accessed=2 * (slots + units) * width + 4 * slots * units,
            transcendentals=0,
        ),
        name=name,
    )(rows, weight, *start)


def score_kernel(
    capacity, rows_hbm, expert_hbm, partial_ref, gates_ref, back_ref, rows, expert, score, sem
):
    slots, width = rows.shape
    group = 2 * capacity
    bm = cut(slots, 128)
    loads = []
    for i in range(slots // bm):
        at = pl.ds(i * bm, bm)
        loads.append(
            [
                pltpu.make_async_copy(rows_hbm.at[at], rows.at[at], sem.at[0, i]),
                pltpu.make_async_copy(expert_hbm.at[at], expert.at[at], sem.at[1, i]),
            ]
        )
    ahead = 8
    for copies in loads[:ahead]:
        for copy in copies:
            copy.start()
    row = lax.broadcasted_iota(jnp.int32, (bm, 128), 0) % group
    lane = lax.broadcasted_iota(jnp.int32, (bm, 128), 1)
    for i, copies in enumerate(loads):
        for copy in copies:
            copy.wait()
        for copy in loads[i + ahead] if i + ahead < len(loads) else []:
            copy.start()
        at = slice(i * bm, (i + 1) * bm)
        total = partial_ref[at, :]
        for k in range(0, width, 128):
            total = total + rows[at, k : k + 128].astype(jnp.float32) * expert[
                at, k : k + 128
            ].astype(jnp.float32)
        total = jnp.sum(total, axis=1, keepdims=True)
        for core in range(2):
            laid = jnp.where((row + core * capacity) % group == lane, total, 0.0)
            score[core, i * bm // group : (i + 1) * bm // group, :] = jnp.sum(
                laid.reshape(bm // group, group, 128), axis=1
            )
    chips = slots // group
    back_ref[pl.ds(0, chips, stride=2), :] = score[0]
    back_ref[pl.ds(1, chips, stride=2), :] = score[1]
    back_ref[...] += gates_ref[...]


def partial_kernel(rows_ref, expert_ref, partial_ref):
    total = jnp.zeros(partial_ref.shape, jnp.float32)
    for k in range(0, rows_ref.shape[1], 128):
        total = total + rows_ref[:, k : k + 128].astype(jnp.float32) * expert_ref[
            :, k : k + 128
        ].astype(jnp.float32)
    partial_ref[...] = total


def partial_scores(rows, expert):
    slots, width = rows.shape
    bm = cut(slots, 128)
    return pl.pallas_call(
        partial_kernel,
        grid=(slots // bm,),
        in_specs=[pl.BlockSpec((bm, width), lambda i: (i, 0))] * 2,
        out_specs=pl.BlockSpec((bm, 128), lambda i: (i, 0)),
        out_shape=jax.ShapeDtypeStruct((slots, 128), jnp.float32),
        compiler_params=pltpu.CompilerParams(vmem_limit_bytes=24 * MIB),
        cost_estimate=pl.CostEstimate(
            flops=2 * slots * width, bytes_accessed=4 * slots * width, transcendentals=0
        ),
        name="partial_scores",
    )(rows, expert)


def scores(rows, expert, partial, gates, capacity):
    slots, width = rows.shape
    bm = cut(slots, 128)
    anywhere = pl.BlockSpec(memory_space=pl.ANY)
    inside = pl.BlockSpec(memory_space=pltpu.VMEM)
    return pl.pallas_call(
        functools.partial(score_kernel, capacity),
        in_specs=[anywhere, anywhere, inside, inside],
        out_specs=inside,
        out_shape=jax.ShapeDtypeStruct((slots // capacity, 128), jnp.float32),
        scratch_shapes=[
            pltpu.VMEM((slots, width), jnp.bfloat16),
            pltpu.VMEM((slots, width), jnp.bfloat16),
            pltpu.VMEM((2, slots // (2 * capacity), 128), jnp.float32),
            pltpu.SemaphoreType.DMA((2, slots // bm)),
        ],
        compiler_params=pltpu.CompilerParams(vmem_limit_bytes=56 * MIB),
        cost_estimate=pl.CostEstimate(
            flops=2 * slots * width, bytes_accessed=4 * slots * width, transcendentals=0
        ),
        name="score_rows",
    )(rows, expert, partial, gates)


def tiles(split, width):
    at = []
    n = 0
    while n < width:
        step = 512 if n == 0 or width - n <= 1024 else 1024
        step = min(step, (split if n < split else width) - n)
        at.append((n, step))
        n += step
    return at


def down_kernel(
    capacity, back_ref, grad_ref, hidden_hbm, proj_hbm, router_hbm, first_hbm, second_hbm,
    dw_hbm, dh_hbm, dn_hbm,
    hidden, proj, router, rows, gated, dw, dh, dn, in_sem, row_sem, dw_sem, out_sem,
):
    units, slots = hidden.shape
    split, width = first_hbm.shape[1], rows.shape[1]
    at = tiles(split, width)
    load_hidden = pltpu.make_async_copy(hidden_hbm, hidden, in_sem.at[0])
    load_proj = pltpu.make_async_copy(proj_hbm, proj, in_sem.at[1])
    load_router = pltpu.make_async_copy(router_hbm, router, in_sem.at[2])
    store_dh = pltpu.make_async_copy(dh, dh_hbm, out_sem.at[0])
    store_dn = pltpu.make_async_copy(dn, dn_hbm, out_sem.at[1])
    loads, stores = [], []
    for i, (n, step) in enumerate(at):
        columns = (slice(None), pl.ds(n, step))
        if n < split:
            source = first_hbm.at[columns]
        else:
            source = second_hbm.at[:, pl.ds(n - split, step)]
        loads.append(pltpu.make_async_copy(source, rows.at[columns], row_sem.at[i]))
        stores.append(pltpu.make_async_copy(dw.at[columns], dw_hbm.at[columns], dw_sem.at[i]))
    load_hidden.start()
    loads[0].start()

    groups = slots // capacity
    slot = lax.broadcasted_iota(jnp.int32, (groups, capacity, 128), 1)
    lane = lax.broadcasted_iota(jnp.int32, (groups, capacity, 128), 2)
    own = jnp.where(lane == slot + 2 * capacity, back_ref[...][:, None, :], 0.0)
    gate = jnp.sum(own.reshape(slots, 128), axis=1, keepdims=True)
    gate_row = jnp.broadcast_to(gate, (slots, 128)).T[0:1, :]
    load_hidden.wait()
    loads[1].start()
    gated[...] = (gate_row * hidden[...].astype(jnp.float32)).astype(gated.dtype)
    for i, (n, step) in enumerate(at):
        columns = slice(n, n + step)
        loads[i].wait()
        if i + 2 < len(loads):
            loads[i + 2].start()
        if i == 0:
            load_proj.start()
            load_router.start()
        dw[:, columns] = jnp.dot(
            gated[...], rows[:, columns], preferred_element_type=jnp.float32
        ).astype(dw.dtype)
        stores[i].start()
        if i == 1:
            load_proj.wait()
            dh[...] = (gate * proj[...].astype(jnp.float32)).astype(dh.dtype)
            store_dh.start()
            load_router.wait()
            grad = grad_ref[...].astype(jnp.float32).T.astype(jnp.bfloat16)
            dn[...] = lax.dot_general(
                grad, router[...], NT, preferred_element_type=jnp.float32
            ).astype(dn.dtype)
            store_dn.start()
    for store in stores:
        store.wait()
    store_dh.wait()
    store_dn.wait()


def down_grads(back, grad, hidden, proj, router, first, second, capacity):
    units, slots = hidden.shape
    split = first.shape[1]
    width = split + second.shape[1]
    experts, tokens = grad.shape
    count = len(tiles(split, width))
    anywhere = pl.BlockSpec(memory_space=pl.ANY)
    inside = pl.BlockSpec(memory_space=pltpu.VMEM)
    return pl.pallas_call(
        functools.partial(down_kernel, capacity),
        in_specs=[inside] * 2 + [anywhere] * 5,
        out_specs=[anywhere] * 3,
        out_shape=[
            jax.ShapeDtypeStruct((units, width), jnp.bfloat16),
            jax.ShapeDtypeStruct((slots, units), jnp.bfloat16),
            jax.ShapeDtypeStruct((tokens, width), jnp.bfloat16),
        ],
        scratch_shapes=[
            pltpu.VMEM((units, slots), jnp.bfloat16),
            pltpu.VMEM((slots, units), jnp.bfloat16),
            pltpu.VMEM((width, experts), jnp.bfloat16),
            pltpu.VMEM((slots, width), jnp.bfloat16),
            pltpu.VMEM((units, slots), jnp.bfloat16),
            pltpu.VMEM((units, width), jnp.bfloat16),
            pltpu.VMEM((slots, units), jnp.bfloat16),
            pltpu.VMEM((tokens, width), jnp.bfloat16),
            pltpu.SemaphoreType.DMA((3,)),
            pltpu.SemaphoreType.DMA((count,)),
            pltpu.SemaphoreType.DMA((count,)),
            pltpu.SemaphoreType.DMA((2,)),
        ],
        compiler_params=pltpu.CompilerParams(vmem_limit_bytes=56 * MIB),
        cost_estimate=pl.CostEstimate(
            flops=2 * slots * units * width + 2 * tokens * experts * width,
            bytes_accessed=2 * (slots + units + 2 * tokens) * width + 6 * slots * units,
            transcendentals=0,
        ),
        name="down_grads",
    )(back, grad, hidden, proj, router, first, second)


def router_kernel(
    capacity, back_ref, code_ref, prob_ref, other_code_ref, other_prob_ref, keep_ref, taken_ref,
    terms_ref, grad_ref,
):
    terms = None
    sides = ((code_ref, prob_ref, keep_ref), (other_code_ref, other_prob_ref, taken_ref))
    for side, (code, prob, normed) in enumerate(sides):
        code = code[...]
        prob = prob[...]
        gate_grad = jnp.zeros(code.shape, jnp.float32)
        for r in range(capacity):
            at = side * capacity + r
            gate_grad = jnp.where(code == r, back_ref[:, at : at + 1], gate_grad)
        prob_grad = route_scale * gate_grad
        mean = jnp.sum(prob * prob_grad, axis=0, keepdims=True)
        grad = (prob * (prob_grad - mean)).astype(jnp.bfloat16)
        if side == 0:
            grad_ref[...] = grad
        part = lax.dot_general(normed[...], grad, NT, preferred_element_type=jnp.float32)
        terms = part if side == 0 else terms + part
    terms_ref[...] = terms.astype(terms_ref.dtype)


def router_terms(back, own, other, keep, taken, capacity):
    experts = back.shape[0]
    columns, tokens = keep.shape
    return pl.pallas_call(
        functools.partial(router_kernel, capacity),
        out_shape=[
            jax.ShapeDtypeStruct((columns, experts), jnp.bfloat16),
            jax.ShapeDtypeStruct((experts, tokens), jnp.bfloat16),
        ],
        compiler_params=pltpu.CompilerParams(vmem_limit_bytes=32 * MIB),
        cost_estimate=pl.CostEstimate(
            flops=4 * columns * experts * tokens,
            bytes_accessed=4 * columns * (experts + tokens),
            transcendentals=0,
        ),
        name="router_terms",
    )(back, own[0], own[1], other[0], other[1], keep, taken)


def all_to_all(x, axes):
    return lax.all_to_all(x, axes, split_axis=0, concat_axis=0, tiled=True)


def body(out_grad, normed, router, expert_ids, hidden_act, down_weight):
    groups = lax.axis_size(ALL)
    core = lax.axis_index("c")
    tokens, width = out_grad.shape
    experts = router.shape[1]
    hidden = hidden_act[0]
    weight = down_weight[0]
    capacity = hidden.shape[0] // groups
    slots = groups * capacity
    swap = [(0, 1), (1, 0)]

    part = width * 3 // 5
    rest = width - part
    send, code_t, pick = route(expert_ids.T, out_grad, experts, capacity, 0, part)
    first = all_to_all(send.reshape(experts, capacity, part), ALL).reshape(slots, part)
    send = route_rest(pick, out_grad[:, part:])
    expert_out = [
        jnp.dot(hidden, w, preferred_element_type=jnp.float32).astype(jnp.bfloat16)
        for w in (weight[:, :part], weight[:, part:])
    ]
    send, expert_out, hidden_t = lax.optimization_barrier((send, expert_out, hidden.T))
    second = all_to_all(send.reshape(experts, capacity, rest), ALL).reshape(slots, rest)

    logits = jnp.dot(normed, router, preferred_element_type=jnp.float32)
    prob = jax.nn.softmax(logits, axis=-1)
    gates = (route_scale * prob).astype(jnp.bfloat16)
    code = code_t.T
    slot = jnp.arange(capacity, dtype=jnp.int32).astype(jnp.float32)
    slot_gate = jnp.sum(
        jnp.where(code[None] == slot[:, None, None], gates[None].astype(jnp.float32), 0.0), axis=1
    ).astype(jnp.bfloat16)
    lanes = ((0, 0), (2 * capacity, 128 - 3 * capacity))
    gate_lanes = jnp.pad(slot_gate.astype(jnp.float32).T, lanes)

    own = (code_t, prob.T)
    other = [lax.ppermute(x, "c", swap) for x in own]
    halves = normed.T.reshape(groups // 2, 2, width // groups, tokens)
    keep = lax.dynamic_index_in_dim(halves, core, 1, keepdims=False)
    give = lax.dynamic_index_in_dim(halves, 1 - core, 1, keepdims=False)
    taken = lax.ppermute(give, "c", swap).reshape(width // 2, tokens)
    keep = keep.reshape(width // 2, tokens)

    partial = partial_scores(first, expert_out[0])
    half = project(first, weight, 0, None, jnp.float32, "project_first")
    partial, half = lax.optimization_barrier((partial, half))

    score = scores(second, expert_out[1], partial, gate_lanes, capacity)
    back = all_to_all(score, ALL)
    proj = project(second, weight, part, half, jnp.bfloat16, "project_second")

    terms, logit_grad_t = router_terms(back, own, other, keep, taken, capacity)
    got = all_to_all(terms.reshape(groups // 2, width // groups, experts), CHIPS)
    d_down, d_hidden, d_normed = down_grads(
        back, logit_grad_t, hidden_t, proj, router, first, second, capacity
    )
    d_router = jnp.sum(got.astype(jnp.float32), axis=0)
    return d_down[None], d_hidden[None], d_router, d_normed


def solution(mesh):
    dp, tensor = mesh.devices.shape
    fine = Mesh(mesh.devices.reshape(dp, tensor // 2, 2), ALL)
    in_specs = (
        P(ALL, None),
        P(ALL, None),
        P(),
        P(ALL, None),
        P(ALL, None, None),
        P(ALL, None, None),
    )
    out_specs = (P(ALL, None, None), P(ALL, None, None), P(ALL, None), P(ALL, None))
    return jax.shard_map(body, mesh=fine, in_specs=in_specs, out_specs=out_specs, check_vma=False)
```

time: 207 us -> 203 us (0.981)
  waiting for transfers between devices: 114 us -> 80.1 us
  matrix products: 2.23 us -> 15.9 us
  Pallas kernels: 45.4 us -> 55.3 us
  starting transfers between devices: 32.7 us -> 37.2 us
  local copies, waits for them, and re-layouts: 6.6 us -> 10.9 us
  other arithmetic: 3.99 us -> 1.66 us
    all_to_all x4, waiting for transfers between devices: 114 us -> 80.1 us  [all_to_all(): return lax.all_to_all(x, axes, split_axis=0, concat_axis=0, tiled=True)]
    pallas_call x2 -> x4, Pallas kernels: 22.3 us -> 38.7 us  [the longest x2 18.8 us: project(): pl.pallas_call(functools.partial(project_kernel, half is not None), grid=...]
    dot_general x1 -> x2, matrix products: 1.59 us -> 14 us  [body(): jnp.dot(hidden, w, preferred_element_type=jnp.float32).astype(jnp.bfloat16)]
    pallas_call x1, Pallas kernels: 12.3 us -> 5.41 us  [scores(): pl.pallas_call(functools.partial(score_kernel, capacity), in_specs=[anywh...]
    all_to_all x4, starting transfers between devices: 31.4 us -> 35.4 us  [all_to_all(): return lax.all_to_all(x, axes, split_axis=0, concat_axis=0, tiled=True)]
    unnamed x13 -> x20, local copies, waits for them, and re-layouts: 4.06 us -> 7.3 us
    select_n x1 -> x0, other arithmetic: 2.28 us -> none  [body(): jnp.where(even, jnp.concatenate([keep, taken], axis=2), jnp.concatenate([...]
    dynamic_slice x1 -> x0, local copies, waits for them, and re-layouts: 2.25 us -> none  [body(): keep = lax.dynamic_index_in_dim(halves, core, 1, keepdims=False)]
  transfers between devices with their start and end apart: 6 -> 7, of which waited for: 3 -> 3; matrix products, arithmetic and copies ran while one was open for 5% -> 12% of each run, Pallas kernels for 19% -> 24%
where the time goes in v3:
time: 203 us; the launch traced here: 202 us
  waiting for transfers between devices  80.1 us (39%)
  Pallas kernels  55.3 us (27%)
  starting transfers between devices  37.2 us (18%)
  matrix products  15.9 us (8%)
  local copies, waits for them, and re-layouts  10.9 us (5%)
    all_to_all x4, waiting for transfers between devices, all_to_all(): return lax.all_to_all(x, axes, split_axis=0, concat_axis=0, tiled=True)  80.1 us
    all_to_all x4, starting transfers between devices, all_to_all(): return lax.all_to_all(x, axes, split_axis=0, concat_axis=0, tiled=True)  35.4 us
    pallas_call x2, Pallas kernels, project(): pl.pallas_call(functools.partial(project_kernel, half is not None), grid=...  18.8 us
    pallas_call x1, Pallas kernels, down_grads(): pl.pallas_call(functools.partial(down_kernel, capacity), in_specs=[inside...  14.1 us
    dot_general x2, matrix products, body(): jnp.dot(hidden, w, preferred_element_type=jnp.float32).astype(jnp.bfloat16)  14 us
    unnamed x20, local copies, waits for them, and re-layouts  7.3 us
    pallas_call x1, Pallas kernels, partial_scores(): pl.pallas_call(partial_kernel, grid=(slots // bm,), in_specs=[pl.BlockSpe...  5.8 us
    pallas_call x1, Pallas kernels, scores(): pl.pallas_call(functools.partial(score_kernel, capacity), in_specs=[anywh...  5.41 us
  transfers between devices with their start and end apart: 7, of which 3 were waited for; matrix products, arithmetic and copies ran while one was open for 12% of the time, Pallas kernels for 24%

profile of v3, /device:TPU:1, one launch (start us, length us, event | category | flops | bytes accessed | tf_op | source)
XLA Modules:
  0.0 202.0 jit_solution(10195506938079677057)
XLA Ops:
  0.6 5.4 %route_rows.1 = (bf16[1024,3072]{1,0:T(8,128)(2,1)}, f32[128,128]{1,0:T(8,128)}, bf16[1024,128]{1,0:T(8,128)(2,1)}) custom-call(s32[6,128]{1,0:T(8,128)} %bitcast.52, bf16[128,5120]{1,0:T(8,128)(2,1)} %grad_ref.1), custom_call_target="tpu_custom_call" | custom-call | flops 805306368 | bytes 7077888 | tf_op jit(solution)/shard_map/route_rows/pallas_call | solution.py:60
  6.0 0.0 copy-start.6
  6.0 11.9 %all-to-all-start.1 = ((bf16[128,8,3072]{2,1,0:T(8,128)(2,1)}), bf16[128,8,3072]{2,1,0:T(8,128)(2,1)}, u32[]{:S(2)}, u32[]{:S(2)}) async-start(bf16[128,8,3072]{2,1,0:T(8,128)(2,1)} %bitcast.47), calls=%async_computation.1 | async-start | bytes 12582912 | tf_op jit(solution)/shard_map/all_to_all | solution.py:414
  17.9 1.9 slice.9.grad_ref
  19.8 0.0 copy-done.6
  19.8 1.7 copy.24
  21.5 3.9 %route_rest.1 = bf16[1024,2048]{1,0:T(8,128)(2,1)} custom-call(bf16[1024,128]{1,0:T(8,128)(2,1)} %get-tuple-element.18.pick_ref, bf16[128,2048]{1,0:T(8,128)(2,1)} %slice.9.grad_ref), custom_call_target="tpu_custom_call" | custom-call | flops 536870912 | bytes 4718592 | tf_op jit(solution)/shard_map/route_rest/pallas_call | solution.py:94
  25.4 0.0 slice-start.1
  25.4 7.0 %convolution_convert_fusion.1.expert_hbm = bf16[1024,2048]{1,0:T(8,128)(2,1)} fusion(bf16[768,5120]{1,0:T(8,128)(2,1)} %bitcast.41, bf16[1,1024,768]{2,1,0:T(8,128)(2,1)S(1)} %copy-done.6), kind=kOutput, calls=%fused_computation.2 | convolution fusion | flops 3223322624 | bytes 8912896 | tf_op jit(solution)/shard_map/dot_general | solution.py:434
  32.4 0.0 slice-done
  32.4 0.0 slice-done.1
  32.4 7.0 %convolution_convert_fusion.expert_ref = bf16[1024,3072]{1,0:T(8,128)(2,1)} fusion(bf16[768,5120]{1,0:T(8,128)(2,1)S(1)} %bitcast.46, bf16[1,1024,768]{2,1,0:T(8,128)(2,1)S(1)} %copy-done.6), kind=kOutput, calls=%fused_computation | convolution fusion | flops 4834983936 | bytes 12582912 | tf_op jit(solution)/shard_map/dot_general | solution.py:434
  39.4 54.1 %all-to-all-done.1 = bf16[128,8,3072]{2,1,0:T(8,128)(2,1)} async-done(((bf16[128,8,3072]{2,1,0:T(8,128)(2,1)}), bf16[128,8,3072]{2,1,0:T(8,128)(2,1)}, u32[]{:S(2)}, u32[]{:S(2)}) %all-to-all-start.1) | async-done | bytes 6291488 | tf_op jit(solution)/shard_map/all_to_all | solution.py:414
  93.5 8.6 %all-to-all-start = ((bf16[128,8,2048]{2,1,0:T(8,128)(2,1)}), bf16[128,8,2048]{2,1,0:T(8,128)(2,1)}, u32[]{:S(2)}, u32[]{:S(2)}) async-start(bf16[128,8,2048]{2,1,0:T(8,128)(2,1)} %bitcast.40), calls=%async_computation | async-start | bytes 8388608 | tf_op jit(solution)/shard_map/all_to_all | solution.py:414
  102.1 0.0 copy-done.5
  102.2 1.4 copy.29
  103.6 1.4 dynamic-slice_bitcast_fusion
  105.0 0.0 copy-start.2
  105.0 1.2 collective-permute-start.2
  106.2 1.9 fusion.8
  108.3 0.1 collective-permute-start.1
  108.4 0.0 copy-done.2
  108.4 0.5 collective-permute-start
  108.9 0.1 copy.26
  109.0 0.1 copy.25
  109.1 0.1 select_reduce_fusion
  109.2 0.1 copy.27
  109.3 0.7 pad_convert_fusion.gates_ref
  110.1 2.8 %copy-done = bf16[1024,3072]{1,0:T(8,128)(2,1)S(1)} copy-done((bf16[1024,3072]{1,0:T(8,128)(2,1)S(1)}, bf16[1024,3072]{1,0:T(8,128)(2,1)}, u32[]{:S(2)}) %copy-start) | copy-done | bytes 6291480
  112.8 5.8 %partial_scores.1.partial_ref = f32[1024,128]{1,0:T(8,128)S(1)} custom-call(bf16[1024,3072]{1,0:T(8,128)(2,1)} %bitcast.7.rows_ref.first_hbm, bf16[1024,3072]{1,0:T(8,128)(2,1)S(1)} %copy-done), custom_call_target="tpu_custom_call" | custom-call | flops 6291456 | bytes 12582912 | tf_op jit(solution)/shard_map/partial_scores/pallas_call | solution.py:219
  118.7 0.0 copy-start.1
  118.7 0.8 copy-done.1
  119.5 10.2 %project_first.1.refs_0_ = f32[1024,768]{1,0:T(8,128)} custom-call(bf16[1024,3072]{1,0:T(8,128)(2,1)} %bitcast.7.rows_ref.first_hbm, bf16[768,5120]{1,0:T(8,128)(2,1)} %bitcast.42), custom_call_target="tpu_custom_call" | custom-call | flops 4831838208 | bytes 14155776 | tf_op jit(solution)/shard_map/project_first/pallas_call | solution.py:142
  129.7 25.3 %all-to-all-done = bf16[128,8,2048]{2,1,0:T(8,128)(2,1)} async-done(((bf16[128,8,2048]{2,1,0:T(8,128)(2,1)}), bf16[128,8,2048]{2,1,0:T(8,128)(2,1)}, u32[]{:S(2)}, u32[]{:S(2)}) %all-to-all-start) | async-done | bytes 4194336 | tf_op jit(solution)/shard_map/all_to_all | solution.py:414
  154.9 5.4 %score_rows.1 = f32[128,128]{1,0:T(8,128)} custom-call(bf16[1024,2048]{1,0:T(8,128)(2,1)} %bitcast.5.rows_hbm.rows_ref.second_hbm, bf16[1024,2048]{1,0:T(8,128)(2,1)} %convolution_convert_fusion.1.expert_hbm, f32[1024,128]{1,0:T(8,128)} %copy-done.1, f32[128,128]{1,0:T(8,128)} %pad_convert_fusion.gates_ref), custom_call_target="tpu_custom_call" | custom-call | flops 4194304 | bytes 8388608 | tf_op jit(solution)/shard_map/score_rows/pallas_call | solution.py:238
  160.3 4.8 %all-to-all-start.2 = ((f32[128,1,128]{2,1,0:T(1,128)}), f32[128,1,128]{2,1,0:T(1,128)S(1)}, u32[]{:S(2)}, u32[]{:S(2)}) async-start(f32[128,1,128]{2,1,0:T(1,128)} %bitcast.50), calls=%async_computation.2 | async-start | bytes 131072 | tf_op jit(solution)/shard_map/all_to_all | solution.py:414
  165.2 8.6 %project_second.1.proj_hbm = bf16[1024,768]{1,0:T(8,128)(2,1)} custom-call(bf16[1024,2048]{1,0:T(8,128)(2,1)} %bitcast.5.rows_hbm.rows_ref.second_hbm, bf16[768,5120]{1,0:T(8,128)(2,1)} %bitcast.43, f32[1024,768]{1,0:T(8,128)} %project_first.1.refs_0_), custom_call_target="tpu_custom_call" | custom-call | flops 3221225472 | bytes 10485760 | tf_op jit(solution)/shard_map/project_second/pallas_call | solution.py:142
  173.8 0.0 collective-permute-done.1.other_prob_ref
  173.8 0.0 collective-permute-done.other_code_ref
  173.8 0.0 collective-permute-done.2
  173.8 0.7 all-to-all-done.2
  174.5 1.9 router_terms.1
  176.5 0.6 copy-done.4
  177.1 10.1 %all-to-all-start.3 = ((bf16[64,40,128]{2,1,0:T(8,128)(2,1)}), bf16[64,40,128]{2,1,0:T(8,128)(2,1)S(1)}, u32[]{:S(2)}, u32[]{:S(2)}) async-start(bf16[64,40,128]{2,1,0:T(8,128)(2,1)} %bitcast.22), calls=%async_computation.3 | async-start | bytes 1310720 | tf_op jit(solution)/shard_map/all_to_all | solution.py:414
  187.1 0.0 copy-done.3
  187.2 14.1 %down_grads.1 = (bf16[768,5120]{1,0:T(8,128)(2,1)}, bf16[1024,768]{1,0:T(8,128)(2,1)}, bf16[128,5120]{1,0:T(8,128)(2,1)}) custom-call(f32[128,128]{1,0:T(8,128)} %bitcast.39, bf16[128,128]{1,0:T(8,128)(2,1)} %copy-done.4, bf16[768,1024]{1,0:T(8,128)(2,1)} %bitcast.49, bf16[1024,768]{1,0:T(8,128)(2,1)} %project_second.1.proj_hbm, ...), custom_call_target="tpu_custom_call" | custom-call | flops 8220835840 | bytes 25690112 | tf_op jit(solution)/shard_map/down_grads/pallas_call | solution.py:338
  201.2 0.0 all-to-all-done.3
  201.3 0.7 convert_reduce_fusion
  (9 shorter events, 0.1 us)
Async XLA Ops:
  6.0 13.8 %copy-start.6 = (bf16[1,1024,768]{2,1,0:T(8,128)(2,1)S(1)}, bf16[1,1024,768]{2,1,0:T(8,128)(2,1)}, u32[]{:S(2)}) copy-start(bf16[1,1024,768]{2,1,0:T(8,128)(2,1)} %param.10) | copy-start | bytes 4718596
  6.0 87.5 %all-to-all-start.1 = ((bf16[128,8,3072]{2,1,0:T(8,128)(2,1)}), bf16[128,8,3072]{2,1,0:T(8,128)(2,1)}, u32[]{:S(2)}, u32[]{:S(2)}) async-start(bf16[128,8,3072]{2,1,0:T(8,128)(2,1)} %bitcast.47), calls=%async_computation.1 | async-start | bytes 12582912 | tf_op jit(solution)/shard_map/all_to_all | solution.py:414
  21.5 10.9 %slice-start = ((s8[7864320]{0:T(1024)(128)(4,1)}), s8[3670016]{0:T(1024)(128)(4,1)S(1)}, s32[]{:S(2)}) async-start(s8[7864320]{0:T(1024)(128)(4,1)} %bitcast.44), calls=%async_computation.4 | async-start | bytes 7340032
  25.4 7.0 %slice-start.1 = ((s8[7864320]{0:T(1024)(128)(4,1)}), s8[4194304]{0:T(1024)(128)(4,1)S(1)}, s32[]{:S(2)}) async-start(s8[7864320]{0:T(1024)(128)(4,1)} %bitcast.44), calls=%async_computation.5 | async-start | bytes 8388608
  93.5 8.7 %copy-start.5 = (bf16[128,5120]{1,0:T(8,128)(2,1)S(1)}, bf16[128,5120]{1,0:T(8,128)(2,1)}, u32[]{:S(2)}) copy-start(bf16[128,5120]{1,0:T(8,128)(2,1)} %param.7) | copy-start | bytes 3932164
  93.5 61.4 %all-to-all-start = ((bf16[128,8,2048]{2,1,0:T(8,128)(2,1)}), bf16[128,8,2048]{2,1,0:T(8,128)(2,1)}, u32[]{:S(2)}, u32[]{:S(2)}) async-start(bf16[128,8,2048]{2,1,0:T(8,128)(2,1)} %bitcast.40), calls=%async_computation | async-start | bytes 8388608 | tf_op jit(solution)/shard_map/all_to_all | solution.py:414
  105.0 3.4 %copy-start.2 = (f32[128,128]{1,0:T(8,128)S(1)}, f32[128,128]{1,0:T(8,128)}, u32[]{:S(2)}) copy-start(f32[128,128]{1,0:T(8,128)} %get-tuple-element.24.code_ref) | copy-start | bytes 196612
  105.0 68.8 %collective-permute-start.2 = (bf16[64,40,128]{2,1,0:T(8,128)(2,1)S(1)}, bf16[64,40,128]{2,1,0:T(8,128)(2,1)S(1)}, u32[]{:S(2)}, u32[]{:S(2)}) collective-permute-start(bf16[64,40,128]{2,1,0:T(8,128)(2,1)S(1)} %get-tuple-element.32), channel_id=1, source_target_pairs={{0,1},{1,0},{2,3},{3,2},{4,5},{5,4},{6,7},{7,6},{8,9},{9,8},{10,11... | collective-permute-start | bytes 1966088 | tf_op jit(solution)/shard_map/ppermute | solution.py:456
  108.3 65.5 %collective-permute-start.1 = (f32[128,128]{1,0:T(8,128)S(1)}, f32[128,128]{1,0:T(8,128)S(1)}, u32[]{:S(2)}, u32[]{:S(2)}) collective-permute-start(f32[128,128]{1,0:T(8,128)S(1)} %get-tuple-element.34.prob_ref), channel_id=1, source_target_pairs={{0,1},{1,0},{2,3},{3,2},{4,5},{5,4},{6,7},{7,6},{8,9},{9,8},{10,11... | collective-permute-start | bytes 196616 | tf_op jit(solution)/shard_map/ppermute | solution.py:452
  108.4 65.4 %collective-permute-start = (f32[128,128]{1,0:T(8,128)S(1)}, f32[128,128]{1,0:T(8,128)S(1)}, u32[]{:S(2)}, u32[]{:S(2)}) collective-permute-start(f32[128,128]{1,0:T(8,128)S(1)} %copy-done.2), channel_id=1, source_target_pairs={{0,1},{1,0},{2,3},{3,2},{4,5},{5,4},{6,7},{7,6},{8,9},{9,8},{10,11... | collective-permute-start | bytes 196616 | tf_op jit(solution)/shard_map/ppermute | solution.py:452
  110.1 2.8 %copy-start = (bf16[1024,3072]{1,0:T(8,128)(2,1)S(1)}, bf16[1024,3072]{1,0:T(8,128)(2,1)}, u32[]{:S(2)}) copy-start(bf16[1024,3072]{1,0:T(8,128)(2,1)} %convolution_convert_fusion.expert_ref) | copy-start | bytes 18874372
  118.7 0.8 copy-start.1
  160.3 14.2 %all-to-all-start.2 = ((f32[128,1,128]{2,1,0:T(1,128)}), f32[128,1,128]{2,1,0:T(1,128)S(1)}, u32[]{:S(2)}, u32[]{:S(2)}) async-start(f32[128,1,128]{2,1,0:T(1,128)} %bitcast.50), calls=%async_computation.2 | async-start | bytes 131072 | tf_op jit(solution)/shard_map/all_to_all | solution.py:414
  174.5 12.6 %copy-start.3 = (f32[128,1,128]{2,1,0:T(1,128)}, f32[128,1,128]{2,1,0:T(1,128)S(1)}, u32[]{:S(2)}) copy-start(f32[128,1,128]{2,1,0:T(1,128)S(1)} %all-to-all-done.2) | copy-start | bytes 196612
  176.5 0.6 copy-start.4
  177.1 24.2 %all-to-all-start.3 = ((bf16[64,40,128]{2,1,0:T(8,128)(2,1)}), bf16[64,40,128]{2,1,0:T(8,128)(2,1)S(1)}, u32[]{:S(2)}, u32[]{:S(2)}) async-start(bf16[64,40,128]{2,1,0:T(8,128)(2,1)} %bitcast.22), calls=%async_computation.3 | async-start | bytes 1310720 | tf_op jit(solution)/shard_map/all_to_all | solution.py:414

commit v4 on v3

--- a/solution.py
+++ b/solution.py
@@ -19,13 +19,14 @@
     return best if size % best == 0 else size
 
 
-def spread_columns(pick_ref, grad_ref, rows_hbm, rows, sem):
+def spread_columns(pick, load, grad, rows, rows_hbm, sem):
     width = rows.shape[1]
-    step = cut(width, 256)
+    step = cut(width, 512)
     copies = []
     for n in range(0, width, step):
+        load(n, step)
         rows[:, n : n + step] = jnp.dot(
-            pick_ref[...], grad_ref[:, n : n + step], preferred_element_type=jnp.float32
+            pick[...], grad[:, n : n + step], preferred_element_type=jnp.float32
         ).astype(rows.dtype)
         columns = (slice(None), pl.ds(n, step))
         copy = pltpu.make_async_copy(rows.at[columns], rows_hbm.at[columns], sem.at[n // step])
@@ -35,7 +36,20 @@
         copy.wait()
 
 
-def route_kernel(capacity, ids_ref, grad_ref, rows_hbm, code_ref, pick_ref, rows, sem):
+def route_kernel(
+    capacity, ids_ref, grad_hbm, rows_hbm, code_hbm, pick_hbm,
+    grad, rows, code_ref, pick, load_sem, sem, save_sem,
+):
+    width = rows.shape[1]
+    half = width // 2
+    loads = [
+        pltpu.make_async_copy(
+            grad_hbm.at[:, pl.ds(n, half)], grad.at[:, pl.ds(n, half)], load_sem.at[n // half]
+        )
+        for n in (0, half)
+    ]
+    for copy in loads:
+        copy.start()
     experts, tokens = code_ref.shape
     expert = lax.broadcasted_iota(jnp.int32, (experts, tokens), 0)
     hit = ids_ref[0:1, :] == expert
@@ -50,33 +64,46 @@
     code_ref[...] = code
     slot = lax.broadcasted_iota(jnp.int32, (experts, capacity, tokens), 1).astype(jnp.float32)
     one = jnp.where(code[:, None, :] == slot, 1.0, 0.0)
-    pick_ref[...] = one.reshape(experts * capacity, tokens).astype(jnp.bfloat16)
-    spread_columns(pick_ref, grad_ref, rows_hbm, rows, sem)
-
-
-def route(ids_t, out_grad, experts, capacity, first, width):
+    pick[...] = one.reshape(experts * capacity, tokens).astype(jnp.bfloat16)
+    saves = [
+        pltpu.make_async_copy(code_ref, code_hbm, save_sem.at[0]),
+        pltpu.make_async_copy(pick, pick_hbm, save_sem.at[1]),
+    ]
+    for copy in saves:
+        copy.start()
+
+    def load(n, step):
+        if n == 0:
+            loads[0].wait()
+        if n < half <= n + step - 1 or n == half:
+            loads[1].wait()
+
+    spread_columns(pick, load, grad, rows, rows_hbm, sem)
+    for copy in saves:
+        copy.wait()
+
+
+def route(ids_t, out_grad, experts, capacity, width):
     tokens = out_grad.shape[0]
     slots = experts * capacity
+    anywhere = pl.BlockSpec(memory_space=pl.ANY)
     return pl.pallas_call(
         functools.partial(route_kernel, capacity),
-        grid=(1,),
-        in_specs=[
-            pl.BlockSpec(ids_t.shape, lambda i: (0, 0)),
-            pl.BlockSpec((tokens, width), lambda i: (0, first // width)),
-        ],
-        out_specs=[
-            pl.BlockSpec(memory_space=pl.ANY),
-            pl.BlockSpec((experts, tokens), lambda i: (0, 0)),
-            pl.BlockSpec((slots, tokens), lambda i: (0, 0)),
-        ],
+        in_specs=[pl.BlockSpec(memory_space=pltpu.VMEM), anywhere],
+        out_specs=[anywhere] * 3,
         out_shape=[
             jax.ShapeDtypeStruct((slots, width), out_grad.dtype),
             jax.ShapeDtypeStruct((experts, tokens), jnp.float32),
             jax.ShapeDtypeStruct((slots, tokens), jnp.bfloat16),
         ],
         scratch_shapes=[
+            pltpu.VMEM((tokens, width), out_grad.dtype),
             pltpu.VMEM((slots, width), out_grad.dtype),
-            pltpu.SemaphoreType.DMA((width // cut(width, 256),)),
+            pltpu.VMEM((experts, tokens), jnp.float32),
+            pltpu.VMEM((slots, tokens), jnp.bfloat16),
+            pltpu.SemaphoreType.DMA((2,)),
+            pltpu.SemaphoreType.DMA((width // cut(width, 512),)),
+            pltpu.SemaphoreType.DMA((2,)),
         ],
         compiler_params=pltpu.CompilerParams(vmem_limit_bytes=56 * MIB),
         cost_estimate=pl.CostEstimate(
@@ -88,11 +115,15 @@
     )(ids_t, out_grad)
 
 
+def rest_kernel(pick_ref, grad_ref, rows_hbm, rows, sem):
+    spread_columns(pick_ref, lambda n, step: None, grad_ref, rows, rows_hbm, sem)
+
+
 def route_rest(pick, out_grad):
     slots, tokens = pick.shape
     width = out_grad.shape[1]
     return pl.pallas_call(
-        spread_columns,
+        rest_kernel,
         grid=(1,),
         in_specs=[
             pl.BlockSpec((slots, tokens), lambda i: (0, 0)),
@@ -102,7 +133,7 @@
         out_shape=jax.ShapeDtypeStruct((slots, width), out_grad.dtype),
         scratch_shapes=[
             pltpu.VMEM((slots, width), out_grad.dtype),
-            pltpu.SemaphoreType.DMA((width // cut(width, 256),)),
+            pltpu.SemaphoreType.DMA((width // cut(width, 512),)),
         ],
         compiler_params=pltpu.CompilerParams(vmem_limit_bytes=56 * MIB),
         cost_estimate=pl.CostEstimate(
@@ -115,22 +146,33 @@
 
 
 def project_kernel(start, rows_ref, weight_ref, *refs):
-    out_ref, total = refs[-2:]
-    part = lax.dot_general(
-        rows_ref[...], weight_ref[...], NT, preferred_element_type=jnp.float32
-    )
+    if start:
+        half_hbm, out_ref, total, half, sem = refs
+        load = pltpu.make_async_copy(half_hbm, half, sem)
+    else:
+        out_ref, total = refs
 
     @pl.when(pl.program_id(0) == 0)
     def _():
-        total[...] = part + refs[0][...] if start else part
+        if start:
+            load.start()
+        total[...] = lax.dot_general(
+            rows_ref[...], weight_ref[...], NT, preferred_element_type=jnp.float32
+        )
 
     @pl.when(pl.program_id(0) > 0)
     def _():
-        total[...] += part
+        total[...] += lax.dot_general(
+            rows_ref[...], weight_ref[...], NT, preferred_element_type=jnp.float32
+        )
 
     @pl.when(pl.program_id(0) == pl.num_programs(0) - 1)
     def _():
-        out_ref[...] = total[...].astype(out_ref.dtype)
+        if start:
+            load.wait()
+            out_ref[...] = (total[...] + half[...]).astype(out_ref.dtype)
+        else:
+            out_ref[...] = total[...].astype(out_ref.dtype)
 
 
 def project(rows, weight, first, half, dtype, name):
@@ -138,7 +180,7 @@
     units = weight.shape[0]
     step = cut(math.gcd(width, first) if first else width, 1024)
     start = [] if half is None else [half]
-    whole = lambda i: (0, 0)
+    total = pltpu.VMEM((slots, units), jnp.float32)
     return pl.pallas_call(
         functools.partial(project_kernel, half is not None),
         grid=(width // step,),
@@ -146,10 +188,10 @@
             pl.BlockSpec((slots, step), lambda i: (0, i)),
             pl.BlockSpec((units, step), lambda i: (0, i + first // step)),
         ]
-        + [pl.BlockSpec((slots, units), whole)] * len(start),
-        out_specs=pl.BlockSpec((slots, units), whole),
+        + [pl.BlockSpec(memory_space=pl.ANY)] * len(start),
+        out_specs=pl.BlockSpec((slots, units), lambda i: (0, 0)),
         out_shape=jax.ShapeDtypeStruct((slots, units), dtype),
-        scratch_shapes=[pltpu.VMEM((slots, units), jnp.float32)],
+        scratch_shapes=[total] + [total, pltpu.SemaphoreType.DMA(())] * len(start),
         compiler_params=pltpu.CompilerParams(vmem_limit_bytes=56 * MIB),
         cost_estimate=pl.CostEstimate(
             flops=2 * slots * units * width,
@@ -427,7 +469,7 @@
 
     part = width * 3 // 5
     rest = width - part
-    send, code_t, pick = route(expert_ids.T, out_grad, experts, capacity, 0, part)
+    send, code_t, pick = route(expert_ids.T, out_grad, experts, capacity, part)
     first = all_to_all(send.reshape(experts, capacity, part), ALL).reshape(slots, part)
     send = route_rest(pick, out_grad[:, part:])
     expert_out = [

time: 203 us -> 201 us (level)
  Pallas kernels: 55.3 us -> 52.6 us
  waiting for transfers between devices: 80.1 us -> 82.3 us
    all_to_all x4, waiting for transfers between devices: 80.1 us -> 82.3 us  [all_to_all(): return lax.all_to_all(x, axes, split_axis=0, concat_axis=0, tiled=True)]
  transfers between devices with their start and end apart: 7 -> 7, of which waited for: 3 -> 3; matrix products, arithmetic and copies ran while one was open for 12% -> 12% of each run, Pallas kernels for 24% -> 23%
where the time goes in v4:
time: 201 us; the launch traced here: 200 us
  waiting for transfers between devices  82.3 us (41%)
  Pallas kernels  52.6 us (26%)
  starting transfers between devices  35.8 us (18%)
  matrix products  15.9 us (8%)
  local copies, waits for them, and re-layouts  10.9 us (5%)
    all_to_all x4, waiting for transfers between devices, all_to_all(): return lax.all_to_all(x, axes, split_axis=0, concat_axis=0, tiled=True)  82.3 us
    all_to_all x4, starting transfers between devices, all_to_all(): return lax.all_to_all(x, axes, split_axis=0, concat_axis=0, tiled=True)  34 us
    pallas_call x2, Pallas kernels, project(): pl.pallas_call(functools.partial(project_kernel, half is not None), grid=...  16.8 us
    pallas_call x1, Pallas kernels, down_grads(): pl.pallas_call(functools.partial(down_kernel, capacity), in_specs=[inside...  14.1 us
    dot_general x2, matrix products, body(): jnp.dot(hidden, w, preferred_element_type=jnp.float32).astype(jnp.bfloat16)  14 us
    unnamed x20, local copies, waits for them, and re-layouts  7.3 us
    pallas_call x1, Pallas kernels, partial_scores(): pl.pallas_call(partial_kernel, grid=(slots // bm,), in_specs=[pl.BlockSpe...  5.8 us
    pallas_call x1, Pallas kernels, scores(): pl.pallas_call(functools.partial(score_kernel, capacity), in_specs=[anywh...  5.41 us
  transfers between devices with their start and end apart: 7, of which 3 were waited for; matrix products, arithmetic and copies ran while one was open for 12% of the time, Pallas kernels for 23%

profile of v4, /device:TPU:1, one launch (start us, length us, event | category | flops | bytes accessed | tf_op | source)
XLA Modules:
  0.0 200.0 jit_solution(3138085150255266262)
XLA Ops:
  0.6 4.9 %route_rows.1 = (bf16[1024,3072]{1,0:T(8,128)(2,1)}, f32[128,128]{1,0:T(8,128)}, bf16[1024,128]{1,0:T(8,128)(2,1)}) custom-call(s32[6,128]{1,0:T(8,128)} %bitcast.52, bf16[128,5120]{1,0:T(8,128)(2,1)} %grad_hbm.1), custom_call_target="tpu_custom_call" | custom-call | flops 805306368 | bytes 7077888 | tf_op jit(solution)/shard_map/route_rows/pallas_call | solution.py:90
  5.5 0.0 copy-start.6
  5.5 11.9 %all-to-all-start.1 = ((bf16[128,8,3072]{2,1,0:T(8,128)(2,1)}), bf16[128,8,3072]{2,1,0:T(8,128)(2,1)}, u32[]{:S(2)}, u32[]{:S(2)}) async-start(bf16[128,8,3072]{2,1,0:T(8,128)(2,1)} %bitcast.47), calls=%async_computation.1 | async-start | bytes 12582912 | tf_op jit(solution)/shard_map/all_to_all | solution.py:456
  17.4 1.9 slice.9.grad_ref
  19.3 0.0 copy-done.6
  19.3 1.7 copy.24
  21.0 3.7 %route_rest.1 = bf16[1024,2048]{1,0:T(8,128)(2,1)} custom-call(bf16[1024,128]{1,0:T(8,128)(2,1)} %get-tuple-element.18.pick_ref, bf16[128,2048]{1,0:T(8,128)(2,1)} %slice.9.grad_ref), custom_call_target="tpu_custom_call" | custom-call | flops 536870912 | bytes 4718592 | tf_op jit(solution)/shard_map/route_rest/pallas_call | solution.py:125
  24.7 0.0 slice-start.1
  24.7 7.0 %convolution_convert_fusion.1.expert_hbm = bf16[1024,2048]{1,0:T(8,128)(2,1)} fusion(bf16[768,5120]{1,0:T(8,128)(2,1)} %bitcast.41, bf16[1,1024,768]{2,1,0:T(8,128)(2,1)S(1)} %copy-done.6), kind=kOutput, calls=%fused_computation.2 | convolution fusion | flops 3223322624 | bytes 8912896 | tf_op jit(solution)/shard_map/dot_general | solution.py:476
  31.7 0.0 slice-done
  31.7 0.0 slice-done.1
  31.7 7.0 %convolution_convert_fusion.expert_ref = bf16[1024,3072]{1,0:T(8,128)(2,1)} fusion(bf16[768,5120]{1,0:T(8,128)(2,1)S(1)} %bitcast.46, bf16[1,1024,768]{2,1,0:T(8,128)(2,1)S(1)} %copy-done.6), kind=kOutput, calls=%fused_computation | convolution fusion | flops 4834983936 | bytes 12582912 | tf_op jit(solution)/shard_map/dot_general | solution.py:476
  38.7 54.3 %all-to-all-done.1 = bf16[128,8,3072]{2,1,0:T(8,128)(2,1)} async-done(((bf16[128,8,3072]{2,1,0:T(8,128)(2,1)}), bf16[128,8,3072]{2,1,0:T(8,128)(2,1)}, u32[]{:S(2)}, u32[]{:S(2)}) %all-to-all-start.1) | async-done | bytes 6291488 | tf_op jit(solution)/shard_map/all_to_all | solution.py:456
  93.0 8.6 %all-to-all-start = ((bf16[128,8,2048]{2,1,0:T(8,128)(2,1)}), bf16[128,8,2048]{2,1,0:T(8,128)(2,1)}, u32[]{:S(2)}, u32[]{:S(2)}) async-start(bf16[128,8,2048]{2,1,0:T(8,128)(2,1)} %bitcast.40), calls=%async_computation | async-start | bytes 8388608 | tf_op jit(solution)/shard_map/all_to_all | solution.py:456
  101.6 0.0 copy-done.5
  101.7 1.4 copy.29
  103.1 1.4 dynamic-slice_bitcast_fusion
  104.5 0.0 copy-start.2
  104.5 1.2 collective-permute-start.2
  105.7 1.9 fusion.8
  107.8 0.1 collective-permute-start.1
  107.9 0.0 copy-done.2
  107.9 0.5 collective-permute-start
  108.4 0.1 copy.26
  108.5 0.1 copy.25
  108.6 0.1 select_reduce_fusion
  108.7 0.1 copy.27
  108.8 0.7 pad_convert_fusion.gates_ref
  109.6 2.8 %copy-done = bf16[1024,3072]{1,0:T(8,128)(2,1)S(1)} copy-done((bf16[1024,3072]{1,0:T(8,128)(2,1)S(1)}, bf16[1024,3072]{1,0:T(8,128)(2,1)}, u32[]{:S(2)}) %copy-start) | copy-done | bytes 6291480
  112.3 5.8 %partial_scores.1.partial_ref = f32[1024,128]{1,0:T(8,128)S(1)} custom-call(bf16[1024,3072]{1,0:T(8,128)(2,1)} %bitcast.7.rows_ref.first_hbm, bf16[1024,3072]{1,0:T(8,128)(2,1)S(1)} %copy-done), custom_call_target="tpu_custom_call" | custom-call | flops 6291456 | bytes 12582912 | tf_op jit(solution)/shard_map/partial_scores/pallas_call | solution.py:261
  118.2 0.0 copy-start.1
  118.2 0.8 copy-done.1
  119.0 9.6 %project_first.1.refs_0_ = f32[1024,768]{1,0:T(8,128)} custom-call(bf16[1024,3072]{1,0:T(8,128)(2,1)} %bitcast.7.rows_ref.first_hbm, bf16[768,5120]{1,0:T(8,128)(2,1)} %bitcast.42), custom_call_target="tpu_custom_call" | custom-call | flops 4831838208 | bytes 14155776 | tf_op jit(solution)/shard_map/project_first/pallas_call | solution.py:184
  128.6 25.8 %all-to-all-done = bf16[128,8,2048]{2,1,0:T(8,128)(2,1)} async-done(((bf16[128,8,2048]{2,1,0:T(8,128)(2,1)}), bf16[128,8,2048]{2,1,0:T(8,128)(2,1)}, u32[]{:S(2)}, u32[]{:S(2)}) %all-to-all-start) | async-done | bytes 4194336 | tf_op jit(solution)/shard_map/all_to_all | solution.py:456
  154.4 5.4 %score_rows.1 = f32[128,128]{1,0:T(8,128)} custom-call(bf16[1024,2048]{1,0:T(8,128)(2,1)} %bitcast.5.rows_hbm.rows_ref.second_hbm, bf16[1024,2048]{1,0:T(8,128)(2,1)} %convolution_convert_fusion.1.expert_hbm, f32[1024,128]{1,0:T(8,128)} %copy-done.1, f32[128,128]{1,0:T(8,128)} %pad_convert_fusion.gates_ref), custom_call_target="tpu_custom_call" | custom-call | flops 4194304 | bytes 8388608 | tf_op jit(solution)/shard_map/score_rows/pallas_call | solution.py:280
  159.8 4.8 %all-to-all-start.2 = ((f32[128,1,128]{2,1,0:T(1,128)}), f32[128,1,128]{2,1,0:T(1,128)S(1)}, u32[]{:S(2)}, u32[]{:S(2)}) async-start(f32[128,1,128]{2,1,0:T(1,128)} %bitcast.50), calls=%async_computation.2 | async-start | bytes 131072 | tf_op jit(solution)/shard_map/all_to_all | solution.py:456
  164.7 7.2 %project_second.1.proj_hbm = bf16[1024,768]{1,0:T(8,128)(2,1)} custom-call(bf16[1024,2048]{1,0:T(8,128)(2,1)} %bitcast.5.rows_hbm.rows_ref.second_hbm, bf16[768,5120]{1,0:T(8,128)(2,1)} %bitcast.43, f32[1024,768]{1,0:T(8,128)} %project_first.1.refs_0_), custom_call_target="tpu_custom_call" | custom-call | flops 3221225472 | bytes 10485760 | tf_op jit(solution)/shard_map/project_second/pallas_call | solution.py:184
  171.9 0.0 collective-permute-done.1.other_prob_ref
  171.9 0.0 collective-permute-done.other_code_ref
  171.9 0.0 collective-permute-done.2
  171.9 2.2 %all-to-all-done.2 = f32[128,1,128]{2,1,0:T(1,128)S(1)} async-done(((f32[128,1,128]{2,1,0:T(1,128)}), f32[128,1,128]{2,1,0:T(1,128)S(1)}, u32[]{:S(2)}, u32[]{:S(2)}) %all-to-all-start.2) | async-done | bytes 65568 | tf_op jit(solution)/shard_map/all_to_all | solution.py:456
  174.0 1.9 router_terms.1
  176.0 0.6 copy-done.4
  176.6 8.6 %all-to-all-start.3 = ((bf16[64,40,128]{2,1,0:T(8,128)(2,1)}), bf16[64,40,128]{2,1,0:T(8,128)(2,1)S(1)}, u32[]{:S(2)}, u32[]{:S(2)}) async-start(bf16[64,40,128]{2,1,0:T(8,128)(2,1)} %bitcast.22), calls=%async_computation.3 | async-start | bytes 1310720 | tf_op jit(solution)/shard_map/all_to_all | solution.py:456
  185.2 0.0 copy-done.3
  185.2 14.1 %down_grads.1 = (bf16[768,5120]{1,0:T(8,128)(2,1)}, bf16[1024,768]{1,0:T(8,128)(2,1)}, bf16[128,5120]{1,0:T(8,128)(2,1)}) custom-call(f32[128,128]{1,0:T(8,128)} %bitcast.39, bf16[128,128]{1,0:T(8,128)(2,1)} %copy-done.4, bf16[768,1024]{1,0:T(8,128)(2,1)} %bitcast.49, bf16[1024,768]{1,0:T(8,128)(2,1)} %project_second.1.proj_hbm, ...), custom_call_target="tpu_custom_call" | custom-call | flops 8220835840 | bytes 25690112 | tf_op jit(solution)/shard_map/down_grads/pallas_call | solution.py:380
  199.3 0.0 all-to-all-done.3
  199.3 0.7 convert_reduce_fusion
  (9 shorter events, 0.1 us)
Async XLA Ops:
  5.5 13.8 %copy-start.6 = (bf16[1,1024,768]{2,1,0:T(8,128)(2,1)S(1)}, bf16[1,1024,768]{2,1,0:T(8,128)(2,1)}, u32[]{:S(2)}) copy-start(bf16[1,1024,768]{2,1,0:T(8,128)(2,1)} %param.10) | copy-start | bytes 4718596
  5.5 87.5 %all-to-all-start.1 = ((bf16[128,8,3072]{2,1,0:T(8,128)(2,1)}), bf16[128,8,3072]{2,1,0:T(8,128)(2,1)}, u32[]{:S(2)}, u32[]{:S(2)}) async-start(bf16[128,8,3072]{2,1,0:T(8,128)(2,1)} %bitcast.47), calls=%async_computation.1 | async-start | bytes 12582912 | tf_op jit(solution)/shard_map/all_to_all | solution.py:456
  21.0 10.8 %slice-start = ((s8[7864320]{0:T(1024)(128)(4,1)}), s8[3670016]{0:T(1024)(128)(4,1)S(1)}, s32[]{:S(2)}) async-start(s8[7864320]{0:T(1024)(128)(4,1)} %bitcast.44), calls=%async_computation.4 | async-start | bytes 7340032
  24.7 7.0 %slice-start.1 = ((s8[7864320]{0:T(1024)(128)(4,1)}), s8[4194304]{0:T(1024)(128)(4,1)S(1)}, s32[]{:S(2)}) async-start(s8[7864320]{0:T(1024)(128)(4,1)} %bitcast.44), calls=%async_computation.5 | async-start | bytes 8388608
  93.0 8.7 %copy-start.5 = (bf16[128,5120]{1,0:T(8,128)(2,1)S(1)}, bf16[128,5120]{1,0:T(8,128)(2,1)}, u32[]{:S(2)}) copy-start(bf16[128,5120]{1,0:T(8,128)(2,1)} %param.7) | copy-start | bytes 3932164
  93.0 61.4 %all-to-all-start = ((bf16[128,8,2048]{2,1,0:T(8,128)(2,1)}), bf16[128,8,2048]{2,1,0:T(8,128)(2,1)}, u32[]{:S(2)}, u32[]{:S(2)}) async-start(bf16[128,8,2048]{2,1,0:T(8,128)(2,1)} %bitcast.40), calls=%async_computation | async-start | bytes 8388608 | tf_op jit(solution)/shard_map/all_to_all | solution.py:456
  104.5 3.4 %copy-start.2 = (f32[128,128]{1,0:T(8,128)S(1)}, f32[128,128]{1,0:T(8,128)}, u32[]{:S(2)}) copy-start(f32[128,128]{1,0:T(8,128)} %get-tuple-element.24.code_ref) | copy-start | bytes 196612
  104.5 67.4 %collective-permute-start.2 = (bf16[64,40,128]{2,1,0:T(8,128)(2,1)S(1)}, bf16[64,40,128]{2,1,0:T(8,128)(2,1)S(1)}, u32[]{:S(2)}, u32[]{:S(2)}) collective-permute-start(bf16[64,40,128]{2,1,0:T(8,128)(2,1)S(1)} %get-tuple-element.32), channel_id=1, source_target_pairs={{0,1},{1,0},{2,3},{3,2},{4,5},{5,4},{6,7},{7,6},{8,9},{9,8},{10,11... | collective-permute-start | bytes 1966088 | tf_op jit(solution)/shard_map/ppermute | solution.py:498
  107.8 64.1 %collective-permute-start.1 = (f32[128,128]{1,0:T(8,128)S(1)}, f32[128,128]{1,0:T(8,128)S(1)}, u32[]{:S(2)}, u32[]{:S(2)}) collective-permute-start(f32[128,128]{1,0:T(8,128)S(1)} %get-tuple-element.34.prob_ref), channel_id=1, source_target_pairs={{0,1},{1,0},{2,3},{3,2},{4,5},{5,4},{6,7},{7,6},{8,9},{9,8},{10,11... | collective-permute-start | bytes 196616 | tf_op jit(solution)/shard_map/ppermute | solution.py:494
  107.9 64.0 %collective-permute-start = (f32[128,128]{1,0:T(8,128)S(1)}, f32[128,128]{1,0:T(8,128)S(1)}, u32[]{:S(2)}, u32[]{:S(2)}) collective-permute-start(f32[128,128]{1,0:T(8,128)S(1)} %copy-done.2), channel_id=1, source_target_pairs={{0,1},{1,0},{2,3},{3,2},{4,5},{5,4},{6,7},{7,6},{8,9},{9,8},{10,11... | collective-permute-start | bytes 196616 | tf_op jit(solution)/shard_map/ppermute | solution.py:494
  109.6 2.8 %copy-start = (bf16[1024,3072]{1,0:T(8,128)(2,1)S(1)}, bf16[1024,3072]{1,0:T(8,128)(2,1)}, u32[]{:S(2)}) copy-start(bf16[1024,3072]{1,0:T(8,128)(2,1)} %convolution_convert_fusion.expert_ref) | copy-start | bytes 18874372
  118.2 0.8 copy-start.1
  159.8 14.2 %all-to-all-start.2 = ((f32[128,1,128]{2,1,0:T(1,128)}), f32[128,1,128]{2,1,0:T(1,128)S(1)}, u32[]{:S(2)}, u32[]{:S(2)}) async-start(f32[128,1,128]{2,1,0:T(1,128)} %bitcast.50), calls=%async_computation.2 | async-start | bytes 131072 | tf_op jit(solution)/shard_map/all_to_all | solution.py:456
  174.0 11.2 %copy-start.3 = (f32[128,1,128]{2,1,0:T(1,128)}, f32[128,1,128]{2,1,0:T(1,128)S(1)}, u32[]{:S(2)}) copy-start(f32[128,1,128]{2,1,0:T(1,128)S(1)} %all-to-all-done.2) | copy-start | bytes 196612
  176.0 0.6 copy-start.4
  176.6 22.7 %all-to-all-start.3 = ((bf16[64,40,128]{2,1,0:T(8,128)(2,1)}), bf16[64,40,128]{2,1,0:T(8,128)(2,1)S(1)}, u32[]{:S(2)}, u32[]{:S(2)}) async-start(bf16[64,40,128]{2,1,0:T(8,128)(2,1)} %bitcast.22), calls=%async_computation.3 | async-start | bytes 1310720 | tf_op jit(solution)/shard_map/all_to_all | solution.py:456

commit v5 on v4

--- a/solution.py
+++ b/solution.py
@@ -206,7 +206,6 @@
     capacity, rows_hbm, expert_hbm, partial_ref, gates_ref, back_ref, rows, expert, score, sem
 ):
     slots, width = rows.shape
-    group = 2 * capacity
     bm = cut(slots, 128)
     loads = []
     for i in range(slots // bm):
@@ -221,7 +220,7 @@
     for copies in loads[:ahead]:
         for copy in copies:
             copy.start()
-    row = lax.broadcasted_iota(jnp.int32, (bm, 128), 0) % group
+    row = lax.broadcasted_iota(jnp.int32, (bm, 128), 0) % capacity
     lane = lax.broadcasted_iota(jnp.int32, (bm, 128), 1)
     for i, copies in enumerate(loads):
         for copy in copies:
@@ -235,15 +234,15 @@
                 at, k : k + 128
             ].astype(jnp.float32)
         total = jnp.sum(total, axis=1, keepdims=True)
-        for core in range(2):
-            laid = jnp.where((row + core * capacity) % group == lane, total, 0.0)
-            score[core, i * bm // group : (i + 1) * bm // group, :] = jnp.sum(
-                laid.reshape(bm // group, group, 128), axis=1
-            )
-    chips = slots // group
-    back_ref[pl.ds(0, chips, stride=2), :] = score[0]
-    back_ref[pl.ds(1, chips, stride=2), :] = score[1]
-    back_ref[...] += gates_ref[...]
+        laid = jnp.where(row == lane, total, 0.0)
+        score[i * bm // capacity : (i + 1) * bm // capacity, :] = jnp.sum(
+            laid.reshape(bm // capacity, capacity, 128), axis=1
+        )
+    own = score[...]
+    devices = own.shape[0]
+    even = lax.broadcasted_iota(jnp.int32, own.shape, 0) % 2 == 0
+    partner = jnp.where(even, pltpu.roll(own, devices - 1, 0), pltpu.roll(own, 1, 0))
+    back_ref[...] = own + pltpu.roll(partner, capacity, 1) + gates_ref[...]
 
 
 def partial_kernel(rows_ref, expert_ref, partial_ref):
@@ -285,7 +284,7 @@
         scratch_shapes=[
             pltpu.VMEM((slots, width), jnp.bfloat16),
             pltpu.VMEM((slots, width), jnp.bfloat16),
-            pltpu.VMEM((2, slots // (2 * capacity), 128), jnp.float32),
+            pltpu.VMEM((slots // capacity, 128), jnp.float32),
             pltpu.SemaphoreType.DMA((2, slots // bm)),
         ],
         compiler_params=pltpu.CompilerParams(vmem_limit_bytes=56 * MIB),

time: 201 us -> 201 us (level)
  no operation moved by 1% of the time
where the time goes in v5:
time: 201 us; the launch traced here: 200 us
  waiting for transfers between devices  82.3 us (41%)
  Pallas kernels  52.7 us (26%)
  starting transfers between devices  35.8 us (18%)
  matrix products  15.9 us (8%)
  local copies, waits for them, and re-layouts  10.9 us (5%)
    all_to_all x4, waiting for transfers between devices, all_to_all(): return lax.all_to_all(x, axes, split_axis=0, concat_axis=0, tiled=True)  82.3 us
    all_to_all x4, starting transfers between devices, all_to_all(): return lax.all_to_all(x, axes, split_axis=0, concat_axis=0, tiled=True)  34 us
    pallas_call x2, Pallas kernels, project(): pl.pallas_call(functools.partial(project_kernel, half is not None), grid=...  16.8 us
    pallas_call x1, Pallas kernels, down_grads(): pl.pallas_call(functools.partial(down_kernel, capacity), in_specs=[inside...  14.1 us
    dot_general x2, matrix products, body(): jnp.dot(hidden, w, preferred_element_type=jnp.float32).astype(jnp.bfloat16)  14 us
    unnamed x20, local copies, waits for them, and re-layouts  7.3 us
    pallas_call x1, Pallas kernels, partial_scores(): pl.pallas_call(partial_kernel, grid=(slots // bm,), in_specs=[pl.BlockSpe...  5.8 us
    pallas_call x1, Pallas kernels, scores(): pl.pallas_call(functools.partial(score_kernel, capacity), in_specs=[anywh...  5.48 us
  transfers between devices with their start and end apart: 7, of which 3 were waited for; matrix products, arithmetic and copies ran while one was open for 12% of the time, Pallas kernels for 23%

profile of v5, /device:TPU:1, one launch (start us, length us, event | category | flops | bytes accessed | tf_op | source)
XLA Modules:
  0.0 200.1 jit_solution(9386204981025644174)
XLA Ops:
  0.6 4.9 %route_rows.1 = (bf16[1024,3072]{1,0:T(8,128)(2,1)}, f32[128,128]{1,0:T(8,128)}, bf16[1024,128]{1,0:T(8,128)(2,1)}) custom-call(s32[6,128]{1,0:T(8,128)} %bitcast.52, bf16[128,5120]{1,0:T(8,128)(2,1)} %grad_hbm.1), custom_call_target="tpu_custom_call" | custom-call | flops 805306368 | bytes 7077888 | tf_op jit(solution)/shard_map/route_rows/pallas_call | solution.py:90
  5.5 0.0 copy-start.6
  5.5 11.9 %all-to-all-start.1 = ((bf16[128,8,3072]{2,1,0:T(8,128)(2,1)}), bf16[128,8,3072]{2,1,0:T(8,128)(2,1)}, u32[]{:S(2)}, u32[]{:S(2)}) async-start(bf16[128,8,3072]{2,1,0:T(8,128)(2,1)} %bitcast.47), calls=%async_computation.1 | async-start | bytes 12582912 | tf_op jit(solution)/shard_map/all_to_all | solution.py:455
  17.4 1.9 slice.9.grad_ref
  19.3 0.0 copy-done.6
  19.3 1.7 copy.24
  21.0 3.7 %route_rest.1 = bf16[1024,2048]{1,0:T(8,128)(2,1)} custom-call(bf16[1024,128]{1,0:T(8,128)(2,1)} %get-tuple-element.18.pick_ref, bf16[128,2048]{1,0:T(8,128)(2,1)} %slice.9.grad_ref), custom_call_target="tpu_custom_call" | custom-call | flops 536870912 | bytes 4718592 | tf_op jit(solution)/shard_map/route_rest/pallas_call | solution.py:125
  24.7 0.0 slice-start.1
  24.7 7.0 %convolution_convert_fusion.1.expert_hbm = bf16[1024,2048]{1,0:T(8,128)(2,1)} fusion(bf16[768,5120]{1,0:T(8,128)(2,1)} %bitcast.41, bf16[1,1024,768]{2,1,0:T(8,128)(2,1)S(1)} %copy-done.6), kind=kOutput, calls=%fused_computation.2 | convolution fusion | flops 3223322624 | bytes 8912896 | tf_op jit(solution)/shard_map/dot_general | solution.py:475
  31.7 0.0 slice-done
  31.7 0.0 slice-done.1
  31.7 7.0 %convolution_convert_fusion.expert_ref = bf16[1024,3072]{1,0:T(8,128)(2,1)} fusion(bf16[768,5120]{1,0:T(8,128)(2,1)S(1)} %bitcast.46, bf16[1,1024,768]{2,1,0:T(8,128)(2,1)S(1)} %copy-done.6), kind=kOutput, calls=%fused_computation | convolution fusion | flops 4834983936 | bytes 12582912 | tf_op jit(solution)/shard_map/dot_general | solution.py:475
  38.7 54.3 %all-to-all-done.1 = bf16[128,8,3072]{2,1,0:T(8,128)(2,1)} async-done(((bf16[128,8,3072]{2,1,0:T(8,128)(2,1)}), bf16[128,8,3072]{2,1,0:T(8,128)(2,1)}, u32[]{:S(2)}, u32[]{:S(2)}) %all-to-all-start.1) | async-done | bytes 6291488 | tf_op jit(solution)/shard_map/all_to_all | solution.py:455
  93.0 8.6 %all-to-all-start = ((bf16[128,8,2048]{2,1,0:T(8,128)(2,1)}), bf16[128,8,2048]{2,1,0:T(8,128)(2,1)}, u32[]{:S(2)}, u32[]{:S(2)}) async-start(bf16[128,8,2048]{2,1,0:T(8,128)(2,1)} %bitcast.40), calls=%async_computation | async-start | bytes 8388608 | tf_op jit(solution)/shard_map/all_to_all | solution.py:455
  101.6 0.0 copy-done.5
  101.7 1.4 copy.29
  103.1 1.4 dynamic-slice_bitcast_fusion
  104.5 0.0 copy-start.2
  104.5 1.2 collective-permute-start.2
  105.7 1.9 fusion.8
  107.8 0.1 collective-permute-start.1
  107.9 0.0 copy-done.2
  107.9 0.5 collective-permute-start
  108.4 0.1 copy.26
  108.5 0.1 copy.25
  108.6 0.1 select_reduce_fusion
  108.7 0.1 copy.27
  108.8 0.7 pad_convert_fusion.gates_ref
  109.6 2.8 %copy-done = bf16[1024,3072]{1,0:T(8,128)(2,1)S(1)} copy-done((bf16[1024,3072]{1,0:T(8,128)(2,1)S(1)}, bf16[1024,3072]{1,0:T(8,128)(2,1)}, u32[]{:S(2)}) %copy-start) | copy-done | bytes 6291480
  112.3 5.8 %partial_scores.1.partial_ref = f32[1024,128]{1,0:T(8,128)S(1)} custom-call(bf16[1024,3072]{1,0:T(8,128)(2,1)} %bitcast.7.rows_ref.first_hbm, bf16[1024,3072]{1,0:T(8,128)(2,1)S(1)} %copy-done), custom_call_target="tpu_custom_call" | custom-call | flops 6291456 | bytes 12582912 | tf_op jit(solution)/shard_map/partial_scores/pallas_call | solution.py:260
  118.2 0.0 copy-start.1
  118.2 0.8 copy-done.1
  119.0 9.6 %project_first.1.refs_0_ = f32[1024,768]{1,0:T(8,128)} custom-call(bf16[1024,3072]{1,0:T(8,128)(2,1)} %bitcast.7.rows_ref.first_hbm, bf16[768,5120]{1,0:T(8,128)(2,1)} %bitcast.42), custom_call_target="tpu_custom_call" | custom-call | flops 4831838208 | bytes 14155776 | tf_op jit(solution)/shard_map/project_first/pallas_call | solution.py:184
  128.6 25.8 %all-to-all-done = bf16[128,8,2048]{2,1,0:T(8,128)(2,1)} async-done(((bf16[128,8,2048]{2,1,0:T(8,128)(2,1)}), bf16[128,8,2048]{2,1,0:T(8,128)(2,1)}, u32[]{:S(2)}, u32[]{:S(2)}) %all-to-all-start) | async-done | bytes 4194336 | tf_op jit(solution)/shard_map/all_to_all | solution.py:455
  154.4 5.5 %score_rows.1 = f32[128,128]{1,0:T(8,128)} custom-call(bf16[1024,2048]{1,0:T(8,128)(2,1)} %bitcast.5.rows_hbm.rows_ref.second_hbm, bf16[1024,2048]{1,0:T(8,128)(2,1)} %convolution_convert_fusion.1.expert_hbm, f32[1024,128]{1,0:T(8,128)} %copy-done.1, f32[128,128]{1,0:T(8,128)} %pad_convert_fusion.gates_ref), custom_call_target="tpu_custom_call" | custom-call | flops 4194304 | bytes 8388608 | tf_op jit(solution)/shard_map/score_rows/pallas_call | solution.py:279
  159.9 4.8 %all-to-all-start.2 = ((f32[128,1,128]{2,1,0:T(1,128)}), f32[128,1,128]{2,1,0:T(1,128)S(1)}, u32[]{:S(2)}, u32[]{:S(2)}) async-start(f32[128,1,128]{2,1,0:T(1,128)} %bitcast.50), calls=%async_computation.2 | async-start | bytes 131072 | tf_op jit(solution)/shard_map/all_to_all | solution.py:455
  164.8 7.2 %project_second.1.proj_hbm = bf16[1024,768]{1,0:T(8,128)(2,1)} custom-call(bf16[1024,2048]{1,0:T(8,128)(2,1)} %bitcast.5.rows_hbm.rows_ref.second_hbm, bf16[768,5120]{1,0:T(8,128)(2,1)} %bitcast.43, f32[1024,768]{1,0:T(8,128)} %project_first.1.refs_0_), custom_call_target="tpu_custom_call" | custom-call | flops 3221225472 | bytes 10485760 | tf_op jit(solution)/shard_map/project_second/pallas_call | solution.py:184
  171.9 0.0 collective-permute-done.1.other_prob_ref
  171.9 0.0 collective-permute-done.other_code_ref
  171.9 0.0 collective-permute-done.2
  172.0 2.1 %all-to-all-done.2 = f32[128,1,128]{2,1,0:T(1,128)S(1)} async-done(((f32[128,1,128]{2,1,0:T(1,128)}), f32[128,1,128]{2,1,0:T(1,128)S(1)}, u32[]{:S(2)}, u32[]{:S(2)}) %all-to-all-start.2) | async-done | bytes 65568 | tf_op jit(solution)/shard_map/all_to_all | solution.py:455
  174.1 1.9 router_terms.1
  176.0 0.6 copy-done.4
  176.6 8.6 %all-to-all-start.3 = ((bf16[64,40,128]{2,1,0:T(8,128)(2,1)}), bf16[64,40,128]{2,1,0:T(8,128)(2,1)S(1)}, u32[]{:S(2)}, u32[]{:S(2)}) async-start(bf16[64,40,128]{2,1,0:T(8,128)(2,1)} %bitcast.22), calls=%async_computation.3 | async-start | bytes 1310720 | tf_op jit(solution)/shard_map/all_to_all | solution.py:455
  185.3 0.0 copy-done.3
  185.3 14.1 %down_grads.1 = (bf16[768,5120]{1,0:T(8,128)(2,1)}, bf16[1024,768]{1,0:T(8,128)(2,1)}, bf16[128,5120]{1,0:T(8,128)(2,1)}) custom-call(f32[128,128]{1,0:T(8,128)} %bitcast.39, bf16[128,128]{1,0:T(8,128)(2,1)} %copy-done.4, bf16[768,1024]{1,0:T(8,128)(2,1)} %bitcast.49, bf16[1024,768]{1,0:T(8,128)(2,1)} %project_second.1.proj_hbm, ...), custom_call_target="tpu_custom_call" | custom-call | flops 8220835840 | bytes 25690112 | tf_op jit(solution)/shard_map/down_grads/pallas_call | solution.py:379
  199.4 0.0 all-to-all-done.3
  199.4 0.7 convert_reduce_fusion
  (9 shorter events, 0.1 us)
Async XLA Ops:
  5.5 13.8 %copy-start.6 = (bf16[1,1024,768]{2,1,0:T(8,128)(2,1)S(1)}, bf16[1,1024,768]{2,1,0:T(8,128)(2,1)}, u32[]{:S(2)}) copy-start(bf16[1,1024,768]{2,1,0:T(8,128)(2,1)} %param.10) | copy-start | bytes 4718596
  5.5 87.5 %all-to-all-start.1 = ((bf16[128,8,3072]{2,1,0:T(8,128)(2,1)}), bf16[128,8,3072]{2,1,0:T(8,128)(2,1)}, u32[]{:S(2)}, u32[]{:S(2)}) async-start(bf16[128,8,3072]{2,1,0:T(8,128)(2,1)} %bitcast.47), calls=%async_computation.1 | async-start | bytes 12582912 | tf_op jit(solution)/shard_map/all_to_all | solution.py:455
  21.0 10.8 %slice-start = ((s8[7864320]{0:T(1024)(128)(4,1)}), s8[3670016]{0:T(1024)(128)(4,1)S(1)}, s32[]{:S(2)}) async-start(s8[7864320]{0:T(1024)(128)(4,1)} %bitcast.44), calls=%async_computation.4 | async-start | bytes 7340032
  24.7 7.0 %slice-start.1 = ((s8[7864320]{0:T(1024)(128)(4,1)}), s8[4194304]{0:T(1024)(128)(4,1)S(1)}, s32[]{:S(2)}) async-start(s8[7864320]{0:T(1024)(128)(4,1)} %bitcast.44), calls=%async_computation.5 | async-start | bytes 8388608
  93.0 8.7 %copy-start.5 = (bf16[128,5120]{1,0:T(8,128)(2,1)S(1)}, bf16[128,5120]{1,0:T(8,128)(2,1)}, u32[]{:S(2)}) copy-start(bf16[128,5120]{1,0:T(8,128)(2,1)} %param.7) | copy-start | bytes 3932164
  93.0 61.4 %all-to-all-start = ((bf16[128,8,2048]{2,1,0:T(8,128)(2,1)}), bf16[128,8,2048]{2,1,0:T(8,128)(2,1)}, u32[]{:S(2)}, u32[]{:S(2)}) async-start(bf16[128,8,2048]{2,1,0:T(8,128)(2,1)} %bitcast.40), calls=%async_computation | async-start | bytes 8388608 | tf_op jit(solution)/shard_map/all_to_all | solution.py:455
  104.5 3.4 %copy-start.2 = (f32[128,128]{1,0:T(8,128)S(1)}, f32[128,128]{1,0:T(8,128)}, u32[]{:S(2)}) copy-start(f32[128,128]{1,0:T(8,128)} %get-tuple-element.24.code_ref) | copy-start | bytes 196612
  104.5 67.4 %collective-permute-start.2 = (bf16[64,40,128]{2,1,0:T(8,128)(2,1)S(1)}, bf16[64,40,128]{2,1,0:T(8,128)(2,1)S(1)}, u32[]{:S(2)}, u32[]{:S(2)}) collective-permute-start(bf16[64,40,128]{2,1,0:T(8,128)(2,1)S(1)} %get-tuple-element.32), channel_id=1, source_target_pairs={{0,1},{1,0},{2,3},{3,2},{4,5},{5,4},{6,7},{7,6},{8,9},{9,8},{10,11... | collective-permute-start | bytes 1966088 | tf_op jit(solution)/shard_map/ppermute | solution.py:497
  107.8 64.2 %collective-permute-start.1 = (f32[128,128]{1,0:T(8,128)S(1)}, f32[128,128]{1,0:T(8,128)S(1)}, u32[]{:S(2)}, u32[]{:S(2)}) collective-permute-start(f32[128,128]{1,0:T(8,128)S(1)} %get-tuple-element.34.prob_ref), channel_id=1, source_target_pairs={{0,1},{1,0},{2,3},{3,2},{4,5},{5,4},{6,7},{7,6},{8,9},{9,8},{10,11... | collective-permute-start | bytes 196616 | tf_op jit(solution)/shard_map/ppermute | solution.py:493
  107.9 64.1 %collective-permute-start = (f32[128,128]{1,0:T(8,128)S(1)}, f32[128,128]{1,0:T(8,128)S(1)}, u32[]{:S(2)}, u32[]{:S(2)}) collective-permute-start(f32[128,128]{1,0:T(8,128)S(1)} %copy-done.2), channel_id=1, source_target_pairs={{0,1},{1,0},{2,3},{3,2},{4,5},{5,4},{6,7},{7,6},{8,9},{9,8},{10,11... | collective-permute-start | bytes 196616 | tf_op jit(solution)/shard_map/ppermute | solution.py:493
  109.6 2.8 %copy-start = (bf16[1024,3072]{1,0:T(8,128)(2,1)S(1)}, bf16[1024,3072]{1,0:T(8,128)(2,1)}, u32[]{:S(2)}) copy-start(bf16[1024,3072]{1,0:T(8,128)(2,1)} %convolution_convert_fusion.expert_ref) | copy-start | bytes 18874372
  118.2 0.8 copy-start.1
  159.9 14.2 %all-to-all-start.2 = ((f32[128,1,128]{2,1,0:T(1,128)}), f32[128,1,128]{2,1,0:T(1,128)S(1)}, u32[]{:S(2)}, u32[]{:S(2)}) async-start(f32[128,1,128]{2,1,0:T(1,128)} %bitcast.50), calls=%async_computation.2 | async-start | bytes 131072 | tf_op jit(solution)/shard_map/all_to_all | solution.py:455
  174.1 11.2 %copy-start.3 = (f32[128,1,128]{2,1,0:T(1,128)}, f32[128,1,128]{2,1,0:T(1,128)S(1)}, u32[]{:S(2)}) copy-start(f32[128,1,128]{2,1,0:T(1,128)S(1)} %all-to-all-done.2) | copy-start | bytes 196612
  176.0 0.6 copy-start.4
  176.6 22.7 %all-to-all-start.3 = ((bf16[64,40,128]{2,1,0:T(8,128)(2,1)}), bf16[64,40,128]{2,1,0:T(8,128)(2,1)S(1)}, u32[]{:S(2)}, u32[]{:S(2)}) async-start(bf16[64,40,128]{2,1,0:T(8,128)(2,1)} %bitcast.22), calls=%async_computation.3 | async-start | bytes 1310720 | tf_op jit(solution)/shard_map/all_to_all | solution.py:455

commit v6 on v5

--- a/solution.py
+++ b/solution.py
@@ -203,7 +203,7 @@
 
 
 def score_kernel(
-    capacity, rows_hbm, expert_hbm, partial_ref, gates_ref, back_ref, rows, expert, score, sem
+    capacity, rows_hbm, expert_hbm, base_ref, back_ref, rows, expert, score, sem
 ):
     slots, width = rows.shape
     bm = cut(slots, 128)
@@ -228,7 +228,7 @@
         for copy in loads[i + ahead] if i + ahead < len(loads) else []:
             copy.start()
         at = slice(i * bm, (i + 1) * bm)
-        total = partial_ref[at, :]
+        total = jnp.zeros((bm, 128), jnp.float32)
         for k in range(0, width, 128):
             total = total + rows[at, k : k + 128].astype(jnp.float32) * expert[
                 at, k : k + 128
@@ -242,43 +242,17 @@
     devices = own.shape[0]
     even = lax.broadcasted_iota(jnp.int32, own.shape, 0) % 2 == 0
     partner = jnp.where(even, pltpu.roll(own, devices - 1, 0), pltpu.roll(own, 1, 0))
-    back_ref[...] = own + pltpu.roll(partner, capacity, 1) + gates_ref[...]
-
-
-def partial_kernel(rows_ref, expert_ref, partial_ref):
-    total = jnp.zeros(partial_ref.shape, jnp.float32)
-    for k in range(0, rows_ref.shape[1], 128):
-        total = total + rows_ref[:, k : k + 128].astype(jnp.float32) * expert_ref[
-            :, k : k + 128
-        ].astype(jnp.float32)
-    partial_ref[...] = total
-
-
-def partial_scores(rows, expert):
-    slots, width = rows.shape
-    bm = cut(slots, 128)
-    return pl.pallas_call(
-        partial_kernel,
-        grid=(slots // bm,),
-        in_specs=[pl.BlockSpec((bm, width), lambda i: (i, 0))] * 2,
-        out_specs=pl.BlockSpec((bm, 128), lambda i: (i, 0)),
-        out_shape=jax.ShapeDtypeStruct((slots, 128), jnp.float32),
-        compiler_params=pltpu.CompilerParams(vmem_limit_bytes=24 * MIB),
-        cost_estimate=pl.CostEstimate(
-            flops=2 * slots * width, bytes_accessed=4 * slots * width, transcendentals=0
-        ),
-        name="partial_scores",
-    )(rows, expert)
-
-
-def scores(rows, expert, partial, gates, capacity):
+    back_ref[...] = own + pltpu.roll(partner, capacity, 1) + base_ref[...]
+
+
+def scores(rows, expert, base, capacity, name):
     slots, width = rows.shape
     bm = cut(slots, 128)
     anywhere = pl.BlockSpec(memory_space=pl.ANY)
     inside = pl.BlockSpec(memory_space=pltpu.VMEM)
     return pl.pallas_call(
         functools.partial(score_kernel, capacity),
-        in_specs=[anywhere, anywhere, inside, inside],
+        in_specs=[anywhere, anywhere, inside],
         out_specs=inside,
         out_shape=jax.ShapeDtypeStruct((slots // capacity, 128), jnp.float32),
         scratch_shapes=[
@@ -291,8 +265,8 @@
         cost_estimate=pl.CostEstimate(
             flops=2 * slots * width, bytes_accessed=4 * slots * width, transcendentals=0
         ),
-        name="score_rows",
-    )(rows, expert, partial, gates)
+        name=name,
+    )(rows, expert, base)
 
 
 def tiles(split, width):
@@ -497,11 +471,11 @@
     taken = lax.ppermute(give, "c", swap).reshape(width // 2, tokens)
     keep = keep.reshape(width // 2, tokens)
 
-    partial = partial_scores(first, expert_out[0])
+    base = scores(first, expert_out[0], gate_lanes, capacity, "score_first")
     half = project(first, weight, 0, None, jnp.float32, "project_first")
-    partial, half = lax.optimization_barrier((partial, half))
-
-    score = scores(second, expert_out[1], partial, gate_lanes, capacity)
+    base, half = lax.optimization_barrier((base, half))
+
+    score = scores(second, expert_out[1], base, capacity, "score_rows")
     back = all_to_all(score, ALL)
     proj = project(second, weight, part, half, jnp.bfloat16, "project_second")
 

time: 201 us -> 201 us (level)
  waiting for transfers between devices: 82.3 us -> 86.9 us
  local copies, waits for them, and re-layouts: 10.9 us -> 6.76 us
    pallas_call x1 -> x2, Pallas kernels: 5.48 us -> 11.8 us  [scores(): pl.pallas_call(functools.partial(score_kernel, capacity), in_specs=[anywh...]
    pallas_call x1 -> x0, Pallas kernels: 5.8 us -> none  [partial_scores(): pl.pallas_call(partial_kernel, grid=(slots // bm,), in_specs=[pl.BlockSpe...]
    all_to_all x4, waiting for transfers between devices: 82.3 us -> 86.9 us  [all_to_all(): return lax.all_to_all(x, axes, split_axis=0, concat_axis=0, tiled=True)]
    unnamed x20 -> x18, local copies, waits for them, and re-layouts: 7.3 us -> 3.61 us
  transfers between devices with their start and end apart: 7 -> 7, of which waited for: 3 -> 3; matrix products, arithmetic and copies ran while one was open for 12% -> 11% of each run, Pallas kernels for 23% -> 23%
where the time goes in v6:
time: 201 us; the launch traced here: 200 us
  waiting for transfers between devices  86.9 us (43%)
  Pallas kernels  53.2 us (26%)
  starting transfers between devices  35.4 us (18%)
  matrix products  14.6 us (7%)
  local copies, waits for them, and re-layouts  6.76 us (3%)
  other arithmetic  2.3 us (1%)
    all_to_all x4, waiting for transfers between devices, all_to_all(): return lax.all_to_all(x, axes, split_axis=0, concat_axis=0, tiled=True)  86.9 us
    all_to_all x4, starting transfers between devices, all_to_all(): return lax.all_to_all(x, axes, split_axis=0, concat_axis=0, tiled=True)  34.1 us
    pallas_call x2, Pallas kernels, project(): pl.pallas_call(functools.partial(project_kernel, half is not None), grid=...  16.8 us
    pallas_call x1, Pallas kernels, down_grads(): pl.pallas_call(functools.partial(down_kernel, capacity), in_specs=[inside...  14.1 us
    dot_general x2, matrix products, body(): jnp.dot(hidden, w, preferred_element_type=jnp.float32).astype(jnp.bfloat16)  13.9 us
    pallas_call x2, Pallas kernels, scores(): pl.pallas_call(functools.partial(score_kernel, capacity), in_specs=[anywh...  11.8 us
    pallas_call x1, Pallas kernels, route(): pl.pallas_call(functools.partial(route_kernel, capacity), in_specs=[pl.Bl...  4.86 us
  transfers between devices with their start and end apart: 7, of which 3 were waited for; matrix products, arithmetic and copies ran while one was open for 11% of the time, Pallas kernels for 23%

profile of v6, /device:TPU:1, one launch (start us, length us, event | category | flops | bytes accessed | tf_op | source)
XLA Modules:
  0.0 199.9 jit_solution(9064164991457821086)
XLA Ops:
  0.6 4.9 %route_rows.1 = (bf16[1024,3072]{1,0:T(8,128)(2,1)}, f32[128,128]{1,0:T(8,128)}, bf16[1024,128]{1,0:T(8,128)(2,1)}) custom-call(s32[6,128]{1,0:T(8,128)} %bitcast.52, bf16[128,5120]{1,0:T(8,128)(2,1)} %grad_hbm.1), custom_call_target="tpu_custom_call" | custom-call | flops 805306368 | bytes 7077888 | tf_op jit(solution)/shard_map/route_rows/pallas_call | solution.py:90
  5.5 0.0 copy-start.4
  5.5 11.9 %all-to-all-start.1 = ((bf16[128,8,3072]{2,1,0:T(8,128)(2,1)}), bf16[128,8,3072]{2,1,0:T(8,128)(2,1)}, u32[]{:S(2)}, u32[]{:S(2)}) async-start(bf16[128,8,3072]{2,1,0:T(8,128)(2,1)} %bitcast.47), calls=%async_computation.1 | async-start | bytes 12582912 | tf_op jit(solution)/shard_map/all_to_all | solution.py:429
  17.4 1.9 slice.9.grad_ref
  19.3 0.0 copy-done.4
  19.3 1.7 copy.24
  21.0 0.0 slice-start
  21.0 3.7 %route_rest.1 = bf16[1024,2048]{1,0:T(8,128)(2,1)} custom-call(bf16[1024,128]{1,0:T(8,128)(2,1)} %get-tuple-element.18.pick_ref, bf16[128,2048]{1,0:T(8,128)(2,1)} %slice.9.grad_ref), custom_call_target="tpu_custom_call" | custom-call | flops 536870912 | bytes 4718592 | tf_op jit(solution)/shard_map/route_rest/pallas_call | solution.py:125
  24.7 0.0 slice-start.1
  24.7 7.0 %convolution_convert_fusion.1.expert_hbm = bf16[1024,2048]{1,0:T(8,128)(2,1)} fusion(bf16[768,5120]{1,0:T(8,128)(2,1)} %bitcast.41, bf16[1,1024,768]{2,1,0:T(8,128)(2,1)S(1)} %copy-done.4), kind=kOutput, calls=%fused_computation.2 | convolution fusion | flops 3223322624 | bytes 8912896 | tf_op jit(solution)/shard_map/dot_general | solution.py:449
  31.7 0.0 slice-done
  31.7 0.0 slice-done.1
  31.7 6.9 %convolution_convert_fusion.expert_hbm = bf16[1024,3072]{1,0:T(8,128)(2,1)} fusion(bf16[768,5120]{1,0:T(8,128)(2,1)S(1)} %bitcast.46, bf16[1,1024,768]{2,1,0:T(8,128)(2,1)S(1)} %copy-done.4), kind=kOutput, calls=%fused_computation | convolution fusion | flops 4834983936 | bytes 12582912 | tf_op jit(solution)/shard_map/dot_general | solution.py:449
  38.6 54.3 %all-to-all-done.1 = bf16[128,8,3072]{2,1,0:T(8,128)(2,1)} async-done(((bf16[128,8,3072]{2,1,0:T(8,128)(2,1)}), bf16[128,8,3072]{2,1,0:T(8,128)(2,1)}, u32[]{:S(2)}, u32[]{:S(2)}) %all-to-all-start.1) | async-done | bytes 6291488 | tf_op jit(solution)/shard_map/all_to_all | solution.py:429
  93.0 8.6 %all-to-all-start = ((bf16[128,8,2048]{2,1,0:T(8,128)(2,1)}), bf16[128,8,2048]{2,1,0:T(8,128)(2,1)}, u32[]{:S(2)}, u32[]{:S(2)}) async-start(bf16[128,8,2048]{2,1,0:T(8,128)(2,1)} %bitcast.40), calls=%async_computation | async-start | bytes 8388608 | tf_op jit(solution)/shard_map/all_to_all | solution.py:429
  101.6 0.0 copy-done.3
  101.7 0.0 copy-done.5
  101.7 0.6 fusion.8
  102.4 0.7 fusion.7
  103.0 1.1 collective-permute-start.1
  104.1 0.8 copy.29
  104.9 0.0 copy-start
  104.9 0.1 dynamic-slice_bitcast_fusion
  105.1 0.1 collective-permute-start.2
  105.2 0.6 copy-done
  105.8 0.0 collective-permute-start
  105.8 0.9 copy.26
  106.7 0.1 copy.25
  106.8 0.1 select_reduce_fusion
  107.0 0.1 copy.27
  107.1 0.7 pad_convert_fusion.base_ref
  107.8 6.6 %score_first.1.base_ref = f32[128,128]{1,0:T(8,128)} custom-call(bf16[1024,3072]{1,0:T(8,128)(2,1)} %bitcast.7.rows_hbm.rows_ref.first_hbm, bf16[1024,3072]{1,0:T(8,128)(2,1)} %convolution_convert_fusion.expert_hbm, f32[128,128]{1,0:T(8,128)} %pad_convert_fusion.base_ref), custom_call_target="tpu_custom_call" | custom-call | flops 6291456 | bytes 12582912 | tf_op jit(solution)/shard_map/score_first/pallas_call | solution.py:253
  114.4 9.6 %project_first.1.refs_0_ = f32[1024,768]{1,0:T(8,128)} custom-call(bf16[1024,3072]{1,0:T(8,128)(2,1)} %bitcast.7.rows_hbm.rows_ref.first_hbm, bf16[768,5120]{1,0:T(8,128)(2,1)} %bitcast.42), custom_call_target="tpu_custom_call" | custom-call | flops 4831838208 | bytes 14155776 | tf_op jit(solution)/shard_map/project_first/pallas_call | solution.py:184
  124.0 30.4 %all-to-all-done = bf16[128,8,2048]{2,1,0:T(8,128)(2,1)} async-done(((bf16[128,8,2048]{2,1,0:T(8,128)(2,1)}), bf16[128,8,2048]{2,1,0:T(8,128)(2,1)}, u32[]{:S(2)}, u32[]{:S(2)}) %all-to-all-start) | async-done | bytes 4194336 | tf_op jit(solution)/shard_map/all_to_all | solution.py:429
  154.4 5.3 %score_rows.1 = f32[128,128]{1,0:T(8,128)} custom-call(bf16[1024,2048]{1,0:T(8,128)(2,1)} %bitcast.5.rows_hbm.rows_ref.second_hbm, bf16[1024,2048]{1,0:T(8,128)(2,1)} %convolution_convert_fusion.1.expert_hbm, f32[128,128]{1,0:T(8,128)} %score_first.1.base_ref), custom_call_target="tpu_custom_call" | custom-call | flops 4194304 | bytes 8388608 | tf_op jit(solution)/shard_map/score_rows/pallas_call | solution.py:253
  159.7 4.8 %all-to-all-start.2 = ((f32[128,1,128]{2,1,0:T(1,128)}), f32[128,1,128]{2,1,0:T(1,128)S(1)}, u32[]{:S(2)}, u32[]{:S(2)}) async-start(f32[128,1,128]{2,1,0:T(1,128)} %bitcast.50), calls=%async_computation.2 | async-start | bytes 131072 | tf_op jit(solution)/shard_map/all_to_all | solution.py:429
  164.6 7.2 %project_second.1.proj_hbm = bf16[1024,768]{1,0:T(8,128)(2,1)} custom-call(bf16[1024,2048]{1,0:T(8,128)(2,1)} %bitcast.5.rows_hbm.rows_ref.second_hbm, bf16[768,5120]{1,0:T(8,128)(2,1)} %bitcast.43, f32[1024,768]{1,0:T(8,128)} %project_first.1.refs_0_), custom_call_target="tpu_custom_call" | custom-call | flops 3221225472 | bytes 10485760 | tf_op jit(solution)/shard_map/project_second/pallas_call | solution.py:184
  171.7 0.0 collective-permute-done.1.other_prob_ref
  171.7 0.0 collective-permute-done.other_code_ref
  171.7 0.0 collective-permute-done.2
  171.8 2.1 %all-to-all-done.2 = f32[128,1,128]{2,1,0:T(1,128)S(1)} async-done(((f32[128,1,128]{2,1,0:T(1,128)}), f32[128,1,128]{2,1,0:T(1,128)S(1)}, u32[]{:S(2)}, u32[]{:S(2)}) %all-to-all-start.2) | async-done | bytes 65568 | tf_op jit(solution)/shard_map/all_to_all | solution.py:429
  173.8 1.9 router_terms.1
  175.8 0.6 copy-done.2
  176.4 8.7 %all-to-all-start.3 = ((bf16[64,40,128]{2,1,0:T(8,128)(2,1)}), bf16[64,40,128]{2,1,0:T(8,128)(2,1)S(1)}, u32[]{:S(2)}, u32[]{:S(2)}) async-start(bf16[64,40,128]{2,1,0:T(8,128)(2,1)} %bitcast.22), calls=%async_computation.3 | async-start | bytes 1310720 | tf_op jit(solution)/shard_map/all_to_all | solution.py:429
  185.1 0.0 copy-done.1
  185.1 14.1 %down_grads.1 = (bf16[768,5120]{1,0:T(8,128)(2,1)}, bf16[1024,768]{1,0:T(8,128)(2,1)}, bf16[128,5120]{1,0:T(8,128)(2,1)}) custom-call(f32[128,128]{1,0:T(8,128)} %bitcast.39, bf16[128,128]{1,0:T(8,128)(2,1)} %copy-done.2, bf16[768,1024]{1,0:T(8,128)(2,1)} %bitcast.49, bf16[1024,768]{1,0:T(8,128)(2,1)} %project_second.1.proj_hbm, ...), custom_call_target="tpu_custom_call" | custom-call | flops 8220835840 | bytes 25690112 | tf_op jit(solution)/shard_map/down_grads/pallas_call | solution.py:353
  199.2 0.0 all-to-all-done.3
  199.2 0.7 convert_reduce_fusion
  (7 shorter events, 0.1 us)
Async XLA Ops:
  5.5 13.8 %copy-start.4 = (bf16[1,1024,768]{2,1,0:T(8,128)(2,1)S(1)}, bf16[1,1024,768]{2,1,0:T(8,128)(2,1)}, u32[]{:S(2)}) copy-start(bf16[1,1024,768]{2,1,0:T(8,128)(2,1)} %param.10) | copy-start | bytes 4718596
  5.5 87.5 %all-to-all-start.1 = ((bf16[128,8,3072]{2,1,0:T(8,128)(2,1)}), bf16[128,8,3072]{2,1,0:T(8,128)(2,1)}, u32[]{:S(2)}, u32[]{:S(2)}) async-start(bf16[128,8,3072]{2,1,0:T(8,128)(2,1)} %bitcast.47), calls=%async_computation.1 | async-start | bytes 12582912 | tf_op jit(solution)/shard_map/all_to_all | solution.py:429
  21.0 10.7 %slice-start = ((s8[7864320]{0:T(1024)(128)(4,1)}), s8[3670016]{0:T(1024)(128)(4,1)S(1)}, s32[]{:S(2)}) async-start(s8[7864320]{0:T(1024)(128)(4,1)} %bitcast.44), calls=%async_computation.4 | async-start | bytes 7340032
  24.7 7.0 %slice-start.1 = ((s8[7864320]{0:T(1024)(128)(4,1)}), s8[4194304]{0:T(1024)(128)(4,1)S(1)}, s32[]{:S(2)}) async-start(s8[7864320]{0:T(1024)(128)(4,1)} %bitcast.44), calls=%async_computation.5 | async-start | bytes 8388608
  93.0 8.7 %copy-start.3 = (bf16[128,5120]{1,0:T(8,128)(2,1)S(1)}, bf16[128,5120]{1,0:T(8,128)(2,1)}, u32[]{:S(2)}) copy-start(bf16[128,5120]{1,0:T(8,128)(2,1)} %param.7) | copy-start | bytes 3932164
  93.0 8.7 %copy-start.5 = (bf16[5120,128]{1,0:T(8,128)(2,1)S(1)}, bf16[5120,128]{1,0:T(8,128)(2,1)}, u32[]{:S(2)}) copy-start(bf16[5120,128]{1,0:T(8,128)(2,1)} %router_hbm.1) | copy-start | bytes 3932164
  93.0 61.4 %all-to-all-start = ((bf16[128,8,2048]{2,1,0:T(8,128)(2,1)}), bf16[128,8,2048]{2,1,0:T(8,128)(2,1)}, u32[]{:S(2)}, u32[]{:S(2)}) async-start(bf16[128,8,2048]{2,1,0:T(8,128)(2,1)} %bitcast.40), calls=%async_computation | async-start | bytes 8388608 | tf_op jit(solution)/shard_map/all_to_all | solution.py:429
  103.0 68.7 %collective-permute-start.1 = (f32[128,128]{1,0:T(8,128)S(1)}, f32[128,128]{1,0:T(8,128)S(1)}, u32[]{:S(2)}, u32[]{:S(2)}) collective-permute-start(f32[128,128]{1,0:T(8,128)S(1)} %get-tuple-element.34.prob_ref), channel_id=1, source_target_pairs={{0,1},{1,0},{2,3},{3,2},{4,5},{5,4},{6,7},{7,6},{8,9},{9,8},{10,11... | collective-permute-start | bytes 196616 | tf_op jit(solution)/shard_map/ppermute | solution.py:467
  104.9 0.8 copy-start
  105.1 66.7 %collective-permute-start.2 = (bf16[64,40,128]{2,1,0:T(8,128)(2,1)S(1)}, bf16[64,40,128]{2,1,0:T(8,128)(2,1)S(1)}, u32[]{:S(2)}, u32[]{:S(2)}) collective-permute-start(bf16[64,40,128]{2,1,0:T(8,128)(2,1)S(1)} %get-tuple-element.32), channel_id=1, source_target_pairs={{0,1},{1,0},{2,3},{3,2},{4,5},{5,4},{6,7},{7,6},{8,9},{9,8},{10,11... | collective-permute-start | bytes 1966088 | tf_op jit(solution)/shard_map/ppermute | solution.py:471
  105.8 66.0 %collective-permute-start = (f32[128,128]{1,0:T(8,128)S(1)}, f32[128,128]{1,0:T(8,128)S(1)}, u32[]{:S(2)}, u32[]{:S(2)}) collective-permute-start(f32[128,128]{1,0:T(8,128)S(1)} %copy-done), channel_id=1, source_target_pairs={{0,1},{1,0},{2,3},{3,2},{4,5},{5,4},{6,7},{7,6},{8,9},{9,8},{10,11... | collective-permute-start | bytes 196616 | tf_op jit(solution)/shard_map/ppermute | solution.py:467
  159.7 14.1 %all-to-all-start.2 = ((f32[128,1,128]{2,1,0:T(1,128)}), f32[128,1,128]{2,1,0:T(1,128)S(1)}, u32[]{:S(2)}, u32[]{:S(2)}) async-start(f32[128,1,128]{2,1,0:T(1,128)} %bitcast.50), calls=%async_computation.2 | async-start | bytes 131072 | tf_op jit(solution)/shard_map/all_to_all | solution.py:429
  173.8 11.2 %copy-start.1 = (f32[128,1,128]{2,1,0:T(1,128)}, f32[128,1,128]{2,1,0:T(1,128)S(1)}, u32[]{:S(2)}) copy-start(f32[128,1,128]{2,1,0:T(1,128)S(1)} %all-to-all-done.2) | copy-start | bytes 196612
  175.8 0.6 copy-start.2
  176.4 22.8 %all-to-all-start.3 = ((bf16[64,40,128]{2,1,0:T(8,128)(2,1)}), bf16[64,40,128]{2,1,0:T(8,128)(2,1)S(1)}, u32[]{:S(2)}, u32[]{:S(2)}) async-start(bf16[64,40,128]{2,1,0:T(8,128)(2,1)} %bitcast.22), calls=%async_computation.3 | async-start | bytes 1310720 | tf_op jit(solution)/shard_map/all_to_all | solution.py:429

commit v7 on v6

--- a/solution.py
+++ b/solution.py
@@ -313,7 +313,7 @@
     gate_row = jnp.broadcast_to(gate, (slots, 128)).T[0:1, :]
     load_hidden.wait()
     loads[1].start()
-    gated[...] = (gate_row * hidden[...].astype(jnp.float32)).astype(gated.dtype)
+    gated[...] = gate_row.astype(gated.dtype) * hidden[...]
     for i, (n, step) in enumerate(at):
         columns = slice(n, n + step)
         loads[i].wait()
@@ -328,7 +328,7 @@
         stores[i].start()
         if i == 1:
             load_proj.wait()
-            dh[...] = (gate * proj[...].astype(jnp.float32)).astype(dh.dtype)
+            dh[...] = gate.astype(dh.dtype) * proj[...]
             store_dh.start()
             load_router.wait()
             grad = grad_ref[...].astype(jnp.float32).T.astype(jnp.bfloat16)

time: 201 us -> 200 us (level)
  no operation moved by 1% of the time
where the time goes in v7:
time: 200 us
  waiting for transfers between devices  86.9 us (43%)
  Pallas kernels  53.1 us (27%)
  starting transfers between devices  35.4 us (18%)
  matrix products  14.6 us (7%)
  local copies, waits for them, and re-layouts  6.76 us (3%)
  other arithmetic  2.3 us (1%)
    all_to_all x4, waiting for transfers between devices, all_to_all(): return lax.all_to_all(x, axes, split_axis=0, concat_axis=0, tiled=True)  86.9 us
    all_to_all x4, starting transfers between devices, all_to_all(): return lax.all_to_all(x, axes, split_axis=0, concat_axis=0, tiled=True)  34.1 us
    pallas_call x2, Pallas kernels, project(): pl.pallas_call(functools.partial(project_kernel, half is not None), grid=...  16.8 us
    pallas_call x1, Pallas kernels, down_grads(): pl.pallas_call(functools.partial(down_kernel, capacity), in_specs=[inside...  14 us
    dot_general x2, matrix products, body(): jnp.dot(hidden, w, preferred_element_type=jnp.float32).astype(jnp.bfloat16)  13.9 us
    pallas_call x2, Pallas kernels, scores(): pl.pallas_call(functools.partial(score_kernel, capacity), in_specs=[anywh...  11.8 us
    pallas_call x1, Pallas kernels, route(): pl.pallas_call(functools.partial(route_kernel, capacity), in_specs=[pl.Bl...  4.86 us
  transfers between devices with their start and end apart: 7, of which 3 were waited for; matrix products, arithmetic and copies ran while one was open for 11% of the time, Pallas kernels for 23%

profile of v7, /device:TPU:1, one launch (start us, length us, event | category | flops | bytes accessed | tf_op | source)
XLA Modules:
  0.0 199.8 jit_solution(8232345547966595183)
XLA Ops:
  0.6 4.9 %route_rows.1 = (bf16[1024,3072]{1,0:T(8,128)(2,1)}, f32[128,128]{1,0:T(8,128)}, bf16[1024,128]{1,0:T(8,128)(2,1)}) custom-call(s32[6,128]{1,0:T(8,128)} %bitcast.52, bf16[128,5120]{1,0:T(8,128)(2,1)} %grad_hbm.1), custom_call_target="tpu_custom_call" | custom-call | flops 805306368 | bytes 7077888 | tf_op jit(solution)/shard_map/route_rows/pallas_call | solution.py:90
  5.5 0.0 copy-start.4
  5.5 11.9 %all-to-all-start.1 = ((bf16[128,8,3072]{2,1,0:T(8,128)(2,1)}), bf16[128,8,3072]{2,1,0:T(8,128)(2,1)}, u32[]{:S(2)}, u32[]{:S(2)}) async-start(bf16[128,8,3072]{2,1,0:T(8,128)(2,1)} %bitcast.47), calls=%async_computation.1 | async-start | bytes 12582912 | tf_op jit(solution)/shard_map/all_to_all | solution.py:429
  17.4 1.9 slice.9.grad_ref
  19.3 0.0 copy-done.4
  19.3 1.7 copy.24
  21.0 0.0 slice-start
  21.0 3.7 %route_rest.1 = bf16[1024,2048]{1,0:T(8,128)(2,1)} custom-call(bf16[1024,128]{1,0:T(8,128)(2,1)} %get-tuple-element.18.pick_ref, bf16[128,2048]{1,0:T(8,128)(2,1)} %slice.9.grad_ref), custom_call_target="tpu_custom_call" | custom-call | flops 536870912 | bytes 4718592 | tf_op jit(solution)/shard_map/route_rest/pallas_call | solution.py:125
  24.7 0.0 slice-start.1
  24.7 7.0 %convolution_convert_fusion.1.expert_hbm = bf16[1024,2048]{1,0:T(8,128)(2,1)} fusion(bf16[768,5120]{1,0:T(8,128)(2,1)} %bitcast.41, bf16[1,1024,768]{2,1,0:T(8,128)(2,1)S(1)} %copy-done.4), kind=kOutput, calls=%fused_computation.2 | convolution fusion | flops 3223322624 | bytes 8912896 | tf_op jit(solution)/shard_map/dot_general | solution.py:449
  31.7 0.0 slice-done
  31.7 0.0 slice-done.1
  31.7 6.9 %convolution_convert_fusion.expert_hbm = bf16[1024,3072]{1,0:T(8,128)(2,1)} fusion(bf16[768,5120]{1,0:T(8,128)(2,1)S(1)} %bitcast.46, bf16[1,1024,768]{2,1,0:T(8,128)(2,1)S(1)} %copy-done.4), kind=kOutput, calls=%fused_computation | convolution fusion | flops 4834983936 | bytes 12582912 | tf_op jit(solution)/shard_map/dot_general | solution.py:449
  38.6 54.3 %all-to-all-done.1 = bf16[128,8,3072]{2,1,0:T(8,128)(2,1)} async-done(((bf16[128,8,3072]{2,1,0:T(8,128)(2,1)}), bf16[128,8,3072]{2,1,0:T(8,128)(2,1)}, u32[]{:S(2)}, u32[]{:S(2)}) %all-to-all-start.1) | async-done | bytes 6291488 | tf_op jit(solution)/shard_map/all_to_all | solution.py:429
  93.0 8.6 %all-to-all-start = ((bf16[128,8,2048]{2,1,0:T(8,128)(2,1)}), bf16[128,8,2048]{2,1,0:T(8,128)(2,1)}, u32[]{:S(2)}, u32[]{:S(2)}) async-start(bf16[128,8,2048]{2,1,0:T(8,128)(2,1)} %bitcast.40), calls=%async_computation | async-start | bytes 8388608 | tf_op jit(solution)/shard_map/all_to_all | solution.py:429
  101.6 0.0 copy-done.3
  101.7 0.0 copy-done.5
  101.7 0.6 fusion.8
  102.4 0.7 fusion.7
  103.0 1.1 collective-permute-start.1
  104.1 0.8 copy.29
  104.9 0.0 copy-start
  104.9 0.1 dynamic-slice_bitcast_fusion
  105.1 0.1 collective-permute-start.2
  105.2 0.6 copy-done
  105.8 0.0 collective-permute-start
  105.8 0.9 copy.26
  106.7 0.1 copy.25
  106.8 0.1 select_reduce_fusion
  107.0 0.1 copy.27
  107.1 0.7 pad_convert_fusion.base_ref
  107.8 6.6 %score_first.1.base_ref = f32[128,128]{1,0:T(8,128)} custom-call(bf16[1024,3072]{1,0:T(8,128)(2,1)} %bitcast.7.rows_hbm.rows_ref.first_hbm, bf16[1024,3072]{1,0:T(8,128)(2,1)} %convolution_convert_fusion.expert_hbm, f32[128,128]{1,0:T(8,128)} %pad_convert_fusion.base_ref), custom_call_target="tpu_custom_call" | custom-call | flops 6291456 | bytes 12582912 | tf_op jit(solution)/shard_map/score_first/pallas_call | solution.py:253
  114.4 9.6 %project_first.1.refs_0_ = f32[1024,768]{1,0:T(8,128)} custom-call(bf16[1024,3072]{1,0:T(8,128)(2,1)} %bitcast.7.rows_hbm.rows_ref.first_hbm, bf16[768,5120]{1,0:T(8,128)(2,1)} %bitcast.42), custom_call_target="tpu_custom_call" | custom-call | flops 4831838208 | bytes 14155776 | tf_op jit(solution)/shard_map/project_first/pallas_call | solution.py:184
  124.0 30.4 %all-to-all-done = bf16[128,8,2048]{2,1,0:T(8,128)(2,1)} async-done(((bf16[128,8,2048]{2,1,0:T(8,128)(2,1)}), bf16[128,8,2048]{2,1,0:T(8,128)(2,1)}, u32[]{:S(2)}, u32[]{:S(2)}) %all-to-all-start) | async-done | bytes 4194336 | tf_op jit(solution)/shard_map/all_to_all | solution.py:429
  154.4 5.3 %score_rows.1 = f32[128,128]{1,0:T(8,128)} custom-call(bf16[1024,2048]{1,0:T(8,128)(2,1)} %bitcast.5.rows_hbm.rows_ref.second_hbm, bf16[1024,2048]{1,0:T(8,128)(2,1)} %convolution_convert_fusion.1.expert_hbm, f32[128,128]{1,0:T(8,128)} %score_first.1.base_ref), custom_call_target="tpu_custom_call" | custom-call | flops 4194304 | bytes 8388608 | tf_op jit(solution)/shard_map/score_rows/pallas_call | solution.py:253
  159.7 4.8 %all-to-all-start.2 = ((f32[128,1,128]{2,1,0:T(1,128)}), f32[128,1,128]{2,1,0:T(1,128)S(1)}, u32[]{:S(2)}, u32[]{:S(2)}) async-start(f32[128,1,128]{2,1,0:T(1,128)} %bitcast.50), calls=%async_computation.2 | async-start | bytes 131072 | tf_op jit(solution)/shard_map/all_to_all | solution.py:429
  164.6 7.2 %project_second.1.proj_hbm = bf16[1024,768]{1,0:T(8,128)(2,1)} custom-call(bf16[1024,2048]{1,0:T(8,128)(2,1)} %bitcast.5.rows_hbm.rows_ref.second_hbm, bf16[768,5120]{1,0:T(8,128)(2,1)} %bitcast.43, f32[1024,768]{1,0:T(8,128)} %project_first.1.refs_0_), custom_call_target="tpu_custom_call" | custom-call | flops 3221225472 | bytes 10485760 | tf_op jit(solution)/shard_map/project_second/pallas_call | solution.py:184
  171.7 0.0 collective-permute-done.1.other_prob_ref
  171.7 0.0 collective-permute-done.other_code_ref
  171.7 0.0 collective-permute-done.2
  171.8 2.1 %all-to-all-done.2 = f32[128,1,128]{2,1,0:T(1,128)S(1)} async-done(((f32[128,1,128]{2,1,0:T(1,128)}), f32[128,1,128]{2,1,0:T(1,128)S(1)}, u32[]{:S(2)}, u32[]{:S(2)}) %all-to-all-start.2) | async-done | bytes 65568 | tf_op jit(solution)/shard_map/all_to_all | solution.py:429
  173.8 1.9 router_terms.1
  175.8 0.6 copy-done.2
  176.4 8.7 %all-to-all-start.3 = ((bf16[64,40,128]{2,1,0:T(8,128)(2,1)}), bf16[64,40,128]{2,1,0:T(8,128)(2,1)S(1)}, u32[]{:S(2)}, u32[]{:S(2)}) async-start(bf16[64,40,128]{2,1,0:T(8,128)(2,1)} %bitcast.22), calls=%async_computation.3 | async-start | bytes 1310720 | tf_op jit(solution)/shard_map/all_to_all | solution.py:429
  185.1 0.0 copy-done.1
  185.1 14.0 %down_grads.1 = (bf16[768,5120]{1,0:T(8,128)(2,1)}, bf16[1024,768]{1,0:T(8,128)(2,1)}, bf16[128,5120]{1,0:T(8,128)(2,1)}) custom-call(f32[128,128]{1,0:T(8,128)} %bitcast.39, bf16[128,128]{1,0:T(8,128)(2,1)} %copy-done.2, bf16[768,1024]{1,0:T(8,128)(2,1)} %bitcast.49, bf16[1024,768]{1,0:T(8,128)(2,1)} %project_second.1.proj_hbm, ...), custom_call_target="tpu_custom_call" | custom-call | flops 8220835840 | bytes 25690112 | tf_op jit(solution)/shard_map/down_grads/pallas_call | solution.py:353
  199.1 0.0 all-to-all-done.3
  199.1 0.7 convert_reduce_fusion
  (7 shorter events, 0.1 us)
Async XLA Ops:
  5.5 13.8 %copy-start.4 = (bf16[1,1024,768]{2,1,0:T(8,128)(2,1)S(1)}, bf16[1,1024,768]{2,1,0:T(8,128)(2,1)}, u32[]{:S(2)}) copy-start(bf16[1,1024,768]{2,1,0:T(8,128)(2,1)} %param.10) | copy-start | bytes 4718596
  5.5 87.5 %all-to-all-start.1 = ((bf16[128,8,3072]{2,1,0:T(8,128)(2,1)}), bf16[128,8,3072]{2,1,0:T(8,128)(2,1)}, u32[]{:S(2)}, u32[]{:S(2)}) async-start(bf16[128,8,3072]{2,1,0:T(8,128)(2,1)} %bitcast.47), calls=%async_computation.1 | async-start | bytes 12582912 | tf_op jit(solution)/shard_map/all_to_all | solution.py:429
  21.0 10.7 %slice-start = ((s8[7864320]{0:T(1024)(128)(4,1)}), s8[3670016]{0:T(1024)(128)(4,1)S(1)}, s32[]{:S(2)}) async-start(s8[7864320]{0:T(1024)(128)(4,1)} %bitcast.44), calls=%async_computation.4 | async-start | bytes 7340032
  24.7 7.0 %slice-start.1 = ((s8[7864320]{0:T(1024)(128)(4,1)}), s8[4194304]{0:T(1024)(128)(4,1)S(1)}, s32[]{:S(2)}) async-start(s8[7864320]{0:T(1024)(128)(4,1)} %bitcast.44), calls=%async_computation.5 | async-start | bytes 8388608
  93.0 8.7 %copy-start.3 = (bf16[128,5120]{1,0:T(8,128)(2,1)S(1)}, bf16[128,5120]{1,0:T(8,128)(2,1)}, u32[]{:S(2)}) copy-start(bf16[128,5120]{1,0:T(8,128)(2,1)} %param.7) | copy-start | bytes 3932164
  93.0 8.7 %copy-start.5 = (bf16[5120,128]{1,0:T(8,128)(2,1)S(1)}, bf16[5120,128]{1,0:T(8,128)(2,1)}, u32[]{:S(2)}) copy-start(bf16[5120,128]{1,0:T(8,128)(2,1)} %router_hbm.1) | copy-start | bytes 3932164
  93.0 61.4 %all-to-all-start = ((bf16[128,8,2048]{2,1,0:T(8,128)(2,1)}), bf16[128,8,2048]{2,1,0:T(8,128)(2,1)}, u32[]{:S(2)}, u32[]{:S(2)}) async-start(bf16[128,8,2048]{2,1,0:T(8,128)(2,1)} %bitcast.40), calls=%async_computation | async-start | bytes 8388608 | tf_op jit(solution)/shard_map/all_to_all | solution.py:429
  103.0 68.7 %collective-permute-start.1 = (f32[128,128]{1,0:T(8,128)S(1)}, f32[128,128]{1,0:T(8,128)S(1)}, u32[]{:S(2)}, u32[]{:S(2)}) collective-permute-start(f32[128,128]{1,0:T(8,128)S(1)} %get-tuple-element.34.prob_ref), channel_id=1, source_target_pairs={{0,1},{1,0},{2,3},{3,2},{4,5},{5,4},{6,7},{7,6},{8,9},{9,8},{10,11... | collective-permute-start | bytes 196616 | tf_op jit(solution)/shard_map/ppermute | solution.py:467
  104.9 0.8 copy-start
  105.1 66.7 %collective-permute-start.2 = (bf16[64,40,128]{2,1,0:T(8,128)(2,1)S(1)}, bf16[64,40,128]{2,1,0:T(8,128)(2,1)S(1)}, u32[]{:S(2)}, u32[]{:S(2)}) collective-permute-start(bf16[64,40,128]{2,1,0:T(8,128)(2,1)S(1)} %get-tuple-element.32), channel_id=1, source_target_pairs={{0,1},{1,0},{2,3},{3,2},{4,5},{5,4},{6,7},{7,6},{8,9},{9,8},{10,11... | collective-permute-start | bytes 1966088 | tf_op jit(solution)/shard_map/ppermute | solution.py:471
  105.8 66.0 %collective-permute-start = (f32[128,128]{1,0:T(8,128)S(1)}, f32[128,128]{1,0:T(8,128)S(1)}, u32[]{:S(2)}, u32[]{:S(2)}) collective-permute-start(f32[128,128]{1,0:T(8,128)S(1)} %copy-done), channel_id=1, source_target_pairs={{0,1},{1,0},{2,3},{3,2},{4,5},{5,4},{6,7},{7,6},{8,9},{9,8},{10,11... | collective-permute-start | bytes 196616 | tf_op jit(solution)/shard_map/ppermute | solution.py:467
  159.7 14.1 %all-to-all-start.2 = ((f32[128,1,128]{2,1,0:T(1,128)}), f32[128,1,128]{2,1,0:T(1,128)S(1)}, u32[]{:S(2)}, u32[]{:S(2)}) async-start(f32[128,1,128]{2,1,0:T(1,128)} %bitcast.50), calls=%async_computation.2 | async-start | bytes 131072 | tf_op jit(solution)/shard_map/all_to_all | solution.py:429
  173.8 11.2 %copy-start.1 = (f32[128,1,128]{2,1,0:T(1,128)}, f32[128,1,128]{2,1,0:T(1,128)S(1)}, u32[]{:S(2)}) copy-start(f32[128,1,128]{2,1,0:T(1,128)S(1)} %all-to-all-done.2) | copy-start | bytes 196612
  175.8 0.6 copy-start.2
  176.4 22.7 %all-to-all-start.3 = ((bf16[64,40,128]{2,1,0:T(8,128)(2,1)}), bf16[64,40,128]{2,1,0:T(8,128)(2,1)S(1)}, u32[]{:S(2)}, u32[]{:S(2)}) async-start(bf16[64,40,128]{2,1,0:T(8,128)(2,1)} %bitcast.22), calls=%async_computation.3 | async-start | bytes 1310720 | tf_op jit(solution)/shard_map/all_to_all | solution.py:429
